TPU v7x, 32 devices: a whole 2x2x4 slice. The times are simulated.
32 devices in a mesh: tm: 8 (over y, x, core), space: 4 (over z).
Axes of the slice: x: 2, y: 2, z: 4, core: 2. Of those that a mesh axis runs over, the one named last changes fastest.
Arguments:
- frames: bfloat16 [4096, 4, 256], P('tm', 'space'), may hold values from -8 to 8
- patch_cell: int32 [4], P('space'), may hold values from 0 to 2047
- enc_in: bfloat16 [256, 1024], replicated, may hold values from -0.375 to 0.375
- enc_bias: float32 [1024], replicated, may hold values from -3 to 3
- enc_out: bfloat16 [1024, 1024], replicated, may hold values from -0.1875 to 0.1875
- pos_table: bfloat16 [2048, 1024], replicated, may hold values from -3 to 3
- norm_gain: float32 [1024], replicated, may hold values from 0.1 to 1.9
- w_pair: bfloat16 [1024, 4096], replicated, may hold values from -0.1875 to 0.1875
- w_keys: bfloat16 [1024, 256], replicated, may hold values from -0.0234375 to 0.0234375
- w_step: bfloat16 [1024, 32], replicated, may hold values from -0.1875 to 0.1875
- step_bias: float32 [32], replicated, may hold values from -1.5 to 1
- decay_code: int32 [32], replicated, may hold values from 0 to 15
- skip_gain: float32 [32], replicated, may hold values from 0.5 to 1.5
- out_gain: float32 [2048], replicated, may hold values from 0.1 to 1.9
- w_out: bfloat16 [2048, 1024], replicated, may hold values from -0.125 to 0.125
Outputs:
- layer_output: bfloat16 [4096, 4, 1024], P('tm', 'space')
All inputs are finite; a program needn't handle non-finite values.
Results may differ from a plain program's by a relative error of at most 0.013.
Values may be sent and summed in bfloat16 or wider, within the bound.
No kernel may reach another device: no remote copies, remote signals or barrier semaphores. Data moves between devices by JAX's collectives and lax.ppermute only.
A program may use at most 128 MiB of HBM per device.

v0:
```python
import jax
import jax.numpy as jnp
from jax import lax
from jax.sharding import PartitionSpec as P


def carried_in(array, axis, combine, identity):
    peers, here = (lax.axis_size(axis), lax.axis_index(axis))
    everything = jax.tree.map(lambda part: lax.all_gather(part, axis), array)
    start = jax.tree.map(
        lambda part, zero: jnp.broadcast_to(jnp.asarray(zero, part.dtype), part.shape),
        array,
        identity,
    )

    def turn(k, before):
        reached = k < here
        new = combine(before, jax.tree.map(lambda part: part[k], everything))
        return jax.tree.map(lambda a, b: jnp.where(reached, a, b), new, before)

    return lax.fori_loop(0, peers, turn, start)


def rate_table(decay_code):
    return -0.0005 - 0.003 * decay_code.astype(jnp.float32)


def encode(frame_block, pos_rows, enc_in, enc_bias, enc_out, norm_gain):
    hidden = jax.nn.gelu(
        jnp.dot(frame_block, enc_in, preferred_element_type=jnp.float32) + enc_bias,
        approximate=True,
    ).astype(jnp.bfloat16)
    encoded = (
        jnp.dot(hidden, enc_out, preferred_element_type=jnp.float32) + pos_rows.astype(jnp.float32)
    ).astype(jnp.bfloat16)
    widened = encoded.astype(jnp.float32)
    normed = (
        widened * lax.rsqrt(jnp.mean(widened * widened, axis=-1, keepdims=True) + 1e-05) * norm_gain
    ).astype(jnp.bfloat16)
    return (encoded, normed)


def body(
    frames,
    patch_cell,
    enc_in,
    enc_bias,
    enc_out,
    pos_table,
    norm_gain,
    w_pair,
    w_keys,
    w_step,
    step_bias,
    decay_code,
    skip_gain,
    out_gain,
    w_out,
):
    frame_count = frames.shape[0]
    own_count = frames.shape[1]
    heads_all = w_step.shape[1]
    head_dim = w_pair.shape[1] // (2 * heads_all)
    spread = lax.axis_size("space")
    local_heads = heads_all // spread
    head_start = lax.axis_index("space") * local_heads
    pos_rows = jnp.take(pos_table, patch_cell, axis=0)
    decay_rates = lax.dynamic_slice_in_dim(rate_table(decay_code), head_start, local_heads)
    skip_row = lax.dynamic_slice_in_dim(skip_gain, head_start, local_heads)
    gain_rows = lax.dynamic_slice_in_dim(
        out_gain, head_start * head_dim, local_heads * head_dim
    ).reshape(local_heads, head_dim)
    all_frames, all_pos = (
        lax.all_gather(frames, "space", axis=1, tiled=True),
        lax.all_gather(pos_rows, "space", axis=0, tiled=True),
    )
    all_encoded, everyone = encode(all_frames, all_pos, enc_in, enc_bias, enc_out, norm_gain)
    encoded = lax.dynamic_slice_in_dim(
        all_encoded, lax.axis_index("space") * own_count, own_count, 1
    )
    pair_weight = lax.dynamic_slice_in_dim(
        w_pair, head_start * 2 * head_dim, local_heads * 2 * head_dim, 1
    )
    step_weight = lax.dynamic_slice_in_dim(w_step, head_start, local_heads, 1)
    step_shift = lax.dynamic_slice_in_dim(step_bias, head_start, local_heads)
    pair_cols = (
        jnp.dot(everyone, pair_weight, preferred_element_type=jnp.float32)
        .astype(jnp.bfloat16)
        .reshape(frame_count, own_count * spread, local_heads, 2 * head_dim)
    )
    key_rows = jnp.dot(everyone, w_keys, preferred_element_type=jnp.float32).astype(jnp.bfloat16)
    step_sizes = jax.nn.sigmoid(
        jnp.dot(everyone, step_weight, preferred_element_type=jnp.float32) + step_shift
    ).astype(jnp.bfloat16)
    patch_total = key_rows.shape[1]
    width = key_rows.shape[2] // 2
    patch_ids = jnp.arange(patch_total, dtype=jnp.int32)

    def first_pass(patch_id):
        pair_one = lax.dynamic_index_in_dim(pair_cols, patch_id, 1, keepdims=False)
        step_one = lax.dynamic_index_in_dim(step_sizes, patch_id, 1, keepdims=False)
        key_one = lax.dynamic_index_in_dim(key_rows, patch_id, 1, keepdims=False)
        x_vals = pair_one[..., :head_dim]
        b_rows = key_one[:, :width]
        c_rows = key_one[:, width:]
        cumlog = jnp.cumsum(step_one.astype(jnp.float32) * decay_rates[None, :], axis=0)
        scores = jnp.dot(c_rows, b_rows.T, preferred_element_type=jnp.float32)
        causal = lax.broadcasted_iota(
            jnp.int32, (frame_count, frame_count), 0
        ) >= lax.broadcasted_iota(jnp.int32, (frame_count, frame_count), 1)
        log_gap = cumlog.T[:, :, None] - cumlog.T[:, None, :]
        weights = (
            jnp.where(causal[None], jnp.exp(jnp.where(causal[None], log_gap, 0.0)), 0.0)
            * scores[None]
        ).astype(jnp.bfloat16)
        inner_part = jnp.einsum("hts,shd->thd", weights, x_vals, preferred_element_type=jnp.float32)
        to_end = jnp.exp(cumlog[-1][None, :] - cumlog)
        decayed_keys = (to_end[:, :, None] * b_rows.astype(jnp.float32)[:, None, :]).astype(
            jnp.bfloat16
        )
        block_state = jnp.einsum(
            "shn,shd->hnd", decayed_keys, x_vals, preferred_element_type=jnp.float32
        )
        return (inner_part, block_state, jnp.exp(cumlog[-1]), cumlog)

    inner_parts, block_states, decay_totals, cumlogs = lax.map(first_pass, patch_ids)

    def combine(earlier, later_part):
        return (
            earlier[0] * later_part[1][:, :, None, None] + later_part[0],
            earlier[1] * later_part[1],
        )

    states_in, _ = carried_in(
        (block_states, decay_totals),
        "tm",
        combine,
        (jnp.zeros_like(block_states), jnp.ones_like(decay_totals)),
    )

    def second_pass(packed):
        patch_id, inner_part, cumlog, state_in = packed
        pair_one = lax.dynamic_index_in_dim(pair_cols, patch_id, 1, keepdims=False)
        key_one = lax.dynamic_index_in_dim(key_rows, patch_id, 1, keepdims=False)
        x_vals = pair_one[..., :head_dim]
        z_vals = pair_one[..., head_dim:]
        c_rows = key_one[:, width:]
        carried = jnp.exp(cumlog)[:, :, None] * jnp.einsum(
            "tn,hnd->thd", c_rows.astype(jnp.float32), state_in, precision=lax.Precision.HIGHEST
        )
        summed = inner_part + carried + skip_row[None, :, None] * x_vals.astype(jnp.float32)
        gated = summed * jax.nn.silu(z_vals.astype(jnp.float32))
        scaled = (
            gated
            * lax.rsqrt(jnp.mean(gated * gated, axis=-1, keepdims=True) + 1e-05)
            * gain_rows[None]
        )
        return scaled.astype(jnp.bfloat16).reshape(frame_count, local_heads * head_dim)

    outputs = lax.map(second_pass, (patch_ids, inner_parts, cumlogs, states_in))
    merged = jnp.dot(
        lax.all_to_all(outputs, "space", split_axis=0, concat_axis=2, tiled=True),
        w_out,
        preferred_element_type=jnp.float32,
    )
    return (encoded.astype(jnp.float32) + jnp.swapaxes(merged, 0, 1)).astype(jnp.bfloat16)


def solution(mesh):
    placed = (
        P("tm", "space", None),
        P("space"),
        P(),
        P(),
        P(),
        P(),
        P(),
        P(),
        P(),
        P(),
        P(),
        P(),
        P(),
        P(),
        P(),
    )
    return jax.shard_map(
        body, mesh=mesh, in_specs=placed, out_specs=P("tm", "space", None), check_vma=False
    )
```

profile of v0, /device:TPU:0, one launch (start us, length us, event | category | flops | bytes accessed | tf_op | source)
XLA Modules:
  0.0 312.7 jit_solution(12823100967736022865)
XLA Ops:
  8.7 14.9 %all-gather.2 = bf16[4,1,1024]{2,1,0:T(2,128)(2,1)S(1)} all-gather(bf16[1,1,1024]{2,1,0:T(2,128)(2,1)S(1)} %fusion.74), channel_id=1, replica_groups=mesh['tm'=8,'space'=4] {'space'}, dimensions={0}, use_global_device_ids=true | all-gather | bytes 10240 | tf_op jit(solution)/shard_map/all_gather | solution.py:75
  25.1 14.6 %all-gather.7.cloned.1.call-done = bf16[512,4,256]{2,0,1:T(8,128)(2,1)} async-done(((bf16[512,1,256]{2,0,1:T(8,128)(2,1)}), bf16[512,4,256]{2,0,1:T(8,128)(2,1)}) %all-gather.7.cloned.1.call-update) | async-done | bytes 1048592 | tf_op jit(solution)/shard_map/all_gather | solution.py:74
  39.7 9.6 %fusion.22 = (f32[512,4]{0,1:T(4,128)S(1)}, bf16[512,4,1024]{2,0,1:T(8,128)(2,1)}) fusion(f32[4,1024]{1,0:T(4,128)S(1)} %bitcast.143, bf16[1024,1024]{1,0:T(8,128)(2,1)S(1)} %copy-done, f32[1024]{0:T(1024)} %param.24, bf16[512,4,256]{2,0,1:T(8,128)(2,1)} %all-gather.7.cloned.1.call-done, bf16[256,1024]{1,0:T(8,128)(2,1)} %param.23), kind=kOutput, calls=%fused_computation.54 | convolution fusion | flops 5400164352 | bytes 7892992 | tf_op jit(solution)/shard_map/dot_general | solution.py:34
  49.3 9.5 %convolution_convert_fusion = bf16[512,4,1024]{2,0,1:T(8,128)(2,1)} fusion(bf16[512,4,1024]{2,0,1:T(8,128)(2,1)} %get-tuple-element.383, f32[1024]{0:T(1024)S(1)} %copy-done.4, f32[512,4]{0,1:T(4,128)S(1)} %add_rsqrt_fusion.1, bf16[1024,4096]{1,0:T(8,128)(2,1)} %param.28, s32[]{:T(128)S(6)} %select_n.76), kind=kOutput, calls=%fused_computation.68 | convolution fusion | flops 4305453056 | bytes 10498052 | tf_op jit(solution)/shard_map/dot_general | solution.py:87
  58.8 6.3 %copy.39 = bf16[512,4,1024]{0,2,1:T(8,128)(2,1)} copy(bf16[512,4,1024]{2,0,1:T(8,128)(2,1)} %convolution_convert_fusion) | data formatting | bytes 8388608 | tf_op jit(solution)/shard_map/while | solution.py:126
  65.0 3.7 %fusion.48 = bf16[512,4,256]{2,0,1:T(8,128)(2,1)S(1)} fusion(bf16[512,4,1024]{2,0,1:T(8,128)(2,1)} %get-tuple-element.383, f32[1024]{0:T(1024)S(1)} %copy-done.4, f32[512,4]{0,1:T(4,128)S(1)} %add_rsqrt_fusion.1, bf16[1024,256]{1,0:T(8,128)(2,1)S(1)} %copy-done.3), kind=kOutput, calls=%fused_computation.76 | convolution fusion | flops 1082654720 | bytes 5779456 | tf_op jit(solution)/shard_map/dot_general | solution.py:91
  68.8 2.0 fusion.66
  70.8 45.2 %while.41 = (s32[]{:T(128)}, f32[4,512,8,64]{1,3,2,0:T(8,128)}, f32[4,8,128,64]{2,3,1,0:T(8,128)}, f32[4,8]{1,0:T(4,128)S(1)}, f32[4,512,8]{1,2,0:T(8,128)S(1)},...) while((s32[]{:T(128)}, f32[4,512,8,64]{1,3,2,0:T(8,128)}, ...), condition=%wide.region_4.5_spmd, body=%wide.region_1.0_spmd.sunk | while | flops 415056000 | bytes 8745359 | solution.py:126
  73.5 1.1 reduce-window.12
  75.3 1.3 dynamic-slice_bitcast_fusion.11
  76.7 3.6 %fusion.106 = f32[4,512,8,64]{1,3,2,0:T(8,128)} fusion(f32[4,512,8,64]{1,3,2,0:T(8,128)} %get-tuple-element.564, s32[]{:T(128)} %get-tuple-element.563, f32[512,512]{1,0:T(8,128)S(1)} %fusion.104, f32[8,512]{1,0:T(8,128)S(1)} %get-tuple-element.528, pred[512,512]{1,0:T(8,128)(4,1)S(1)} %iota_compare_fusion.2, ...), kind=kOutput, calls=%fused_computation.27.clone.1 | convolution fusion | flops 278921216 | bytes 2916864 | tf_op jit(solution)/shard_map/while/body/eval_jaxpr/hts,shd->thd/dot_general | solution.py:116
  80.6 1.5 fusion.107
  84.8 1.1 reduce-window.12
  86.5 1.3 dynamic-slice_bitcast_fusion.11
  87.9 3.6 %fusion.106 = f32[4,512,8,64]{1,3,2,0:T(8,128)} fusion(f32[4,512,8,64]{1,3,2,0:T(8,128)} %get-tuple-element.564, s32[]{:T(128)} %get-tuple-element.563, f32[512,512]{1,0:T(8,128)S(1)} %fusion.104, f32[8,512]{1,0:T(8,128)S(1)} %get-tuple-element.528, pred[512,512]{1,0:T(8,128)(4,1)S(1)} %iota_compare_fusion.2, ...), kind=kOutput, calls=%fused_computation.27.clone.1 | convolution fusion | flops 278921216 | bytes 2916864 | tf_op jit(solution)/shard_map/while/body/eval_jaxpr/hts,shd->thd/dot_general | solution.py:116
  91.8 1.5 fusion.107
  96.0 1.1 reduce-window.12
  97.8 1.3 dynamic-slice_bitcast_fusion.11
  99.2 3.7 %fusion.106 = f32[4,512,8,64]{1,3,2,0:T(8,128)} fusion(f32[4,512,8,64]{1,3,2,0:T(8,128)} %get-tuple-element.564, s32[]{:T(128)} %get-tuple-element.563, f32[512,512]{1,0:T(8,128)S(1)} %fusion.104, f32[8,512]{1,0:T(8,128)S(1)} %get-tuple-element.528, pred[512,512]{1,0:T(8,128)(4,1)S(1)} %iota_compare_fusion.2, ...), kind=kOutput, calls=%fused_computation.27.clone.1 | convolution fusion | flops 278921216 | bytes 2916864 | tf_op jit(solution)/shard_map/while/body/eval_jaxpr/hts,shd->thd/dot_general | solution.py:116
  103.1 1.5 fusion.107
  107.3 1.1 reduce-window.12
  109.1 1.3 dynamic-slice_bitcast_fusion.11
  110.5 3.6 %fusion.106 = f32[4,512,8,64]{1,3,2,0:T(8,128)} fusion(f32[4,512,8,64]{1,3,2,0:T(8,128)} %get-tuple-element.564, s32[]{:T(128)} %get-tuple-element.563, f32[512,512]{1,0:T(8,128)S(1)} %fusion.104, f32[8,512]{1,0:T(8,128)S(1)} %get-tuple-element.528, pred[512,512]{1,0:T(8,128)(4,1)S(1)} %iota_compare_fusion.2, ...), kind=kOutput, calls=%fused_computation.27.clone.1 | convolution fusion | flops 278921216 | bytes 2916864 | tf_op jit(solution)/shard_map/while/body/eval_jaxpr/hts,shd->thd/dot_general | solution.py:116
  114.3 1.5 fusion.107
  117.0 8.8 %all-gather.3 = f32[8,4,8]{2,1,0:T(4,128)S(1)} all-gather(f32[1,4,8]{2,1,0:T(4,128)S(1)} %bitcast.144), channel_id=2, replica_groups=mesh['tm'=8,'space'=4] {'tm'}, dimensions={0}, use_global_device_ids=true | all-gather | bytes 1152 | tf_op jit(solution)/shard_map/all_gather | solution.py:9
  125.8 44.3 %all-gather.9.cloned.1.call-done = f32[32,8,128,64]{2,3,1,0:T(8,128)} async-done(((f32[4,8,128,64]{2,3,1,0:T(8,128)}), f32[32,8,128,64]{2,3,1,0:T(8,128)}) %all-gather.9.cloned.1.call-update) | async-done | bytes 8388624 | tf_op jit(solution)/shard_map/all_gather | solution.py:9
  170.1 40.0 %while.43 = (s32[]{:T(128)}, f32[4,8,128,64]{3,2,1,0:T(8,128)}, s32[]{:T(128)}, f32[8,4,8]{2,1,0:T(4,128)S(1)}, f32[8,4,8,128,64]{3,4,2,1,0:T(8,128)}, /*index=5*/s32[]{:T(128)}, s32[]{:T(128)}) while((s32[]{:T(128)}, f32[4,8,128,64]{3,2,1,0:T(8,128)}, s32[]{:T(128)}, f32[8,4,8]{2,1,0:T(4,128)S(1)}, ...), condition=%wide.region_6.7_spmd.clone, body=%wide.region_5.6_spmd.clone.sunk | while | flops 1048580 | bytes 7340521 | solution.py:21
  170.1 1.3 constant_dynamic-slice_fusion.5
  172.0 1.7 fusion.111
  173.7 1.3 constant_dynamic-slice_fusion.5
  175.6 3.3 %fusion.111 = f32[4,8,128,64]{3,2,1,0:T(8,128)} fusion(f32[1,4,8,128,64]{4,3,2,1,0:T(8,128)S(1)} %copy.50, f32[4,8,128,64]{3,2,1,0:T(8,128)} %get-tuple-element.599, f32[4,8]{1,0:T(4,128)S(1)} %dynamic-slice_bitcast_fusion.14, pred[]{:T(512)S(6)} %compare.4, pred[]{:T(512)S(6)} %lt.70), kind=kLoop, calls=%fused_computation.19.clone.1 | loop fusion | flops 1048576 | bytes 3145858 | tf_op jit(solution)/shard_map/while/body/eval_jaxpr/jit(_where)/select_n | solution.py:19
  178.9 1.3 constant_dynamic-slice_fusion.5
  180.8 3.3 %fusion.111 = f32[4,8,128,64]{3,2,1,0:T(8,128)} fusion(f32[1,4,8,128,64]{4,3,2,1,0:T(8,128)S(1)} %copy.50, f32[4,8,128,64]{3,2,1,0:T(8,128)} %get-tuple-element.599, f32[4,8]{1,0:T(4,128)S(1)} %dynamic-slice_bitcast_fusion.14, pred[]{:T(512)S(6)} %compare.4, pred[]{:T(512)S(6)} %lt.70), kind=kLoop, calls=%fused_computation.19.clone.1 | loop fusion | flops 1048576 | bytes 3145858 | tf_op jit(solution)/shard_map/while/body/eval_jaxpr/jit(_where)/select_n | solution.py:19
  184.1 1.3 constant_dynamic-slice_fusion.5
  186.0 3.3 %fusion.111 = f32[4,8,128,64]{3,2,1,0:T(8,128)} fusion(f32[1,4,8,128,64]{4,3,2,1,0:T(8,128)S(1)} %copy.50, f32[4,8,128,64]{3,2,1,0:T(8,128)} %get-tuple-element.599, f32[4,8]{1,0:T(4,128)S(1)} %dynamic-slice_bitcast_fusion.14, pred[]{:T(512)S(6)} %compare.4, pred[]{:T(512)S(6)} %lt.70), kind=kLoop, calls=%fused_computation.19.clone.1 | loop fusion | flops 1048576 | bytes 3145858 | tf_op jit(solution)/shard_map/while/body/eval_jaxpr/jit(_where)/select_n | solution.py:19
  189.2 1.3 constant_dynamic-slice_fusion.5
  191.2 3.3 %fusion.111 = f32[4,8,128,64]{3,2,1,0:T(8,128)} fusion(f32[1,4,8,128,64]{4,3,2,1,0:T(8,128)S(1)} %copy.50, f32[4,8,128,64]{3,2,1,0:T(8,128)} %get-tuple-element.599, f32[4,8]{1,0:T(4,128)S(1)} %dynamic-slice_bitcast_fusion.14, pred[]{:T(512)S(6)} %compare.4, pred[]{:T(512)S(6)} %lt.70), kind=kLoop, calls=%fused_computation.19.clone.1 | loop fusion | flops 1048576 | bytes 3145858 | tf_op jit(solution)/shard_map/while/body/eval_jaxpr/jit(_where)/select_n | solution.py:19
  194.4 1.3 constant_dynamic-slice_fusion.5
  196.4 3.3 %fusion.111 = f32[4,8,128,64]{3,2,1,0:T(8,128)} fusion(f32[1,4,8,128,64]{4,3,2,1,0:T(8,128)S(1)} %copy.50, f32[4,8,128,64]{3,2,1,0:T(8,128)} %get-tuple-element.599, f32[4,8]{1,0:T(4,128)S(1)} %dynamic-slice_bitcast_fusion.14, pred[]{:T(512)S(6)} %compare.4, pred[]{:T(512)S(6)} %lt.70), kind=kLoop, calls=%fused_computation.19.clone.1 | loop fusion | flops 1048576 | bytes 3145858 | tf_op jit(solution)/shard_map/while/body/eval_jaxpr/jit(_where)/select_n | solution.py:19
  199.6 1.3 constant_dynamic-slice_fusion.5
  201.6 3.3 %fusion.111 = f32[4,8,128,64]{3,2,1,0:T(8,128)} fusion(f32[1,4,8,128,64]{4,3,2,1,0:T(8,128)S(1)} %copy.50, f32[4,8,128,64]{3,2,1,0:T(8,128)} %get-tuple-element.599, f32[4,8]{1,0:T(4,128)S(1)} %dynamic-slice_bitcast_fusion.14, pred[]{:T(512)S(6)} %compare.4, pred[]{:T(512)S(6)} %lt.70), kind=kLoop, calls=%fused_computation.19.clone.1 | loop fusion | flops 1048576 | bytes 3145858 | tf_op jit(solution)/shard_map/while/body/eval_jaxpr/jit(_where)/select_n | solution.py:19
  204.8 1.3 constant_dynamic-slice_fusion.5
  206.8 3.3 %fusion.111 = f32[4,8,128,64]{3,2,1,0:T(8,128)} fusion(f32[1,4,8,128,64]{4,3,2,1,0:T(8,128)S(1)} %copy.50, f32[4,8,128,64]{3,2,1,0:T(8,128)} %get-tuple-element.599, f32[4,8]{1,0:T(4,128)S(1)} %dynamic-slice_bitcast_fusion.14, pred[]{:T(512)S(6)} %compare.4, pred[]{:T(512)S(6)} %lt.70), kind=kLoop, calls=%fused_computation.19.clone.1 | loop fusion | flops 1048576 | bytes 3145858 | tf_op jit(solution)/shard_map/while/body/eval_jaxpr/jit(_where)/select_n | solution.py:19
  210.0 2.2 copy.37
  212.2 33.7 %while.42 = (s32[]{:T(128)}, bf16[4,512,512]{1,2,0:T(8,128)(2,1)}, f32[4,512,8,64]{1,3,2,0:T(8,128)}, f32[4,512,8]{1,2,0:T(8,128)S(1)}, s32[4]{0:T(128)S(1)}, /*...) while((s32[]{:T(128)}, bf16[4,512,512]{1,2,0:T(8,128)(2,1)}, ...), condition=%wide.region_9.10_spmd, body=%wide.region_7.9_spmd.sunk | while | flops 406851584 | bytes 11524831 | solution.py:160
  214.8 1.0 dynamic-slice_bitcast_fusion.13
  216.4 1.3 dynamic-slice_bitcast_fusion.12
  217.7 1.8 multiply_reduce_fusion.2
  219.8 0.8 constant_dynamic-update-slice_fusion.2
  223.2 1.0 dynamic-slice_bitcast_fusion.13
  224.8 1.3 dynamic-slice_bitcast_fusion.12
  226.1 1.8 multiply_reduce_fusion.2
  228.2 0.9 constant_dynamic-update-slice_fusion.2
  231.6 1.0 dynamic-slice_bitcast_fusion.13
  233.2 1.3 dynamic-slice_bitcast_fusion.12
  234.5 1.8 multiply_reduce_fusion.2
  236.7 0.9 constant_dynamic-update-slice_fusion.2
  240.0 1.0 dynamic-slice_bitcast_fusion.13
  241.6 1.3 dynamic-slice_bitcast_fusion.12
  243.0 1.8 multiply_reduce_fusion.2
  245.1 0.8 constant_dynamic-update-slice_fusion.2
  245.9 4.6 %all-to-all-start = ((bf16[4,512,512]{1,2,0:T(8,128)(2,1)}), bf16[4,512,512]{1,2,0:T(8,128)(2,1)}, u32[]{:S(2)}, u32[]{:S(2)}) async-start(bf16[4,512,512]{1,2,0:T(8,128)(2,1)} %get-tuple-element.211), calls=%async_computation | async-start | bytes 4194304 | tf_op jit(solution)/shard_map/all_to_all | solution.py:162
  250.5 48.8 %all-to-all-done = bf16[4,512,512]{1,2,0:T(8,128)(2,1)} async-done(((bf16[4,512,512]{1,2,0:T(8,128)(2,1)}), bf16[4,512,512]{1,2,0:T(8,128)(2,1)}, u32[]{:S(2)}, u32[]{:S(2)}) %all-to-all-start) | async-done | bytes 2097184 | tf_op jit(solution)/shard_map/all_to_all | solution.py:162
  299.3 6.6 %fusion.44 = bf16[512,1,1024]{2,0,1:T(8,128)(2,1)} fusion(bf16[512,2048]{0,1:T(8,128)(2,1)} %bitcast.35, bf16[2048,1024]{1,0:T(8,128)(2,1)} %param.35, bf16[512,4,1024]{2,0,1:T(8,128)(2,1)} %get-tuple-element.383, s32[]{:T(128)S(6)} %select_n.75), kind=kOutput, calls=%fused_computation.72 | convolution fusion | flops 2149056512 | bytes 8388612 | tf_op jit(solution)/shard_map/dot_general | solution.py:161
  (138 shorter events, 21.9 us)
Async XLA Ops:
  6.5 33.1 %copy-start = (bf16[1024,1024]{1,0:T(8,128)(2,1)S(1)}, bf16[1024,1024]{1,0:T(8,128)(2,1)}, u32[]{:S(2)}) copy-start(bf16[1024,1024]{1,0:T(8,128)(2,1)} %param.25) | copy-start | bytes 6291460
  6.5 33.1 %all-gather.7.cloned.1.call-start = ((), (), s32[]{:S(2)}) async-start(), calls=%async_computation.1 | async-start | bytes 1310720 | tf_op jit(solution)/shard_map/all_gather | solution.py:74
  7.3 162.8 %all-gather.9.cloned.1.call-start = ((), (), s32[]{:S(2)}) async-start(), calls=%async_computation.2 | async-start | bytes 9437184 | tf_op jit(solution)/shard_map/all_gather | solution.py:9
  39.7 9.6 %copy-start.4 = (f32[1024]{0:T(1024)S(1)}, f32[1024]{0:T(1024)}, u32[]{:S(2)}) copy-start(f32[1024]{0:T(1024)} %param.27) | copy-start | bytes 12292
  58.8 6.3 %copy-start.3 = (bf16[1024,256]{1,0:T(8,128)(2,1)S(1)}, bf16[1024,256]{1,0:T(8,128)(2,1)}, u32[]{:S(2)}) copy-start(bf16[1024,256]{1,0:T(8,128)(2,1)} %param.29) | copy-start | bytes 1572868
  65.0 3.7 %copy-start.6 = (bf16[512,4,1024]{2,0,1:T(8,128)(2,1)S(1)}, bf16[512,4,1024]{2,0,1:T(8,128)(2,1)}, u32[]{:S(2)}) copy-start(bf16[512,4,1024]{2,0,1:T(8,128)(2,1)} %get-tuple-element.383) | copy-start | bytes 12582916
  70.8 45.3 %copy-start.5 = (f32[32]{0:T(128)S(1)}, f32[32]{0:T(128)}, u32[]{:S(2)}) copy-start(f32[32]{0:T(128)} %param.33) | copy-start | bytes 388
  116.0 54.0 %copy-start.2 = (bf16[512,4,256]{2,0,1:T(8,128)(2,1)}, bf16[512,4,256]{2,0,1:T(8,128)(2,1)S(1)}, u32[]{:S(2)}) copy-start(bf16[512,4,256]{2,0,1:T(8,128)(2,1)S(1)} %get-tuple-element.654) | copy-start | bytes 3145732
  245.9 53.4 %all-to-all-start = ((bf16[4,512,512]{1,2,0:T(8,128)(2,1)}), bf16[4,512,512]{1,2,0:T(8,128)(2,1)}, u32[]{:S(2)}, u32[]{:S(2)}) async-start(bf16[4,512,512]{1,2,0:T(8,128)(2,1)} %get-tuple-element.211), calls=%async_computation | async-start | bytes 4194304 | tf_op jit(solution)/shard_map/all_to_all | solution.py:162
  299.3 6.6 %copy-start.1 = (bf16[1024,1024]{1,0:T(8,128)(2,1)S(1)}, bf16[1024,1024]{1,0:T(8,128)(2,1)}, u32[]{:S(2)}) copy-start(bf16[1024,1024]{1,0:T(8,128)(2,1)} %param.25) | copy-start | bytes 6291460
Sparse Core Ops, SparseCore 0:
  8.9 30.7 all-gather.6
  116.2 53.8 all-gather.8
where the time goes:
time: 315 us; the launch traced here: 313 us
  waiting for transfers between devices  108 us (34%)
  matrix products  55.4 us (18%)
  local copies, waits for them, and re-layouts  50.2 us (16%)
  other arithmetic  40.3 us (13%)
  blocking collectives  23.7 us (8%)
  loops' own time  15.9 us (5%)
  between operations  14.2 us (5%)
  starting transfers between devices  4.63 us (1%)
    all_to_all x1, waiting for transfers between devices, body(): lax.all_to_all(outputs, 'space', split_axis=0, concat_axis=2, tiled=True)  48.8 us
    all_gather x1, waiting for transfers between devices, carried_in(): everything = jax.tree.map(lambda part: lax.all_gather(part, axis), array)  44.3 us
    select_n x8, other arithmetic, turn(): return jax.tree.map(lambda a, b: jnp.where(reached, a, b), new, before)  24.5 us
    dynamic_slice x16, local copies, waits for them, and re-layouts, turn(): new = combine(before, jax.tree.map(lambda part: part[k], everything))  15.2 us
    all_gather x1, blocking collectives, body(): lax.all_gather(pos_rows, 'space', axis=0, tiled=True)  14.9 us
    dot_general x4, matrix products, first_pass(): jnp.einsum('hts,shd->thd', weights, x_vals, preferred_element_type=jnp.fl...  14.6 us
    all_gather x1, waiting for transfers between devices, body(): lax.all_gather(frames, 'space', axis=1, tiled=True)  14.6 us
    dot_general x1, matrix products, encode(): jnp.dot(hidden, enc_out, preferred_element_type=jnp.float32)  9.57 us
  transfers between devices with their start and end apart: 3, of which 3 were waited for; matrix products, arithmetic and copies ran while one was open for 1% of the time, Pallas kernels for 0%

commit v1 on v0

v1 whole, which is shorter than its diff:
```python
import jax
import jax.numpy as jnp
from jax import lax
from jax.sharding import PartitionSpec as P

BF = jnp.bfloat16
F32 = jnp.float32


def dot(a, b):
    return jnp.dot(a, b, preferred_element_type=F32)


def carried_state(state, decay, peers):
    here = lax.axis_index("tm")

    def shifted(value, value_decay, by):
        pairs = [(i, i + by) for i in range(peers - by)]
        got, got_decay = lax.ppermute((value.astype(BF), value_decay), "tm", pairs)
        return got.astype(F32), jnp.where(here < by, 1.0, got_decay)

    before, before_decay = shifted(state, decay, 1)
    reach = 1
    while reach < peers:
        got, got_decay = shifted(before, before_decay, reach)
        before = before + before_decay * got
        before_decay = before_decay * got_decay
        reach *= 2
    return before


def body(frames, patch_cell, enc_in, enc_bias, enc_out, pos_table, norm_gain, w_pair, w_keys, w_step,
         step_bias, decay_code, skip_gain, out_gain, w_out):
    count = frames.shape[0]
    heads = w_step.shape[1]
    head_dim = w_pair.shape[1] // (2 * heads)
    width = w_keys.shape[1] // 2
    flat = heads * head_dim
    rate = -0.0005 - 0.003 * decay_code.astype(F32)
    pos = jnp.take(pos_table, patch_cell, axis=0)
    tokens = frames.reshape(count, frames.shape[2])
    hidden = jax.nn.gelu(dot(tokens, enc_in) + enc_bias, approximate=True).astype(BF)
    encoded = (dot(hidden, enc_out) + pos.astype(F32)).astype(BF)
    wide = encoded.astype(F32)
    normed = (wide * lax.rsqrt(jnp.mean(wide * wide, axis=-1, keepdims=True) + 1e-05) * norm_gain).astype(BF)
    pair = dot(normed, w_pair).astype(BF).reshape(count, heads, 2 * head_dim)
    keys = dot(normed, w_keys).astype(BF)
    step = jax.nn.sigmoid(dot(normed, w_step) + step_bias).astype(BF)
    lower = lax.broadcasted_iota(jnp.int32, (count, count), 0) >= lax.broadcasted_iota(jnp.int32, (count, count), 1)
    cum = dot(lower.astype(BF), step) * rate
    grow, fall = jnp.exp(-cum), jnp.exp(cum)
    x = pair[..., :head_dim]
    gate = pair[..., head_dim:]
    scaled = (x.astype(F32) * grow[:, :, None]).astype(BF).reshape(count, flat)
    b_rows, c_rows = keys[:, :width], keys[:, width:]
    scores = jnp.where(lower, dot(c_rows, b_rows.T), 0.0).astype(BF)
    inner = dot(scores, scaled).reshape(count, heads, head_dim)
    state = dot(b_rows.T, scaled) * jnp.repeat(fall[-1], head_dim)[None]
    entering = carried_state(state, jnp.repeat(fall[-1], head_dim)[None], lax.axis_size("tm"))
    carried = dot(c_rows, entering.astype(BF)).reshape(count, heads, head_dim)
    y = (inner + carried) * fall[:, :, None] + skip_gain[None, :, None] * x.astype(F32)
    g = y * jax.nn.silu(gate.astype(F32))
    mixed = g * lax.rsqrt(jnp.mean(g * g, axis=-1, keepdims=True) + 1e-05) * out_gain.reshape(heads, head_dim)
    merged = dot(mixed.astype(BF).reshape(count, flat), w_out)
    return (wide + merged).astype(BF).reshape(frames.shape[0], 1, -1)


def solution(mesh):
    placed = (P("tm", "space", None), P("space")) + (P(),) * 13
    return jax.shard_map(body, mesh=mesh, in_specs=placed, out_specs=P("tm", "space", None), check_vma=False)
```

time: 315 us -> 101 us (0.32)
  waiting for transfers between devices: 108 us -> 18.1 us
  local copies, waits for them, and re-layouts: 50.2 us -> 11.1 us
  other arithmetic: 40.3 us -> 6.98 us
  starting transfers between devices: 4.63 us -> 31.7 us
  matrix products: 55.4 us -> 31.6 us
  blocking collectives: 23.7 us -> 0 us
  loops' own time: 15.9 us -> 0 us
  between operations: 14.2 us -> 1.03 us
    all_gather x2 -> x0, waiting for transfers between devices: 58.8 us -> none  [the longest x1 44.3 us: carried_in(): everything = jax.tree.map(lambda part: lax.all_gather(part, axis), array)]
    all_to_all x1 -> x0, waiting for transfers between devices: 48.8 us -> none  [body(): lax.all_to_all(outputs, 'space', split_axis=0, concat_axis=2, tiled=True)]
    ppermute x0 -> x7, starting transfers between devices: none -> 31.7 us  [shifted(): got, got_decay = lax.ppermute((value.astype(BF), value_decay), 'tm', pairs)]
    select_n x8 -> x1, other arithmetic: 24.5 us -> 0.01 us  [shifted(): return (got.astype(F32), jnp.where(here < by, 1.0, got_decay))]
    all_gather x2 -> x0, blocking collectives: 23.7 us -> none  [the longest x1 14.9 us: body(): lax.all_gather(pos_rows, 'space', axis=0, tiled=True)]
    dynamic_slice x32 -> x0, local copies, waits for them, and re-layouts: 21.8 us -> none  [the longest x16 15.2 us: turn(): new = combine(before, jax.tree.map(lambda part: part[k], everything))]
    dot_general x17 -> x8, matrix products: 53.1 us -> 31.6 us  [dot(): return jnp.dot(a, b, preferred_element_type=F32)]
    ppermute x0 -> x7, waiting for transfers between devices: none -> 18.1 us  [shifted(): got, got_decay = lax.ppermute((value.astype(BF), value_decay), 'tm', pairs)]
  transfers between devices with their start and end apart: 3 -> 7, of which waited for: 3 -> 6; matrix products, arithmetic and copies ran while one was open for 1% -> 0% of each run, Pallas kernels for 0% -> 0%
where the time goes in v1:
time: 101 us; the launch traced here: 100 us
  starting transfers between devices  31.7 us (31%)
  matrix products  31.6 us (31%)
  waiting for transfers between devices  18.1 us (18%)
  local copies, waits for them, and re-layouts  11.1 us (11%)
  other arithmetic  6.98 us (7%)
  between operations  1.03 us (1%)
    ppermute x7, starting transfers between devices, shifted(): got, got_decay = lax.ppermute((value.astype(BF), value_decay), 'tm', pairs)  31.7 us
    dot_general x8, matrix products, dot(): return jnp.dot(a, b, preferred_element_type=F32)  31.6 us
    ppermute x7, waiting for transfers between devices, shifted(): got, got_decay = lax.ppermute((value.astype(BF), value_decay), 'tm', pairs)  18.1 us
    reshape x1, local copies, waits for them, and re-layouts, body(): pair = dot(normed, w_pair).astype(BF).reshape(count, heads, 2 * head_dim)  6.53 us
    unnamed x26, local copies, waits for them, and re-layouts  4.07 us
    convert_element_type x1, other arithmetic, body(): merged = dot(mixed.astype(BF).reshape(count, flat), w_out)  2.84 us
    convert_element_type x1, other arithmetic, body(): scaled = (x.astype(F32) * grow[:, :, None]).astype(BF).reshape(count, flat)  2.12 us
  transfers between devices with their start and end apart: 7, of which 6 were waited for; matrix products, arithmetic and copies ran while one was open for 0% of the time, Pallas kernels for 0%

profile of v1, /device:TPU:0, one launch (start us, length us, event | category | flops | bytes accessed | tf_op | source)
XLA Modules:
  0.0 100.4 jit_solution(17251082976137837463)
XLA Ops:
  0.0 0.0 copy-start
  0.8 0.7 fusion.49
  1.5 0.1 copy-done
  1.6 0.0 copy-start.7
  1.6 3.0 %fusion.15 = (f32[512]{0:T(512)S(1)}, bf16[512,1024]{1,0:T(8,128)(2,1)S(1)}) fusion(f32[1024]{0:T(1024)S(1)} %bitcast.51, bf16[1024,1024]{1,0:T(8,128)(2,1)S(1)} %copy-done, bf16[256,1024]{1,0:T(8,128)(2,1)} %param.17, f32[1024]{0:T(1024)} %param.18, bf16[512,1,256]{2,0,1:T(8,128)(2,1)} %param.15), kind=kOutput, calls=%fused_computation.27 | convolution fusion | flops 1350041088 | bytes 3942400 | tf_op jit(solution)/shard_map/dot_general | solution.py:11
  4.6 0.0 copy-start.11
  4.6 1.0 copy-done.11
  5.6 0.0 copy-done.7
  5.6 9.6 %convolution_convert_fusion = bf16[512,4096]{1,0:T(8,128)(2,1)} fusion(bf16[1024,4096]{1,0:T(8,128)(2,1)} %param.22, bf16[512,1024]{1,0:T(8,128)(2,1)S(1)} %get-tuple-element.19, f32[1024]{0:T(1024)S(1)} %copy-done.7, f32[512]{0:T(512)S(1)} %add_rsqrt_fusion.1), kind=kOutput, calls=%fused_computation | convolution fusion | flops 4299161600 | bytes 13637632 | tf_op jit(solution)/shard_map/dot_general | solution.py:11
  15.2 0.0 copy-start.8
  15.2 0.0 copy-start.6
  15.2 0.0 copy-start.9
  15.2 6.5 %copy.23 = bf16[512,4096]{0,1:T(8,128)(2,1)} copy(bf16[512,4096]{1,0:T(8,128)(2,1)} %convolution_convert_fusion) | data formatting | bytes 8388608 | tf_op jit(solution)/shard_map/reshape | solution.py:46
  21.7 0.0 copy-done.8
  21.7 0.0 copy-start.5
  21.7 0.0 copy-done.6
  21.7 0.0 copy-done.9
  21.8 2.0 %fusion.60 = (f32[512,32]{0,1:T(8,128)S(1)}, f32[512,32]{0,1:T(8,128)S(1)}) fusion(f32[32]{0:T(128)S(1)} %multiply_subtract_fusion, bf16[1024,32]{0,1:T(8,128)(2,1)S(1)} %copy-done.6, f32[32]{0:T(128)S(1)} %copy-done.9, bf16[512,1024]{1,0:T(8,128)(2,1)} %copy-done.11, f32[1024]{0:T(1024)S(1)} %copy-done.7, f32[512]{0:T(512)S(1)} %add_rsqrt_fusion.1), kind=kOutput, calls=%fused_computation.82 | convolution fusion | flops 52805632 | bytes 1251584 | tf_op jit(solution)/shard_map/dot_general | solution.py:11
  23.7 0.2 slice_reduce_fusion
  23.9 0.1 broadcast_in_dim.39
  24.0 0.1 mul.170
  24.1 0.0 copy-done.5
  24.1 1.7 %convolution_convert_fusion.1 = bf16[512,256]{1,0:T(8,128)(2,1)S(1)} fusion(bf16[1024,256]{1,0:T(8,128)(2,1)S(1)} %copy-done.5, bf16[512,1024]{1,0:T(8,128)(2,1)} %copy-done.11, f32[1024]{0:T(1024)S(1)} %copy-done.7, f32[512]{0:T(512)S(1)} %add_rsqrt_fusion.1), kind=kOutput, calls=%fused_computation.37 | convolution fusion | flops 270663680 | bytes 1841152 | tf_op jit(solution)/shard_map/dot_general | solution.py:11
  25.8 2.1 %fusion = bf16[512,32,64]{0,2,1:T(8,128)(2,1)S(1)} fusion(f32[512,32]{0,1:T(8,128)S(1)} %get-tuple-element.17, bf16[512,32,128]{0,2,1:T(8,128)(2,1)} %bitcast.41), kind=kLoop, calls=%fused_computation.5 | loop fusion | flops 3145728 | bytes 4259840 | tf_op jit(solution)/shard_map/convert_element_type | solution.py:54
  27.9 0.0 copy-start.1
  27.9 1.3 %copy-done.1 = bf16[512,32,64]{0,2,1:T(8,128)(2,1)} copy-done((bf16[512,32,64]{0,2,1:T(8,128)(2,1)}, bf16[512,32,64]{0,2,1:T(8,128)(2,1)S(1)}, u32[]{:S(2)}) %copy-start.1) | copy-done | bytes 2097176
  29.3 0.8 fusion.6
  30.1 0.0 copy-start.3
  30.1 2.4 %collective-permute-start = (bf16[128,2048]{1,0:T(8,128)(2,1)S(1)}, bf16[128,2048]{1,0:T(8,128)(2,1)S(1)}, u32[]{:S(2)}, u32[]{:S(2)}) collective-permute-start(bf16[128,2048]{1,0:T(8,128)(2,1)S(1)} %fusion.6), channel_id=1, source_target_pairs={{0,4},{4,8},{8,12},{12,16},{16,20},{20,24},{24,28},{1,5},{5,9},{9,... | collective-permute-start | bytes 1572872 | tf_op jit(solution)/shard_map/ppermute | solution.py:19
  32.5 1.5 %collective-permute-done = bf16[128,2048]{1,0:T(8,128)(2,1)S(1)} collective-permute-done((bf16[128,2048]{1,0:T(8,128)(2,1)S(1)}, bf16[128,2048]{1,0:T(8,128)(2,1)S(1)}, u32[]{:S(2)}, u32[]{:S(2)}) %collective-permute-start) | collective-permute-done | bytes 524320 | tf_op jit(solution)/shard_map/ppermute | solution.py:19
  34.0 9.1 %collective-permute-start.2 = (bf16[128,2048]{1,0:T(8,128)(2,1)S(1)}, bf16[128,2048]{1,0:T(8,128)(2,1)S(1)}, u32[]{:S(2)}, u32[]{:S(2)}) collective-permute-start(bf16[128,2048]{1,0:T(8,128)(2,1)S(1)} %collective-permute-done), channel_id=1, source_target_pairs={{0,4},{4,8},{8,12},{12,16},{16,20},{20,24},{24,28},{1,5},{5,9},{9,... | collective-permute-start | bytes 1572872 | tf_op jit(solution)/shard_map/ppermute | solution.py:19
  43.1 0.1 broadcast_in_dim_reshape.2
  43.2 4.3 %collective-permute-start.1 = (f32[1,2048]{1,0:T(1,128)S(1)}, f32[1,2048]{1,0:T(1,128)S(1)}, u32[]{:S(2)}, u32[]{:S(2)}) collective-permute-start(f32[1,2048]{1,0:T(1,128)S(1)} %broadcast_in_dim_reshape.2), channel_id=1, source_target_pairs={{0,4},{4,8},{8,12},{12,16},{16,20},{20,24},{24,28},{1,5},{5,9},{9,... | collective-permute-start | bytes 24584 | tf_op jit(solution)/shard_map/ppermute | solution.py:19
  47.5 0.8 collective-permute-done.1
  48.4 0.0 collective-permute-done.2
  48.4 0.2 fusion.30
  48.5 7.7 %collective-permute-start.4 = (bf16[128,2048]{1,0:T(8,128)(2,1)S(1)}, bf16[128,2048]{1,0:T(8,128)(2,1)S(1)}, u32[]{:S(2)}, u32[]{:S(2)}) collective-permute-start(bf16[128,2048]{1,0:T(8,128)(2,1)S(1)} %fusion.30), channel_id=1, source_target_pairs={{0,8},{4,12},{8,16},{12,20},{16,24},{20,28},{1,9},{5,13},{9,17},{1... | collective-permute-start | bytes 1572872 | tf_op jit(solution)/shard_map/ppermute | solution.py:19
  56.2 1.7 %collective-permute-start.3 = (f32[1,2048]{1,0:T(1,128)S(1)}, f32[1,2048]{1,0:T(1,128)S(1)}, u32[]{:S(2)}, u32[]{:S(2)}) collective-permute-start(f32[1,2048]{1,0:T(1,128)S(1)} %broadcast_select_fusion.2), channel_id=1, source_target_pairs={{0,4},{4,8},{8,12},{12,16},{16,20},{20,24},{24,28},{1,5},{5,9},{9,... | collective-permute-start | bytes 24584 | tf_op jit(solution)/shard_map/ppermute | solution.py:19
  57.9 0.8 collective-permute-done.3
  58.7 8.9 %collective-permute-done.4 = bf16[128,2048]{1,0:T(8,128)(2,1)S(1)} collective-permute-done((bf16[128,2048]{1,0:T(8,128)(2,1)S(1)}, bf16[128,2048]{1,0:T(8,128)(2,1)S(1)}, u32[]{:S(2)}, u32[]{:S(2)}) %collective-permute-start.4) | collective-permute-done | bytes 524320 | tf_op jit(solution)/shard_map/ppermute | solution.py:19
  67.7 0.0 copy-start.2
  67.7 0.8 copy-done.2
  68.5 1.1 %fusion.31 = bf16[128,2048]{1,0:T(8,128)(2,1)} fusion(bf16[128,2048]{1,0:T(8,128)(2,1)S(1)} %collective-permute-done.4, bf16[128,2048]{1,0:T(8,128)(2,1)S(1)} %collective-permute-done.2, bf16[128,2048]{1,0:T(8,128)(2,1)S(1)} %collective-permute-done, f32[2048]{0:T(1024)S(1)} %bitcast.48, f32[2048]{0:T(1024)S(1)} %bitcast.46), kind=kLoop, calls=%fused_computation.51 | loop fusion | flops 2097152 | bytes 2113536 | tf_op jit(solution)/shard_map/convert_element_type | solution.py:19
  69.6 5.2 %collective-permute-start.6 = (bf16[128,2048]{1,0:T(8,128)(2,1)}, bf16[128,2048]{1,0:T(8,128)(2,1)}, u32[]{:S(2)}, u32[]{:S(2)}) collective-permute-start(bf16[128,2048]{1,0:T(8,128)(2,1)} %fusion.31), channel_id=1, source_target_pairs={{0,16},{4,20},{8,24},{12,28},{1,17},{5,21},{9,25},{13,29},{2,18},{... | collective-permute-start | bytes 1572872 | tf_op jit(solution)/shard_map/ppermute | solution.py:19
  74.8 1.3 %collective-permute-start.5 = (f32[1,2048]{1,0:T(1,128)S(1)}, f32[1,2048]{1,0:T(1,128)S(1)}, u32[]{:S(2)}, u32[]{:S(2)}) collective-permute-start(f32[1,2048]{1,0:T(1,128)S(1)} %fusion.47), channel_id=1, source_target_pairs={{0,8},{4,12},{8,16},{12,20},{16,24},{20,28},{1,9},{5,13},{9,17},{1... | collective-permute-start | bytes 24584 | tf_op jit(solution)/shard_map/ppermute | solution.py:19
  76.1 0.0 copy-done.3
  76.1 0.1 mul.193
  76.2 1.3 %collective-permute-done.5 = f32[1,2048]{1,0:T(1,128)S(1)} collective-permute-done((f32[1,2048]{1,0:T(1,128)S(1)}, f32[1,2048]{1,0:T(1,128)S(1)}, u32[]{:S(2)}, u32[]{:S(2)}) %collective-permute-start.5) | collective-permute-done | bytes 8224 | tf_op jit(solution)/shard_map/ppermute | solution.py:19
  77.5 4.8 %collective-permute-done.6 = bf16[128,2048]{1,0:T(8,128)(2,1)} collective-permute-done((bf16[128,2048]{1,0:T(8,128)(2,1)}, bf16[128,2048]{1,0:T(8,128)(2,1)}, u32[]{:S(2)}, u32[]{:S(2)}) %collective-permute-start.6) | collective-permute-done | bytes 524320 | tf_op jit(solution)/shard_map/ppermute | solution.py:19
  82.2 0.0 copy-start.10
  82.2 3.9 %fusion.32 = f32[512,2048]{0,1:T(8,128)} fusion(bf16[128,2048]{1,0:T(8,128)(2,1)} %collective-permute-done.6, bf16[128,2048]{1,0:T(8,128)(2,1)} %copy-done.2, bf16[128,2048]{1,0:T(8,128)(2,1)S(1)} %collective-permute-done.2, bf16[128,2048]{1,0:T(8,128)(2,1)S(1)} %collective-permute-done, f32[2048]{0:T(1024)S(1)} %bitcast.50, f32[2048]{0:T(1024)S(1)} %bitcast.49, ...), kind=kOutput, calls=%fused_computation.52 | convolution fusion | flops 271319040 | bytes 6447104 | tf_op jit(solution)/shard_map/dot_general | solution.py:11
  86.2 0.0 copy-done.10
  86.2 7.2 %multiply_reduce_fusion = (f32[512,32]{0,1:T(8,128)S(1)}, f32[512,32,64]{0,2,1:T(8,128)}) fusion(bf16[512,32,128]{0,2,1:T(8,128)(2,1)} %bitcast.42, f32[32]{0:T(128)S(1)} %copy-done.10, f32[512,32]{0,1:T(8,128)S(1)} %get-tuple-element.16, f32[512,32,64]{0,2,1:T(8,128)} %bitcast.40, bf16[512,32,64]{0,2,1:T(8,128)(2,1)} %copy-done.1, ...), kind=kOutput, calls=%fused_computation.12 | convolution fusion | flops 1155252224 | bytes 15073408 | tf_op jit(solution)/shard_map/dot_general | solution.py:11
  93.4 0.0 copy-start.4
  93.4 0.0 copy-start.12
  93.4 2.8 %multiply_convert_fusion = bf16[512,32,64]{0,2,1:T(8,128)(2,1)S(1)} fusion(f32[512,32,64]{0,2,1:T(8,128)} %get-tuple-element.21, f32[32,64]{1,0:T(8,128)S(1)} %mul.193, f32[512,32]{0,1:T(8,128)S(1)} %add_rsqrt_fusion), kind=kLoop, calls=%fused_computation.11 | loop fusion | flops 3145728 | bytes 6365184 | tf_op jit(solution)/shard_map/convert_element_type | solution.py:64
  96.2 0.6 copy-done.4
  96.8 0.3 copy-done.12
  97.1 3.3 %fusion.20 = bf16[512,1,1024]{2,0,1:T(8,128)(2,1)} fusion(bf16[512,2048]{0,1:T(8,128)(2,1)S(1)} %bitcast.44, bf16[2048,1024]{1,0:T(8,128)(2,1)S(1)} %copy-done.4, bf16[512,1024]{1,0:T(8,128)(2,1)S(1)} %copy-done.12), kind=kOutput, calls=%fused_computation.33 | convolution fusion | flops 2149056512 | bytes 8388608 | tf_op jit(solution)/shard_map/dot_general | solution.py:11
  (6 shorter events, 0.1 us)
Async XLA Ops:
  0.0 1.6 %copy-start = (bf16[1024,1024]{1,0:T(8,128)(2,1)S(1)}, bf16[1024,1024]{1,0:T(8,128)(2,1)}, u32[]{:S(2)}) copy-start(bf16[1024,1024]{1,0:T(8,128)(2,1)} %param.19) | copy-start | bytes 6291460
  1.6 4.0 %copy-start.7 = (f32[1024]{0:T(1024)S(1)}, f32[1024]{0:T(1024)}, u32[]{:S(2)}) copy-start(f32[1024]{0:T(1024)} %param.21) | copy-start | bytes 12292
  4.6 1.0 copy-start.11
  15.2 6.5 %copy-start.8 = (s32[32]{0:T(128)S(1)}, s32[32]{0:T(128)}, u32[]{:S(2)}) copy-start(s32[32]{0:T(128)} %param.26) | copy-start | bytes 388
  15.2 6.5 %copy-start.6 = (bf16[1024,32]{0,1:T(8,128)(2,1)S(1)}, bf16[1024,32]{0,1:T(8,128)(2,1)}, u32[]{:S(2)}) copy-start(bf16[1024,32]{0,1:T(8,128)(2,1)} %param.24) | copy-start | bytes 196612
  15.2 6.6 %copy-start.9 = (f32[32]{0:T(128)S(1)}, f32[32]{0:T(128)}, u32[]{:S(2)}) copy-start(f32[32]{0:T(128)} %param.25) | copy-start | bytes 388
  21.7 2.4 %copy-start.5 = (bf16[1024,256]{1,0:T(8,128)(2,1)S(1)}, bf16[1024,256]{1,0:T(8,128)(2,1)}, u32[]{:S(2)}) copy-start(bf16[1024,256]{1,0:T(8,128)(2,1)} %param.23) | copy-start | bytes 1572868
  27.9 1.3 %copy-start.1 = (bf16[512,32,64]{0,2,1:T(8,128)(2,1)}, bf16[512,32,64]{0,2,1:T(8,128)(2,1)S(1)}, u32[]{:S(2)}) copy-start(bf16[512,32,64]{0,2,1:T(8,128)(2,1)S(1)} %fusion) | copy-start | bytes 6291460
  30.1 46.0 %copy-start.3 = (f32[2048]{0:T(1024)S(1)}, f32[2048]{0:T(1024)}, u32[]{:S(2)}) copy-start(f32[2048]{0:T(1024)} %param.28) | copy-start | bytes 24580
  30.1 3.9 %collective-permute-start = (bf16[128,2048]{1,0:T(8,128)(2,1)S(1)}, bf16[128,2048]{1,0:T(8,128)(2,1)S(1)}, u32[]{:S(2)}, u32[]{:S(2)}) collective-permute-start(bf16[128,2048]{1,0:T(8,128)(2,1)S(1)} %fusion.6), channel_id=1, source_target_pairs={{0,4},{4,8},{8,12},{12,16},{16,20},{20,24},{24,28},{1,5},{5,9},{9,... | collective-permute-start | bytes 1572872 | tf_op jit(solution)/shard_map/ppermute | solution.py:19
  34.0 14.4 %collective-permute-start.2 = (bf16[128,2048]{1,0:T(8,128)(2,1)S(1)}, bf16[128,2048]{1,0:T(8,128)(2,1)S(1)}, u32[]{:S(2)}, u32[]{:S(2)}) collective-permute-start(bf16[128,2048]{1,0:T(8,128)(2,1)S(1)} %collective-permute-done), channel_id=1, source_target_pairs={{0,4},{4,8},{8,12},{12,16},{16,20},{20,24},{24,28},{1,5},{5,9},{9,... | collective-permute-start | bytes 1572872 | tf_op jit(solution)/shard_map/ppermute | solution.py:19
  43.2 5.2 %collective-permute-start.1 = (f32[1,2048]{1,0:T(1,128)S(1)}, f32[1,2048]{1,0:T(1,128)S(1)}, u32[]{:S(2)}, u32[]{:S(2)}) collective-permute-start(f32[1,2048]{1,0:T(1,128)S(1)} %broadcast_in_dim_reshape.2), channel_id=1, source_target_pairs={{0,4},{4,8},{8,12},{12,16},{16,20},{20,24},{24,28},{1,5},{5,9},{9,... | collective-permute-start | bytes 24584 | tf_op jit(solution)/shard_map/ppermute | solution.py:19
  48.5 19.1 %collective-permute-start.4 = (bf16[128,2048]{1,0:T(8,128)(2,1)S(1)}, bf16[128,2048]{1,0:T(8,128)(2,1)S(1)}, u32[]{:S(2)}, u32[]{:S(2)}) collective-permute-start(bf16[128,2048]{1,0:T(8,128)(2,1)S(1)} %fusion.30), channel_id=1, source_target_pairs={{0,8},{4,12},{8,16},{12,20},{16,24},{20,28},{1,9},{5,13},{9,17},{1... | collective-permute-start | bytes 1572872 | tf_op jit(solution)/shard_map/ppermute | solution.py:19
  56.2 2.5 %collective-permute-start.3 = (f32[1,2048]{1,0:T(1,128)S(1)}, f32[1,2048]{1,0:T(1,128)S(1)}, u32[]{:S(2)}, u32[]{:S(2)}) collective-permute-start(f32[1,2048]{1,0:T(1,128)S(1)} %broadcast_select_fusion.2), channel_id=1, source_target_pairs={{0,4},{4,8},{8,12},{12,16},{16,20},{20,24},{24,28},{1,5},{5,9},{9,... | collective-permute-start | bytes 24584 | tf_op jit(solution)/shard_map/ppermute | solution.py:19
  67.7 0.8 copy-start.2
  69.6 12.7 %collective-permute-start.6 = (bf16[128,2048]{1,0:T(8,128)(2,1)}, bf16[128,2048]{1,0:T(8,128)(2,1)}, u32[]{:S(2)}, u32[]{:S(2)}) collective-permute-start(bf16[128,2048]{1,0:T(8,128)(2,1)} %fusion.31), channel_id=1, source_target_pairs={{0,16},{4,20},{8,24},{12,28},{1,17},{5,21},{9,25},{13,29},{2,18},{... | collective-permute-start | bytes 1572872 | tf_op jit(solution)/shard_map/ppermute | solution.py:19
  74.8 2.6 %collective-permute-start.5 = (f32[1,2048]{1,0:T(1,128)S(1)}, f32[1,2048]{1,0:T(1,128)S(1)}, u32[]{:S(2)}, u32[]{:S(2)}) collective-permute-start(f32[1,2048]{1,0:T(1,128)S(1)} %fusion.47), channel_id=1, source_target_pairs={{0,8},{4,12},{8,16},{12,20},{16,24},{20,28},{1,9},{5,13},{9,17},{1... | collective-permute-start | bytes 24584 | tf_op jit(solution)/shard_map/ppermute | solution.py:19
  82.2 3.9 %copy-start.10 = (f32[32]{0:T(128)S(1)}, f32[32]{0:T(128)}, u32[]{:S(2)}) copy-start(f32[32]{0:T(128)} %param.27) | copy-start | bytes 388
  93.4 3.5 %copy-start.4 = (bf16[2048,1024]{1,0:T(8,128)(2,1)S(1)}, bf16[2048,1024]{1,0:T(8,128)(2,1)}, u32[]{:S(2)}) copy-start(bf16[2048,1024]{1,0:T(8,128)(2,1)} %param.29) | copy-start | bytes 12582916
  93.4 3.7 %copy-start.12 = (bf16[512,1024]{1,0:T(8,128)(2,1)S(1)}, bf16[512,1024]{1,0:T(8,128)(2,1)}, u32[]{:S(2)}) copy-start(bf16[512,1024]{1,0:T(8,128)(2,1)} %copy-done.11) | copy-start | bytes 3145732

commit v2 on v1

v2 whole, which is shorter than its diff:
```python
import functools

import jax
import jax.numpy as jnp
from jax import lax
from jax.experimental import pallas as pl
from jax.experimental.pallas import tpu as pltpu
from jax.sharding import PartitionSpec as P

BF = jnp.bfloat16
F32 = jnp.float32
VM = pl.BlockSpec(memory_space=pltpu.VMEM)
SM = pl.BlockSpec(memory_space=pltpu.SMEM)
ANY = pl.BlockSpec(memory_space=pl.ANY)
LANES = 128
CHUNK = 256
EXTRA = 16


def dot(a, b):
    return jnp.dot(a, b, preferred_element_type=F32)


def dot_t(a, b):
    return lax.dot_general(a, b, (((1,), (1,)), ((), ())), preferred_element_type=F32)


def iota(shape, axis):
    return lax.broadcasted_iota(jnp.int32, shape, axis)


def params(mib):
    return pltpu.CompilerParams(vmem_limit_bytes=mib * 2**20)


def sds(shape, dtype):
    return jax.ShapeDtypeStruct(shape, dtype)


def spread_heads(first_head, heads, head_dim):
    row = iota((2 * heads, CHUNK), 0)
    lane = iota((2 * heads, CHUNK), 1)
    row = jnp.where(row < heads, row, row - heads)
    return (row == first_head + lane // head_dim).astype(F32).astype(BF)


def split_two(value, heads):
    high = value.astype(BF).astype(F32)
    return jnp.where(iota(value.shape, 1) < heads, high, value - high).astype(BF)


def pick_half(tile_a, tile_b, part):
    half = LANES // 2
    low = iota(tile_a.shape, 1) < half
    if part == 0:
        return jnp.where(low, tile_a, pltpu.roll(tile_b, half, 1))
    return jnp.where(low, pltpu.roll(tile_a, half, 1), tile_b)


def compact(ref, part):
    tiles = [ref[:, i * LANES:(i + 1) * LANES] for i in range(2 * CHUNK // LANES)]
    pairs = [pick_half(tiles[i], tiles[i + 1], part) for i in range(0, len(tiles), 2)]
    return jnp.concatenate(pairs, axis=1)


def weight_copies(w_ref, buf, sem, half, count):
    copies = []
    for j in range(count):
        start = pl.multiple_of((half * count + j) * 2 * CHUNK, 2 * CHUNK)
        copies.append(pltpu.make_async_copy(w_ref.at[:, pl.ds(start, 2 * CHUNK)], buf.at[j], sem.at[j]))
    return copies


def project(j, half, heads, head_dim, count, buf, normed, b_t, grow, fall_end, x_ref, xs_ref, s_ref):
    width = b_t.shape[0]
    per = CHUNK // head_dim
    first = (half * count + j) * per
    cols = slice(j * CHUNK, (j + 1) * CHUNK)
    spread = spread_heads(first, heads, head_dim)
    x = dot(normed[...], compact(buf.at[j], 0)).astype(BF)
    scaled = (x.astype(F32) * dot(grow, spread)).astype(BF)
    x_ref[:, cols] = x
    xs_ref[:, cols] = scaled
    decay = dot(fall_end, spread)[EXTRA - 1:EXTRA]
    s_ref[0:width, cols] = (dot(b_t, scaled) * decay).astype(BF)
    high = decay.astype(BF).astype(F32)
    row = iota((EXTRA, CHUNK), 0)
    s_ref[width:width + EXTRA, cols] = jnp.where(row == 0, high, jnp.where(row == 1, decay - high, 0.0)).astype(BF)


def encode_kernel(heads, head_dim, half_ref, cell_ref, frames, enc_in, enc_bias, norm_gain, w_keys, w_step, step_bias,
                  rate, enc_out_any, pos_any, w_pair_any, encoded, normed, keys, b_t, grow, fall, x_ref, xs_ref, s_ref,
                  enc_out, pos, buf, sem, wsem):
    half = 1 - half_ref[0]
    count = buf.shape[0]
    cell = cell_ref[0]
    base = pl.multiple_of((cell // EXTRA) * EXTRA, EXTRA)
    out_copy = pltpu.make_async_copy(enc_out_any, enc_out, sem.at[0])
    pos_copy = pltpu.make_async_copy(pos_any.at[pl.ds(base, EXTRA), :], pos, sem.at[1])
    out_copy.start()
    pos_copy.start()
    copies = weight_copies(w_pair_any, buf, wsem, half, count)
    for c in copies:
        c.start()
    rows, depth = encoded.shape
    hidden = []
    for j in range(depth // CHUNK):
        cols = slice(j * CHUNK, (j + 1) * CHUNK)
        h = dot(frames[...], enc_in[:, cols]) + enc_bias[:, cols]
        hidden.append(jax.nn.gelu(h, approximate=True).astype(BF))
    hidden = jnp.concatenate(hidden, axis=1)
    out_copy.wait()
    pos_copy.wait()
    row = jnp.sum(jnp.where(iota(pos.shape, 0) == cell - base, pos[...].astype(F32), 0.0), axis=0, keepdims=True)
    square = jnp.zeros((rows, 1), F32)
    for j in range(depth // CHUNK):
        cols = slice(j * CHUNK, (j + 1) * CHUNK)
        e = (dot(hidden, enc_out[:, cols]) + row[:, cols]).astype(BF)
        encoded[:, cols] = e
        e = e.astype(F32)
        square += jnp.sum(e * e, axis=1, keepdims=True)
    inv = lax.rsqrt(square / depth + 1e-05)
    for j in range(depth // CHUNK):
        cols = slice(j * CHUNK, (j + 1) * CHUNK)
        normed[:, cols] = (encoded[:, cols].astype(F32) * inv * norm_gain[:, cols]).astype(BF)
    k = dot(normed[...], w_keys[...]).astype(BF)
    keys[...] = k
    b_t[...] = k[:, :k.shape[1] // 2].T
    ws = w_step[...]
    twice = lambda v: jnp.concatenate([v, v], axis=1)
    raw = dot_t(normed[...], jnp.concatenate([ws, ws], axis=0)) + twice(step_bias[...])
    step = jax.nn.sigmoid(raw).astype(BF)
    lower = (iota((rows, rows), 0) >= iota((rows, rows), 1)).astype(F32).astype(BF)
    cum = dot(lower, step) * twice(rate[...])
    g = split_two(jnp.exp(-cum), heads)
    f = split_two(jnp.exp(cum), heads)
    grow[...] = g
    fall[...] = f
    for j in range(count):
        copies[j].wait()
        project(j, half, heads, head_dim, count, buf, normed, b_t[...], g, f[rows - EXTRA:], x_ref, xs_ref, s_ref)


def second_kernel(heads, head_dim, half_ref, normed, b_t, grow, fall, w_pair_any, x_ref, xs_ref, s_ref, buf, wsem):
    half = half_ref[0]
    count = buf.shape[0]
    copies = weight_copies(w_pair_any, buf, wsem, half, count)
    for c in copies:
        c.start()
    rows = normed.shape[0]
    for j in range(count):
        copies[j].wait()
        project(j, half, heads, head_dim, count, buf, normed, b_t[...], grow[...], fall[rows - EXTRA:], x_ref, xs_ref, s_ref)


def gate_kernel(half_ref, normed, w_pair_any, mine, other, buf, wsem):
    count = buf.shape[0] // 2
    lists = []
    for k, half in enumerate((half_ref[0], 1 - half_ref[0])):
        lists += weight_copies(w_pair_any, buf.at[pl.ds(k * count, count)], wsem.at[pl.ds(k * count, count)], half, count)
    for c in lists:
        c.start()
    for k, out in enumerate((mine, other)):
        for j in range(count):
            lists[k * count + j].wait()
            z = dot(normed[...], compact(buf.at[k * count + j], 1)).astype(BF).astype(F32)
            out[:, j * CHUNK:(j + 1) * CHUNK] = (z * jax.nn.sigmoid(z)).astype(BF)


def inner_kernel(heads, head_dim, half_ref, keys, fall, skip, x_m, x_o, xs_m, xs_o, sg_m, sg_o, u_m, u_o, v_m, v_o):
    rows = keys.shape[0]
    width = keys.shape[1] // 2
    per = CHUNK // head_dim
    count = x_m.shape[1] // CHUNK
    scores = dot_t(keys[:, width:], keys[:, :width])
    scores = jnp.where(iota((rows, rows), 0) >= iota((rows, rows), 1), scores, 0.0).astype(BF)
    value = jnp.broadcast_to(jnp.concatenate([skip[...], skip[...]], axis=1), (EXTRA, 2 * heads))
    skip_two = split_two(value, heads)
    mid = rows // 2
    groups = ((half_ref[0], x_m, xs_m, sg_m, u_m, v_m), (1 - half_ref[0], x_o, xs_o, sg_o, u_o, v_o))
    for half, x, xs, sg, u, v in groups:
        for j in range(count):
            cols = slice(j * CHUNK, (j + 1) * CHUNK)
            spread = spread_heads((half * count + j) * per, heads, head_dim)
            gain = dot(skip_two, spread)[0:1]
            top = dot(scores[:mid, :mid], xs[:mid, cols])
            low = dot(scores[mid:], xs[:, cols])
            for part, inner in ((slice(0, mid), top), (slice(mid, rows), low)):
                grown = dot(fall[part, :], spread)
                gate = sg[part, cols].astype(F32)
                u[part, cols] = (grown * gate).astype(BF)
                v[part, cols] = ((grown * inner + gain * x[part, cols].astype(F32)) * gate).astype(BF)


def mix(half, head_dim, keys, state, u, v, gain_ref, w_ref, w_copies, acc):
    width = keys.shape[1] // 2
    flat = u.shape[1]
    count = flat // CHUNK
    same = (iota((CHUNK, CHUNK), 0) // head_dim) == (iota((CHUNK, CHUNK), 1) // head_dim)
    mean = jnp.where(same, 1.0 / head_dim, 0.0).astype(BF)
    parts = []
    for j in range(count):
        cols = slice(j * CHUNK, (j + 1) * CHUNK)
        carried = dot(keys[:, width:], state[:, cols])
        g = v[:, cols].astype(F32) + u[:, cols].astype(F32) * carried
        m = dot((g * g).astype(BF), mean)
        gain = gain_ref[:, pl.ds(pl.multiple_of(half * flat + j * CHUNK, CHUNK), CHUNK)]
        parts.append((g * lax.rsqrt(m + 1e-05) * gain).astype(BF))
    mixed = jnp.concatenate(parts, axis=1)
    for c in w_copies:
        c.wait()
    return [acc(n) + dot(mixed, w_ref[:, n * CHUNK:(n + 1) * CHUNK]) for n in range(w_ref.shape[1] // CHUNK)]


def mix_kernel(head_dim, last, half_ref, keys, state, u, v, gain, base, w_any, out, w_ref, wsem):
    half = half_ref[0]
    if last:
        half = 1 - half
    flat = u.shape[1]
    start = pl.multiple_of(half * flat, flat)
    copy = pltpu.make_async_copy(w_any.at[pl.ds(start, flat), :], w_ref, wsem)
    copy.start()
    pieces = mix(half, head_dim, keys, state, u, v, gain, w_ref, [copy],
                 lambda n: base[:, n * CHUNK:(n + 1) * CHUNK].astype(F32))
    for n, piece in enumerate(pieces):
        out[:, n * CHUNK:(n + 1) * CHUNK] = piece.astype(out.dtype)


def body(frames, patch_cell, enc_in, enc_bias, enc_out, pos_table, norm_gain, w_pair, w_keys, w_step,
         step_bias, decay_code, skip_gain, out_gain, w_out):
    rows = frames.shape[0]
    pix = frames.shape[2]
    depth = enc_out.shape[1]
    heads = w_step.shape[1]
    head_dim = w_pair.shape[1] // (2 * heads)
    width = w_keys.shape[1] // 2
    flat = heads * head_dim // 2
    count = flat // CHUNK
    peers = lax.axis_size("tm")
    here = lax.axis_index("tm")
    odd = here % 2 == 1
    half = (here % 2).astype(jnp.int32).reshape(1)
    rate = (-0.0005 - 0.003 * decay_code.astype(F32)).reshape(1, heads)
    row = lambda v: v.reshape(1, -1)
    cost = lambda macs: pl.CostEstimate(flops=2 * macs, bytes_accessed=4 * 2**20, transcendentals=0)

    halves = sds((rows, flat), BF)
    message = sds((width + EXTRA, flat), BF)
    encoded, normed, keys, b_t, grow, fall, x_o, xs_o, s_o = pl.pallas_call(
        functools.partial(encode_kernel, heads, head_dim),
        out_shape=(sds((rows, depth), BF), sds((rows, depth), BF), sds((rows, 2 * width), BF), sds((width, rows), BF),
                   sds((rows, 2 * heads), BF), sds((rows, 2 * heads), BF), halves, halves, message),
        in_specs=[SM, SM] + [VM] * 8 + [ANY] * 3,
        out_specs=(VM,) * 9,
        scratch_shapes=[pltpu.VMEM((depth, depth), BF), pltpu.VMEM((EXTRA, depth), BF),
                        pltpu.VMEM((count, depth, 2 * CHUNK), BF),
                        pltpu.SemaphoreType.DMA((2,)), pltpu.SemaphoreType.DMA((count,))],
        compiler_params=params(40), name="encode",
    )(half, patch_cell, frames.reshape(rows, pix), enc_in, row(enc_bias), row(norm_gain), w_keys, w_step.T,
      row(step_bias), rate, enc_out, pos_table, w_pair)
    pair = lambda by: [(i, i ^ by) for i in range(peers)]
    got = lax.ppermute(s_o, "tm", pair(1))
    x_m, xs_m, s_m = pl.pallas_call(
        functools.partial(second_kernel, heads, head_dim),
        out_shape=(halves, halves, message),
        in_specs=[SM] + [VM] * 4 + [ANY],
        out_specs=(VM,) * 3,
        scratch_shapes=[pltpu.VMEM((count, depth, 2 * CHUNK), BF), pltpu.SemaphoreType.DMA((count,))],
        compiler_params=params(40), name="project", cost_estimate=cost(rows * depth * flat),
    )(half, normed, b_t, grow, fall, w_pair)

    def opened(packed):
        return packed[:width].astype(F32), packed[width].astype(F32)[None] + packed[width + 1].astype(F32)[None]

    def closed(state, decay):
        high = decay.astype(BF)
        low = (decay - high.astype(F32)).astype(BF)
        return jnp.concatenate([state.astype(BF), high, low, jnp.zeros((EXTRA - 2, flat), BF)], axis=0)

    mine, mine_decay = opened(s_m)
    theirs, theirs_decay = opened(got)
    even_state, even_decay = jnp.where(odd, theirs, mine), jnp.where(odd, theirs_decay, mine_decay)
    total = jnp.where(odd, mine_decay, theirs_decay) * even_state + jnp.where(odd, mine, theirs)
    total_decay = mine_decay * theirs_decay
    before, before_decay = jnp.zeros_like(total), jnp.ones_like(total_decay)

    sg_m, sg_o = pl.pallas_call(
        gate_kernel,
        out_shape=(halves, halves),
        in_specs=[SM, VM, ANY],
        out_specs=(VM,) * 2,
        scratch_shapes=[pltpu.VMEM((2 * count, depth, 2 * CHUNK), BF), pltpu.SemaphoreType.DMA((2 * count,))],
        compiler_params=params(40), name="gate", cost_estimate=cost(2 * rows * depth * flat),
    )(half, normed, w_pair)
    u_m, u_o, v_m, v_o = pl.pallas_call(
        functools.partial(inner_kernel, heads, head_dim),
        out_shape=(halves,) * 4,
        in_specs=[SM] + [VM] * 9,
        out_specs=(VM,) * 4,
        compiler_params=params(40), name="inner", cost_estimate=cost(rows * depth * flat),
    )(half, keys, fall, row(skip_gain), x_m, x_o, xs_m, xs_o, sg_m, sg_o)

    reach = 2
    while reach < peers:
        arrived, arrived_decay = opened(lax.ppermute(closed(total, total_decay), "tm", pair(reach)))
        later = (here // reach) % 2 == 1
        before = before + jnp.where(later, before_decay, 0.0) * arrived
        before_decay = before_decay * jnp.where(later, arrived_decay, 1.0)
        total = jnp.where(later, total_decay, arrived_decay) * jnp.where(later, arrived, total) + jnp.where(later, total, arrived)
        total_decay = total_decay * arrived_decay
        reach *= 2

    at_even, at_odd = before.astype(BF), (even_decay * before + even_state).astype(BF)
    state_m = jnp.where(odd, at_odd, at_even)
    state_o = lax.ppermute(jnp.where(odd, at_even, at_odd), "tm", pair(1))

    def mixed(last, state, u, v, base, kind):
        return pl.pallas_call(
            functools.partial(mix_kernel, head_dim, last),
            out_shape=sds((rows, depth), kind),
            in_specs=[SM] + [VM] * 6 + [ANY],
            out_specs=VM,
            scratch_shapes=[pltpu.VMEM((flat, depth), BF), pltpu.SemaphoreType.DMA],
            compiler_params=params(40), name="mix", cost_estimate=cost(rows * depth * flat),
        )(half, keys, state, u, v, row(out_gain), base, w_out)

    partial = mixed(False, state_m, u_m, v_m, encoded, F32)
    return mixed(True, state_o, u_o, v_o, partial, BF).reshape(rows, 1, depth)


def solution(mesh):
    placed = (P("tm", "space", None), P("space")) + (P(),) * 13
    return jax.shard_map(body, mesh=mesh, in_specs=placed, out_specs=P("tm", "space", None), check_vma=False)
```

time: 101 us -> 77.9 us (0.77)
  matrix products: 31.6 us -> 0 us
  starting transfers between devices: 31.7 us -> 4.78 us
  Pallas kernels: 0 us -> 26.9 us
  local copies, waits for them, and re-layouts: 11.1 us -> 22.8 us
  waiting for transfers between devices: 18.1 us -> 15 us
    dot_general x8 -> x0, matrix products: 31.6 us -> none  [dot(): return jnp.dot(a, b, preferred_element_type=F32)]
    ppermute x7 -> x4, starting transfers between devices: 31.7 us -> 4.78 us  [the longest x2 4.33 us: body(): lax.ppermute(closed(total, total_decay), 'tm', pair(reach))]
    pallas_call x0 -> x6, Pallas kernels: none -> 26.9 us  [the longest x1 7.56 us: body(): pl.pallas_call(gate_kernel, out_shape=(halves, halves), in_specs=[SM, VM,...]
    unnamed x26 -> x48, local copies, waits for them, and re-layouts: 4.07 us -> 22.7 us
    reshape x1 -> x0, local copies, waits for them, and re-layouts: 6.53 us -> none  [body(): pair = dot(normed, w_pair).astype(BF).reshape(count, heads, 2 * head_dim)]
    convert_element_type x5, other arithmetic: 6.92 us -> 3.06 us  [the longest x2 2.23 us: closed(): state.astype(BF)]
    ppermute x7 -> x4, waiting for transfers between devices: 18.1 us -> 15 us  [the longest x2 15 us: body(): lax.ppermute(closed(total, total_decay), 'tm', pair(reach))]
    select_n x1 -> x3, other arithmetic: 0.01 us -> 2.03 us  [the longest x1 1.17 us: body(): state_m = jnp.where(odd, at_odd, at_even)]
  transfers between devices with their start and end apart: 7 -> 4, of which waited for: 6 -> 2; matrix products, arithmetic and copies ran while one was open for 0% -> 0% of each run, Pallas kernels for 0% -> 21%
where the time goes in v2:
time: 77.9 us; the launch traced here: 77.1 us
  Pallas kernels  26.9 us (35%)
  local copies, waits for them, and re-layouts  22.8 us (29%)
  waiting for transfers between devices  15 us (19%)
  other arithmetic  6.69 us (9%)
  starting transfers between devices  4.78 us (6%)
  between operations  1.01 us (1%)
    unnamed x48, local copies, waits for them, and re-layouts  22.7 us
    ppermute x2, waiting for transfers between devices, body(): lax.ppermute(closed(total, total_decay), 'tm', pair(reach))  15 us
    pallas_call x1, Pallas kernels, body(): pl.pallas_call(gate_kernel, out_shape=(halves, halves), in_specs=[SM, VM,...  7.56 us
    pallas_call x1, Pallas kernels, body(): pl.pallas_call(functools.partial(encode_kernel, heads, head_dim), out_sha...  7.28 us
    pallas_call x2, Pallas kernels, mixed(): pl.pallas_call(functools.partial(mix_kernel, head_dim, last), out_shape=s...  5.75 us
    ppermute x2, starting transfers between devices, body(): lax.ppermute(closed(total, total_decay), 'tm', pair(reach))  4.33 us
    pallas_call x1, Pallas kernels, body(): pl.pallas_call(functools.partial(second_kernel, heads, head_dim), out_sha...  4.28 us
    convert_element_type x2, other arithmetic, closed(): state.astype(BF)  2.23 us
  transfers between devices with their start and end apart: 4, of which 2 were waited for; matrix products, arithmetic and copies ran while one was open for 0% of the time, Pallas kernels for 21%

profile of v2, /device:TPU:0, one launch (start us, length us, event | category | flops | bytes accessed | tf_op | source)
XLA Modules:
  0.0 77.1 jit_solution(11572764733925373027)
XLA Ops:
  0.7 0.7 subtract_bitcast_fusion.rate
  1.3 0.0 copy-start.3
  1.3 2.2 %copy-done.3 = bf16[2048,1024]{1,0:T(8,128)(2,1)S(1)} copy-done((bf16[2048,1024]{1,0:T(8,128)(2,1)S(1)}, bf16[2048,1024]{1,0:T(8,128)(2,1)}, u32[]{:S(2)}) %copy-start.3) | copy-done | bytes 4194328
  3.5 1.6 %copy-done.4 = bf16[1024,1024]{1,0:T(8,128)(2,1)S(1)} copy-done((bf16[1024,1024]{1,0:T(8,128)(2,1)S(1)}, bf16[1024,1024]{1,0:T(8,128)(2,1)}, u32[]{:S(2)}) %copy-start.4) | copy-done | bytes 2097176
  5.1 0.0 copy-start.15
  5.1 1.0 %copy-done.15 = bf16[256,1024]{1,0:T(8,128)(2,1)S(1)} copy-done((bf16[256,1024]{1,0:T(8,128)(2,1)S(1)}, bf16[256,1024]{1,0:T(8,128)(2,1)}, u32[]{:S(2)}) %copy-start.15) | copy-done | bytes 524312
  6.1 0.0 copy-start.16
  6.1 1.0 %copy-done.16 = bf16[1024,256]{1,0:T(8,128)(2,1)S(1)} copy-done((bf16[1024,256]{1,0:T(8,128)(2,1)S(1)}, bf16[1024,256]{1,0:T(8,128)(2,1)}, u32[]{:S(2)}) %copy-start.16) | copy-done | bytes 524312
  7.2 0.0 copy-start.17
  7.2 0.9 %copy-done.17 = bf16[512,1,256]{2,0,1:T(8,128)(2,1)S(1)} copy-done((bf16[512,1,256]{2,0,1:T(8,128)(2,1)S(1)}, bf16[512,1,256]{2,0,1:T(8,128)(2,1)}, u32[]{:S(2)}) %copy-start.17) | copy-done | bytes 262168
  8.1 0.0 copy-start.18
  8.1 0.8 %copy-done.18 = bf16[1024,32]{0,1:T(8,128)(2,1)S(1)} copy-done((bf16[1024,32]{0,1:T(8,128)(2,1)S(1)}, bf16[1024,32]{0,1:T(8,128)(2,1)}, u32[]{:S(2)}) %copy-start.18) | copy-done | bytes 65560
  9.0 0.0 copy-start.20
  9.0 0.7 copy-done.20
  9.7 0.0 copy-start.21
  9.7 0.7 copy-done.21
  10.3 0.0 copy-start.22
  10.3 0.7 copy-done.22
  11.0 7.3 %encode.1 = (bf16[512,1024]{1,0:T(8,128)(2,1)S(1)}, bf16[512,1024]{1,0:T(8,128)(2,1)S(1)}, bf16[512,256]{1,0:T(8,128)(2,1)S(1)}, bf16[128,512]{1,0:T(8,128)(2,1)...) custom-call(s32[1]{0:T(128)} %bitcast.half_ref, ...), custom_call_target="tpu_custom_call" | custom-call | tf_op jit(solution)/shard_map/encode/pallas_call | solution.py:249
  18.3 0.0 copy-start.5
  18.3 1.0 %copy-done.5 = bf16[512,1024]{1,0:T(8,128)(2,1)} copy-done((bf16[512,1024]{1,0:T(8,128)(2,1)}, bf16[512,1024]{1,0:T(8,128)(2,1)S(1)}, u32[]{:S(2)}) %copy-start.5) | copy-done | bytes 1048600
  19.3 0.0 copy-start.7
  19.3 1.0 %copy-done.7 = bf16[512,1024]{1,0:T(8,128)(2,1)} copy-done((bf16[512,1024]{1,0:T(8,128)(2,1)}, bf16[512,1024]{1,0:T(8,128)(2,1)S(1)}, u32[]{:S(2)}) %copy-start.7) | copy-done | bytes 1048600
  20.2 0.5 collective-permute-start
  20.7 0.1 pad.7.clone
  20.8 0.0 copy-start
  20.8 3.4 %copy-done = bf16[1024,4096]{1,0:T(8,128)(2,1)S(1)} copy-done((bf16[1024,4096]{1,0:T(8,128)(2,1)S(1)}, bf16[1024,4096]{1,0:T(8,128)(2,1)}, u32[]{:S(2)}) %copy-start) | copy-done | bytes 8388632
  24.2 4.3 %project.1 = (bf16[512,1024]{1,0:T(8,128)(2,1)S(1)}, bf16[512,1024]{1,0:T(8,128)(2,1)S(1)}, bf16[144,1024]{1,0:T(8,128)(2,1)S(1)}) custom-call(s32[1]{0:T(128)} %bitcast.half_ref, bf16[512,1024]{1,0:T(8,128)(2,1)S(1)} %get-tuple-element.24.normed, bf16[128,512]{1,0:T(8,128)(2,1)S(1)} %get-tuple-element.25.b_t, bf16[512,64]{1,0:T(8,128)(2,1)S(1)} %get-tuple-element.26.grow, ...), custom_call_target="tpu_custom_call" | custom-call | flops 1073741824 | bytes 4194304 | tf_op jit(solution)/shard_map/project/pallas_call | solution.py:263
  28.4 0.0 copy-start.9
  28.5 1.0 %copy-done.9 = bf16[512,1024]{1,0:T(8,128)(2,1)} copy-done((bf16[512,1024]{1,0:T(8,128)(2,1)}, bf16[512,1024]{1,0:T(8,128)(2,1)S(1)}, u32[]{:S(2)}) %copy-start.9) | copy-done | bytes 1048600
  29.4 0.0 copy-start.11
  29.4 1.0 %copy-done.11 = bf16[512,1024]{1,0:T(8,128)(2,1)} copy-done((bf16[512,1024]{1,0:T(8,128)(2,1)}, bf16[512,1024]{1,0:T(8,128)(2,1)S(1)}, u32[]{:S(2)}) %copy-start.11) | copy-done | bytes 1048600
  30.4 0.0 collective-permute-done
  30.4 0.8 %fusion.11 = (bf16[1,1024]{1,0:T(2,128)(2,1)S(1)}, f32[1,1024]{1,0:T(1,128)S(1)}, f32[1,1024]{1,0:T(1,128)S(1)}, f32[1,1024]{1,0:T(1,128)S(1)}) fusion(bf16[144,1024]{1,0:T(8,128)(2,1)} %collective-permute-done, bf16[144,1024]{1,0:T(8,128)(2,1)S(1)} %get-tuple-element.28, pred[]{:T(512)S(6)} %eq.14), kind=kLoop, calls=%fused_computation.34 | loop fusion | flops 10240 | bytes 22529 | tf_op jit(solution)/shard_map/convert_element_type | solution.py:276
  31.2 1.1 %fusion.6 = bf16[128,1024]{1,0:T(8,128)(2,1)S(1)} fusion(f32[1024]{0:T(1024)S(1)} %bitcast.25, pred[]{:T(512)S(6)} %eq.14, bf16[144,1024]{1,0:T(8,128)(2,1)} %collective-permute-done, bf16[144,1024]{1,0:T(8,128)(2,1)S(1)} %get-tuple-element.28), kind=kLoop, calls=%fused_computation.12 | loop fusion | flops 917504 | bytes 790529 | tf_op jit(solution)/shard_map/convert_element_type | solution.py:278
  32.3 0.1 maximum_maximum_fusion
  32.4 2.6 %collective-permute-start.1 = (bf16[144,1024]{1,0:T(8,128)(2,1)S(1)}, bf16[144,1024]{1,0:T(8,128)(2,1)S(1)}, u32[]{:S(2)}, u32[]{:S(2)}) collective-permute-start(bf16[144,1024]{1,0:T(8,128)(2,1)S(1)} %maximum_maximum_fusion), channel_id=1, source_target_pairs={{0,8},{4,12},{8,0},{12,4},{16,24},{20,28},{24,16},{28,20},{1,9},{5... | collective-permute-start | bytes 884744 | tf_op jit(solution)/shard_map/ppermute | solution.py:305
  35.0 7.7 %collective-permute-done.1 = bf16[144,1024]{1,0:T(8,128)(2,1)S(1)} collective-permute-done((bf16[144,1024]{1,0:T(8,128)(2,1)S(1)}, bf16[144,1024]{1,0:T(8,128)(2,1)S(1)}, u32[]{:S(2)}, u32[]{:S(2)}) %collective-permute-start.1) | collective-permute-done | bytes 294944 | tf_op jit(solution)/shard_map/ppermute | solution.py:305
  42.7 1.2 %fusion.4 = bf16[128,1024]{1,0:T(8,128)(2,1)S(1)} fusion(f32[1024]{0:T(1024)S(1)} %bitcast.27, f32[1024]{0:T(1024)S(1)} %bitcast.26, pred[]{:T(512)S(6)} %eq.15, pred[]{:T(512)S(6)} %eq.14, bf16[144,1024]{1,0:T(8,128)(2,1)S(1)} %collective-permute-done.1, bf16[144,1024]{1,0:T(8,128)(2,1)} %collective-permute-done, bf16[144,1024]{1,0:T(8,128)(2,1)S(1)} %get-tuple-element.28), kind=kLoop, calls=%fused_computation.9 | loop fusion | flops 1572864 | bytes 1056770 | tf_op jit(solution)/shard_map/convert_element_type | solution.py:278
  43.9 0.8 %maximum_maximum_fusion.1 = bf16[144,1024]{1,0:T(8,128)(2,1)} fusion(bf16[1,1024]{1,0:T(2,128)(2,1)S(1)} %get-tuple-element.50, bf16[1,1024]{1,0:T(2,128)(2,1)S(1)} %get-tuple-element.49, bf16[128,1024]{1,0:T(8,128)(2,1)S(1)} %fusion.4, bf16[144]{0:T(256)(128)(2,1)S(1)} %pad.7.clone), kind=kLoop, calls=%fused_computation.14 | loop fusion | flops 1179648 | bytes 561440 | tf_op jit(solution)/shard_map/concatenate | solution.py:278
  44.7 1.8 %collective-permute-start.2 = (bf16[144,1024]{1,0:T(8,128)(2,1)}, bf16[144,1024]{1,0:T(8,128)(2,1)S(1)}, u32[]{:S(2)}, u32[]{:S(2)}) collective-permute-start(bf16[144,1024]{1,0:T(8,128)(2,1)} %maximum_maximum_fusion.1), channel_id=1, source_target_pairs={{0,16},{4,20},{8,24},{12,28},{16,0},{20,4},{24,8},{28,12},{1,17},{... | collective-permute-start | bytes 884744 | tf_op jit(solution)/shard_map/ppermute | solution.py:305
  46.5 7.3 %collective-permute-done.2 = bf16[144,1024]{1,0:T(8,128)(2,1)S(1)} collective-permute-done((bf16[144,1024]{1,0:T(8,128)(2,1)}, bf16[144,1024]{1,0:T(8,128)(2,1)S(1)}, u32[]{:S(2)}, u32[]{:S(2)}) %collective-permute-start.2) | collective-permute-done | bytes 294944 | tf_op jit(solution)/shard_map/ppermute | solution.py:305
  53.7 1.2 %broadcast_select_fusion = (bf16[128,1024]{1,0:T(8,128)(2,1)S(1)}, bf16[128,1024]{1,0:T(8,128)(2,1)S(1)}) fusion(pred[]{:T(512)S(6)} %eq.14, bf16[144,1024]{1,0:T(8,128)(2,1)S(1)} %collective-permute-done.2, f32[1024]{0:T(1024)S(1)} %bitcast.23, bf16[144,1024]{1,0:T(8,128)(2,1)S(1)} %collective-permute-done.1, f32[]{:T(128)S(6)} %select_n.105, ...), kind=kLoop, calls=%fused_computation.15 | loop fusion | flops 1703936 | bytes 1581061 | tf_op jit(solution)/shard_map/jit(_where)/select_n | solution.py:314
  54.9 0.8 %broadcast_select_fusion.1 = bf16[128,1024]{1,0:T(8,128)(2,1)} fusion(bf16[128,1024]{1,0:T(8,128)(2,1)S(1)} %get-tuple-element.42, pred[]{:T(512)S(6)} %eq.14, bf16[144,1024]{1,0:T(8,128)(2,1)S(1)} %collective-permute-done.2, f32[1024]{0:T(1024)S(1)} %bitcast.24, bf16[144,1024]{1,0:T(8,128)(2,1)S(1)} %collective-permute-done.1, f32[]{:T(128)S(6)} %select_n.105), kind=kLoop, calls=%fused_computation.16 | loop fusion | flops 917504 | bytes 1052677 | tf_op jit(solution)/shard_map/jit(_where)/select_n | solution.py:315
  55.8 0.0 collective-permute-start.3
  55.8 3.4 %copy-done.1 = bf16[1024,4096]{1,0:T(8,128)(2,1)S(1)} copy-done((bf16[1024,4096]{1,0:T(8,128)(2,1)S(1)}, bf16[1024,4096]{1,0:T(8,128)(2,1)}, u32[]{:S(2)}) %copy-start.1) | copy-done | bytes 8388632
  59.2 0.0 copy-start.23
  59.2 0.0 copy-start.19
  59.2 7.6 %gate.1 = (bf16[512,1024]{1,0:T(8,128)(2,1)S(1)}, bf16[512,1024]{1,0:T(8,128)(2,1)S(1)}) custom-call(s32[1]{0:T(128)} %bitcast.half_ref, bf16[512,1024]{1,0:T(8,128)(2,1)S(1)} %get-tuple-element.24.normed, bf16[1024,4096]{1,0:T(8,128)(2,1)S(1)} %copy-done.1), custom_call_target="tpu_custom_call" | custom-call | flops 2147483648 | bytes 4194304 | tf_op jit(solution)/shard_map/gate/pallas_call | solution.py:287
  66.8 0.0 copy-start.13
  66.8 1.0 %copy-done.13 = bf16[512,1024]{1,0:T(8,128)(2,1)} copy-done((bf16[512,1024]{1,0:T(8,128)(2,1)}, bf16[512,1024]{1,0:T(8,128)(2,1)S(1)}, u32[]{:S(2)}) %copy-start.13) | copy-done | bytes 1048600
  67.7 0.0 copy-done.6
  67.7 0.0 copy-done.8
  67.7 0.0 copy-done.10
  67.7 0.0 copy-done.12
  67.8 0.0 copy-done.23
  67.8 0.0 copy-start.14
  67.8 1.4 %copy-done.14 = bf16[512,1024]{1,0:T(8,128)(2,1)S(1)} copy-done((bf16[512,1024]{1,0:T(8,128)(2,1)S(1)}, bf16[512,1024]{1,0:T(8,128)(2,1)}, u32[]{:S(2)}) %copy-start.14) | copy-done | bytes 1048600
  69.1 2.0 %inner.1 = (bf16[512,1024]{1,0:T(8,128)(2,1)S(1)}, bf16[512,1024]{1,0:T(8,128)(2,1)S(1)}, bf16[512,1024]{1,0:T(8,128)(2,1)S(1)}, bf16[512,1024]{1,0:T(8,128)(2,1)S(1)}) custom-call(s32[1]{0:T(128)} %bitcast.half_ref, bf16[512,256]{1,0:T(8,128)(2,1)S(1)} %get-tuple-element.23.keys, bf16[512,64]{1,0:T(8,128)(2,1)S(1)} %get-tuple-element.27.fall, ...), custom_call_target="tpu_custom_call" | custom-call | flops 1073741824 | bytes 4194304 | tf_op jit(solution)/shard_map/inner/pallas_call | solution.py:295
  71.2 0.0 copy-done.19
  71.2 0.0 copy-done.2
  71.2 2.4 %mix.2.base = f32[512,1024]{1,0:T(8,128)S(1)} custom-call(s32[1]{0:T(128)} %bitcast.half_ref, bf16[512,256]{1,0:T(8,128)(2,1)S(1)} %get-tuple-element.23.keys, bf16[128,1024]{1,0:T(8,128)(2,1)S(1)} %get-tuple-element.41.state, bf16[512,1024]{1,0:T(8,128)(2,1)S(1)} %get-tuple-element.38.u, bf16[512,1024]{1,0:T(8,128)(2,1)S(1)} %get-tuple-element.39.v, ...), custom_call_target="tpu_custom_call" | custom-call | flops 1073741824 | bytes 4194304 | tf_op jit(solution)/shard_map/mix/pallas_call | solution.py:318
  73.6 0.0 collective-permute-done.3.state
  73.6 3.4 %mix.3 = bf16[512,1024]{1,0:T(8,128)(2,1)} custom-call(s32[1]{0:T(128)} %bitcast.half_ref, bf16[512,256]{1,0:T(8,128)(2,1)S(1)} %get-tuple-element.23.keys, bf16[128,1024]{1,0:T(8,128)(2,1)S(1)} %collective-permute-done.3.state, bf16[512,1024]{1,0:T(8,128)(2,1)S(1)} %get-tuple-element.36.u, bf16[512,1024]{1,0:T(8,128)(2,1)S(1)} %get-tuple-element.37.v, ...), custom_call_target="tpu_custom_call" | custom-call | flops 1073741824 | bytes 4194304 | tf_op jit(solution)/shard_map/mix/pallas_call | solution.py:318
  (11 shorter events, 0.0 us)
Async XLA Ops:
  1.3 2.2 %copy-start.3 = (bf16[2048,1024]{1,0:T(8,128)(2,1)S(1)}, bf16[2048,1024]{1,0:T(8,128)(2,1)}, u32[]{:S(2)}) copy-start(bf16[2048,1024]{1,0:T(8,128)(2,1)} %pos_any.1) | copy-start | bytes 12582916
  3.5 1.6 %copy-start.4 = (bf16[1024,1024]{1,0:T(8,128)(2,1)S(1)}, bf16[1024,1024]{1,0:T(8,128)(2,1)}, u32[]{:S(2)}) copy-start(bf16[1024,1024]{1,0:T(8,128)(2,1)} %enc_out_any.1) | copy-start | bytes 6291460
  5.1 1.0 %copy-start.15 = (bf16[256,1024]{1,0:T(8,128)(2,1)S(1)}, bf16[256,1024]{1,0:T(8,128)(2,1)}, u32[]{:S(2)}) copy-start(bf16[256,1024]{1,0:T(8,128)(2,1)} %enc_in.1) | copy-start | bytes 1572868
  6.1 1.0 %copy-start.16 = (bf16[1024,256]{1,0:T(8,128)(2,1)S(1)}, bf16[1024,256]{1,0:T(8,128)(2,1)}, u32[]{:S(2)}) copy-start(bf16[1024,256]{1,0:T(8,128)(2,1)} %w_keys.1) | copy-start | bytes 1572868
  7.2 0.9 %copy-start.17 = (bf16[512,1,256]{2,0,1:T(8,128)(2,1)S(1)}, bf16[512,1,256]{2,0,1:T(8,128)(2,1)}, u32[]{:S(2)}) copy-start(bf16[512,1,256]{2,0,1:T(8,128)(2,1)} %param.15) | copy-start | bytes 786436
  8.1 0.8 %copy-start.18 = (bf16[1024,32]{0,1:T(8,128)(2,1)S(1)}, bf16[1024,32]{0,1:T(8,128)(2,1)}, u32[]{:S(2)}) copy-start(bf16[1024,32]{0,1:T(8,128)(2,1)} %param.24) | copy-start | bytes 196612
  9.0 0.7 copy-start.20
  9.7 0.7 copy-start.21
  10.3 0.7 copy-start.22
  18.3 1.0 %copy-start.5 = (bf16[512,1024]{1,0:T(8,128)(2,1)}, bf16[512,1024]{1,0:T(8,128)(2,1)S(1)}, u32[]{:S(2)}) copy-start(bf16[512,1024]{1,0:T(8,128)(2,1)S(1)} %get-tuple-element.31.x_o) | copy-start | bytes 3145732
  19.3 1.0 %copy-start.7 = (bf16[512,1024]{1,0:T(8,128)(2,1)}, bf16[512,1024]{1,0:T(8,128)(2,1)S(1)}, u32[]{:S(2)}) copy-start(bf16[512,1024]{1,0:T(8,128)(2,1)S(1)} %get-tuple-element.33.xs_o) | copy-start | bytes 3145732
  20.2 10.2 %collective-permute-start = (bf16[144,1024]{1,0:T(8,128)(2,1)S(1)}, bf16[144,1024]{1,0:T(8,128)(2,1)}, u32[]{:S(2)}, u32[]{:S(2)}) collective-permute-start(bf16[144,1024]{1,0:T(8,128)(2,1)S(1)} %get-tuple-element.29), channel_id=1, source_target_pairs={{0,4},{4,0},{8,12},{12,8},{16,20},{20,16},{24,28},{28,24},{1,5},{5... | collective-permute-start | bytes 884744 | tf_op jit(solution)/shard_map/ppermute | solution.py:262
  20.8 3.4 %copy-start = (bf16[1024,4096]{1,0:T(8,128)(2,1)S(1)}, bf16[1024,4096]{1,0:T(8,128)(2,1)}, u32[]{:S(2)}) copy-start(bf16[1024,4096]{1,0:T(8,128)(2,1)} %w_pair_any.5) | copy-start | bytes 25165828
  28.4 1.0 %copy-start.9 = (bf16[512,1024]{1,0:T(8,128)(2,1)}, bf16[512,1024]{1,0:T(8,128)(2,1)S(1)}, u32[]{:S(2)}) copy-start(bf16[512,1024]{1,0:T(8,128)(2,1)S(1)} %get-tuple-element.30.x_m) | copy-start | bytes 3145732
  29.4 1.0 %copy-start.11 = (bf16[512,1024]{1,0:T(8,128)(2,1)}, bf16[512,1024]{1,0:T(8,128)(2,1)S(1)}, u32[]{:S(2)}) copy-start(bf16[512,1024]{1,0:T(8,128)(2,1)S(1)} %get-tuple-element.32.xs_m) | copy-start | bytes 3145732
  32.4 10.2 %collective-permute-start.1 = (bf16[144,1024]{1,0:T(8,128)(2,1)S(1)}, bf16[144,1024]{1,0:T(8,128)(2,1)S(1)}, u32[]{:S(2)}, u32[]{:S(2)}) collective-permute-start(bf16[144,1024]{1,0:T(8,128)(2,1)S(1)} %maximum_maximum_fusion), channel_id=1, source_target_pairs={{0,8},{4,12},{8,0},{12,4},{16,24},{20,28},{24,16},{28,20},{1,9},{5... | collective-permute-start | bytes 884744 | tf_op jit(solution)/shard_map/ppermute | solution.py:305
  44.7 9.1 %collective-permute-start.2 = (bf16[144,1024]{1,0:T(8,128)(2,1)}, bf16[144,1024]{1,0:T(8,128)(2,1)S(1)}, u32[]{:S(2)}, u32[]{:S(2)}) collective-permute-start(bf16[144,1024]{1,0:T(8,128)(2,1)} %maximum_maximum_fusion.1), channel_id=1, source_target_pairs={{0,16},{4,20},{8,24},{12,28},{16,0},{20,4},{24,8},{28,12},{1,17},{... | collective-permute-start | bytes 884744 | tf_op jit(solution)/shard_map/ppermute | solution.py:305
  55.8 17.8 %collective-permute-start.3 = (bf16[128,1024]{1,0:T(8,128)(2,1)}, bf16[128,1024]{1,0:T(8,128)(2,1)S(1)}, u32[]{:S(2)}, u32[]{:S(2)}) collective-permute-start(bf16[128,1024]{1,0:T(8,128)(2,1)} %broadcast_select_fusion.1), channel_id=1, source_target_pairs={{0,4},{4,0},{8,12},{12,8},{16,20},{20,16},{24,28},{28,24},{1,5},{5... | collective-permute-start | bytes 786440 | tf_op jit(solution)/shard_map/ppermute | solution.py:315
  55.8 3.4 %copy-start.1 = (bf16[1024,4096]{1,0:T(8,128)(2,1)S(1)}, bf16[1024,4096]{1,0:T(8,128)(2,1)}, u32[]{:S(2)}) copy-start(bf16[1024,4096]{1,0:T(8,128)(2,1)} %w_pair_any.5) | copy-start | bytes 25165828
  59.1 8.6 %copy-start.6 = (bf16[512,1024]{1,0:T(8,128)(2,1)S(1)}, bf16[512,1024]{1,0:T(8,128)(2,1)}, u32[]{:S(2)}) copy-start(bf16[512,1024]{1,0:T(8,128)(2,1)} %copy-done.5) | copy-start | bytes 3145732
  59.1 8.6 %copy-start.8 = (bf16[512,1024]{1,0:T(8,128)(2,1)S(1)}, bf16[512,1024]{1,0:T(8,128)(2,1)}, u32[]{:S(2)}) copy-start(bf16[512,1024]{1,0:T(8,128)(2,1)} %copy-done.7) | copy-start | bytes 3145732
  59.1 8.6 %copy-start.10 = (bf16[512,1024]{1,0:T(8,128)(2,1)S(1)}, bf16[512,1024]{1,0:T(8,128)(2,1)}, u32[]{:S(2)}) copy-start(bf16[512,1024]{1,0:T(8,128)(2,1)} %copy-done.9) | copy-start | bytes 3145732
  59.2 8.6 %copy-start.12 = (bf16[512,1024]{1,0:T(8,128)(2,1)S(1)}, bf16[512,1024]{1,0:T(8,128)(2,1)}, u32[]{:S(2)}) copy-start(bf16[512,1024]{1,0:T(8,128)(2,1)} %copy-done.11) | copy-start | bytes 3145732
  59.2 8.6 %copy-start.23 = (f32[32]{0:T(128)S(1)}, f32[32]{0:T(128)}, u32[]{:S(2)}) copy-start(f32[32]{0:T(128)} %param.27) | copy-start | bytes 388
  59.2 12.0 %copy-start.19 = (f32[2048]{0:T(1024)S(1)}, f32[2048]{0:T(1024)}, u32[]{:S(2)}) copy-start(f32[2048]{0:T(1024)} %param.28) | copy-start | bytes 24580
  66.8 1.0 %copy-start.13 = (bf16[512,1024]{1,0:T(8,128)(2,1)}, bf16[512,1024]{1,0:T(8,128)(2,1)S(1)}, u32[]{:S(2)}) copy-start(bf16[512,1024]{1,0:T(8,128)(2,1)S(1)} %get-tuple-element.35.sg_o) | copy-start | bytes 3145732
  67.7 3.5 %copy-start.2 = (bf16[2048,1024]{1,0:T(8,128)(2,1)S(1)}, bf16[2048,1024]{1,0:T(8,128)(2,1)}, u32[]{:S(2)}) copy-start(bf16[2048,1024]{1,0:T(8,128)(2,1)} %w_any.3) | copy-start | bytes 12582916
  67.8 1.4 %copy-start.14 = (bf16[512,1024]{1,0:T(8,128)(2,1)S(1)}, bf16[512,1024]{1,0:T(8,128)(2,1)}, u32[]{:S(2)}) copy-start(bf16[512,1024]{1,0:T(8,128)(2,1)} %copy-done.13) | copy-start | bytes 3145732

commit v3 on v2

v3 whole, which is shorter than its diff:
```python
import functools

import jax
import jax.numpy as jnp
from jax import lax
from jax.experimental import pallas as pl
from jax.experimental.pallas import tpu as pltpu
from jax.sharding import PartitionSpec as P

BF = jnp.bfloat16
F32 = jnp.float32
VM = pl.BlockSpec(memory_space=pltpu.VMEM)
SM = pl.BlockSpec(memory_space=pltpu.SMEM)
ANY = pl.BlockSpec(memory_space=pl.ANY)
LANES = 128
CHUNK = 256
EXTRA = 16


def dot(a, b):
    return jnp.dot(a, b, preferred_element_type=F32)


def dot_t(a, b):
    return lax.dot_general(a, b, (((1,), (1,)), ((), ())), preferred_element_type=F32)


def iota(shape, axis):
    return lax.broadcasted_iota(jnp.int32, shape, axis)


def params(mib):
    return pltpu.CompilerParams(vmem_limit_bytes=mib * 2**20)


def sds(shape, dtype):
    return jax.ShapeDtypeStruct(shape, dtype)


def spread_heads(first_head, heads, head_dim):
    row = iota((2 * heads, CHUNK), 0)
    lane = iota((2 * heads, CHUNK), 1)
    row = jnp.where(row < heads, row, row - heads)
    return (row == first_head + lane // head_dim).astype(F32).astype(BF)


def split_two(value, heads):
    high = value.astype(BF).astype(F32)
    return jnp.where(iota(value.shape, 1) < heads, high, value - high).astype(BF)


def pick_half(tile_a, tile_b, part):
    half = LANES // 2
    low = iota(tile_a.shape, 1) < half
    if part == 0:
        return jnp.where(low, tile_a, pltpu.roll(tile_b, half, 1))
    return jnp.where(low, pltpu.roll(tile_a, half, 1), tile_b)


def compact(ref, part):
    tiles = [ref[:, i * LANES:(i + 1) * LANES] for i in range(2 * CHUNK // LANES)]
    pairs = [pick_half(tiles[i], tiles[i + 1], part) for i in range(0, len(tiles), 2)]
    return jnp.concatenate(pairs, axis=1)


def weight_copies(w_ref, buf, sem, half, count):
    copies = []
    for j in range(count):
        start = pl.multiple_of((half * count + j) * 2 * CHUNK, 2 * CHUNK)
        copies.append(pltpu.make_async_copy(w_ref.at[:, pl.ds(start, 2 * CHUNK)], buf.at[j], sem.at[j]))
    return copies


def project(j, half, heads, head_dim, count, buf, normed, b_t, grow, fall_end, x_ref, xs_ref, s_ref):
    width = b_t.shape[0]
    per = CHUNK // head_dim
    first = (half * count + j) * per
    cols = slice(j * CHUNK, (j + 1) * CHUNK)
    spread = spread_heads(first, heads, head_dim)
    x = dot(normed[...], compact(buf.at[j], 0)).astype(BF)
    scaled = (x.astype(F32) * dot(grow, spread)).astype(BF)
    x_ref[:, cols] = x
    xs_ref[:, cols] = scaled
    decay = dot(fall_end, spread)[EXTRA - 1:EXTRA]
    s_ref[0:width, cols] = (dot(b_t, scaled) * decay).astype(BF)
    high = decay.astype(BF).astype(F32)
    row = iota((EXTRA, CHUNK), 0)
    s_ref[width:width + EXTRA, cols] = jnp.where(row == 0, high, jnp.where(row == 1, decay - high, 0.0)).astype(BF)


def start_all(pairs, sem):
    copies = [pltpu.make_async_copy(src, dst, sem.at[i]) for i, (src, dst) in enumerate(pairs)]
    for c in copies:
        c.start()
    return copies


def encode_kernel(heads, head_dim, here_ref, cell_ref, frames_any, enc_in_any, bias_any, enc_out_any, pos_any, gain_any,
                  w_keys_any, w_step_any, step_bias_any, code_any, w_pair_any,
                  encoded, normed, keys, b_t, grow, fall, x_ref, xs_ref, s_ref,
                  frames, enc_in, bias, enc_out, pos, norm_gain, w_keys, w_step, step_bias, code, buf, sem, wsem):
    half = 1 - here_ref[0] % 2
    count = buf.shape[0]
    cell = cell_ref[0]
    base = pl.multiple_of((cell // EXTRA) * EXTRA, EXTRA)
    small = start_all([(frames_any, frames), (enc_in_any, enc_in), (bias_any, bias), (enc_out_any, enc_out),
                       (pos_any.at[pl.ds(base, EXTRA), :], pos), (gain_any, norm_gain), (w_keys_any, w_keys),
                       (w_step_any, w_step), (step_bias_any, step_bias), (code_any, code)], sem)
    copies = weight_copies(w_pair_any, buf, wsem, half, count)
    for c in copies:
        c.start()
    rows, depth = encoded.shape
    lower = (iota((rows, rows), 0) >= iota((rows, rows), 1)).astype(F32).astype(BF)
    for c in small[:3]:
        c.wait()
    hidden = []
    for j in range(depth // CHUNK):
        cols = slice(j * CHUNK, (j + 1) * CHUNK)
        h = dot(frames[...], enc_in[:, cols]) + bias[:, cols]
        hidden.append(jax.nn.gelu(h, approximate=True).astype(BF))
    hidden = jnp.concatenate(hidden, axis=1)
    for c in small[3:]:
        c.wait()
    row = jnp.sum(jnp.where(iota(pos.shape, 0) == cell - base, pos[...].astype(F32), 0.0), axis=0, keepdims=True)
    square = jnp.zeros((rows, 1), F32)
    for j in range(depth // CHUNK):
        cols = slice(j * CHUNK, (j + 1) * CHUNK)
        e = (dot(hidden, enc_out[:, cols]) + row[:, cols]).astype(BF)
        encoded[:, cols] = e
        e = e.astype(F32)
        square += jnp.sum(e * e, axis=1, keepdims=True)
    inv = lax.rsqrt(square / depth + 1e-05)
    for j in range(depth // CHUNK):
        cols = slice(j * CHUNK, (j + 1) * CHUNK)
        normed[:, cols] = (encoded[:, cols].astype(F32) * inv * norm_gain[:, cols]).astype(BF)
    k = dot(normed[...], w_keys[...]).astype(BF)
    keys[...] = k
    b_t[...] = k[:, :k.shape[1] // 2].T
    ws = w_step[...]
    twice = lambda v: jnp.concatenate([v, v], axis=1)
    raw = dot_t(normed[...], jnp.concatenate([ws, ws], axis=0)) + twice(step_bias[...])
    step = jax.nn.sigmoid(raw).astype(BF)
    cum = dot(lower, step) * twice(-0.0005 - 0.003 * code[...].astype(F32))
    g = split_two(jnp.exp(-cum), heads)
    f = split_two(jnp.exp(cum), heads)
    grow[...] = g
    fall[...] = f
    for j in range(count):
        copies[j].wait()
        project(j, half, heads, head_dim, count, buf, normed, b_t[...], g, f[rows - EXTRA:], x_ref, xs_ref, s_ref)


def second_kernel(heads, head_dim, here_ref, normed, b_t, grow, fall, w_pair_any, x_ref, xs_ref, s_ref, buf, wsem):
    half = here_ref[0] % 2
    count = buf.shape[0]
    copies = weight_copies(w_pair_any, buf, wsem, half, count)
    for c in copies:
        c.start()
    rows = normed.shape[0]
    for j in range(count):
        copies[j].wait()
        project(j, half, heads, head_dim, count, buf, normed, b_t[...], grow[...], fall[rows - EXTRA:], x_ref, xs_ref, s_ref)


def opened(ref):
    width = ref.shape[0] - EXTRA
    tail = ref[width:, :].astype(F32)
    return ref[:width, :].astype(F32), tail[0:1] + tail[1:2]


def close(ref, state, decay):
    width = ref.shape[0] - EXTRA
    ref[:width, :] = state.astype(BF)
    high = decay.astype(BF).astype(F32)
    row = iota((EXTRA, decay.shape[1]), 0)
    ref[width:, :] = jnp.where(row == 0, high, jnp.where(row == 1, decay - high, 0.0)).astype(BF)


def total_kernel(here_ref, mine_ref, got_ref, total_ref):
    mine, mine_decay = opened(mine_ref)
    got, got_decay = opened(got_ref)

    @pl.when(here_ref[0] % 2 == 1)
    def _():
        close(total_ref, mine_decay * got + mine, mine_decay * got_decay)

    @pl.when(here_ref[0] % 2 == 0)
    def _():
        close(total_ref, got_decay * mine + got, mine_decay * got_decay)


def step_kernel(first, reach, here_ref, total_ref, got_ref, before_ref, new_before_ref, new_total_ref):
    later = (here_ref[0] // reach) % 2 == 1
    got, got_decay = opened(got_ref)
    total, total_decay = opened(total_ref)

    @pl.when(later)
    def _():
        if first:
            close(new_before_ref, got, got_decay)
        else:
            before, before_decay = opened(before_ref)
            close(new_before_ref, before + before_decay * got, before_decay * got_decay)
        close(new_total_ref, total_decay * got + total, total_decay * got_decay)

    @pl.when(jnp.logical_not(later))
    def _():
        if first:
            close(new_before_ref, jnp.zeros_like(got), jnp.ones_like(got_decay))
        else:
            new_before_ref[...] = before_ref[...]
        close(new_total_ref, got_decay * total + got, total_decay * got_decay)


def last_kernel(reach, here_ref, got_ref, before_ref, mine_ref, first_ref, keep_ref, send_ref):
    width = keep_ref.shape[0]
    later = (here_ref[0] // reach) % 2 == 1
    got, _ = opened(got_ref)
    before, before_decay = opened(before_ref)
    before = before + jnp.where(later, before_decay, 0.0) * got

    @pl.when(here_ref[0] % 2 == 1)
    def _():
        state, decay = opened(first_ref)
        keep_ref[...] = (decay * before + state).astype(BF)
        send_ref[...] = before.astype(BF)

    @pl.when(here_ref[0] % 2 == 0)
    def _():
        state, decay = opened(mine_ref)
        send_ref[...] = (decay * before + state).astype(BF)
        keep_ref[...] = before.astype(BF)


def gate_kernel(here_ref, normed, w_pair_any, mine, other, buf, wsem):
    count = buf.shape[0] // 2
    lists = []
    for k, half in enumerate((here_ref[0] % 2, 1 - here_ref[0] % 2)):
        lists += weight_copies(w_pair_any, buf.at[pl.ds(k * count, count)], wsem.at[pl.ds(k * count, count)], half, count)
    for c in lists:
        c.start()
    for k, out in enumerate((mine, other)):
        for j in range(count):
            lists[k * count + j].wait()
            z = dot(normed[...], compact(buf.at[k * count + j], 1)).astype(BF).astype(F32)
            out[:, j * CHUNK:(j + 1) * CHUNK] = (z * jax.nn.sigmoid(z)).astype(BF)


def inner_kernel(heads, head_dim, here_ref, keys, fall, skip_any, x_m, x_o, xs_m, xs_o, sg_m, sg_o, u_m, u_o, v_m, v_o, skip, sem):
    copy = pltpu.make_async_copy(skip_any, skip, sem)
    copy.start()
    rows = keys.shape[0]
    width = keys.shape[1] // 2
    per = CHUNK // head_dim
    count = x_m.shape[1] // CHUNK
    scores = dot_t(keys[:, width:], keys[:, :width])
    scores = jnp.where(iota((rows, rows), 0) >= iota((rows, rows), 1), scores, 0.0).astype(BF)
    copy.wait()
    value = jnp.broadcast_to(jnp.concatenate([skip[...], skip[...]], axis=1), (EXTRA, 2 * heads))
    skip_two = split_two(value, heads)
    mid = rows // 2
    groups = ((here_ref[0] % 2, x_m, xs_m, sg_m, u_m, v_m), (1 - here_ref[0] % 2, x_o, xs_o, sg_o, u_o, v_o))
    for half, x, xs, sg, u, v in groups:
        for j in range(count):
            cols = slice(j * CHUNK, (j + 1) * CHUNK)
            spread = spread_heads((half * count + j) * per, heads, head_dim)
            gain = dot(skip_two, spread)[0:1]
            top = dot(scores[:mid, :mid], xs[:mid, cols])
            low = dot(scores[mid:], xs[:, cols])
            for part, inner in ((slice(0, mid), top), (slice(mid, rows), low)):
                grown = dot(fall[part, :], spread)
                gate = sg[part, cols].astype(F32)
                u[part, cols] = (grown * gate).astype(BF)
                v[part, cols] = ((grown * inner + gain * x[part, cols].astype(F32)) * gate).astype(BF)


def mix_kernel(head_dim, last, here_ref, keys, state, u, v, base, gain_any, w_any, out, gain_ref, w_ref, sem):
    half = here_ref[0] % 2
    if last:
        half = 1 - half
    width = keys.shape[1] // 2
    flat = u.shape[1]
    start = pl.multiple_of(half * flat, flat)
    copies = start_all([(gain_any.at[:, pl.ds(start, flat)], gain_ref), (w_any.at[pl.ds(start, flat), :], w_ref)], sem)
    same = (iota((CHUNK, CHUNK), 0) // head_dim) == (iota((CHUNK, CHUNK), 1) // head_dim)
    mean = jnp.where(same, 1.0 / head_dim, 0.0).astype(BF)
    parts = []
    for j in range(flat // CHUNK):
        cols = slice(j * CHUNK, (j + 1) * CHUNK)
        carried = dot(keys[:, width:], state[:, cols])
        g = v[:, cols].astype(F32) + u[:, cols].astype(F32) * carried
        m = dot((g * g).astype(BF), mean)
        if j == 0:
            copies[0].wait()
        parts.append((g * lax.rsqrt(m + 1e-05) * gain_ref[:, cols]).astype(BF))
    mixed = jnp.concatenate(parts, axis=1)
    copies[1].wait()
    for n in range(w_ref.shape[1] // CHUNK):
        cols = slice(n * CHUNK, (n + 1) * CHUNK)
        out[:, cols] = (base[:, cols].astype(F32) + dot(mixed, w_ref[:, cols])).astype(out.dtype)


def body(frames, patch_cell, enc_in, enc_bias, enc_out, pos_table, norm_gain, w_pair, w_keys, w_step,
         step_bias, decay_code, skip_gain, out_gain, w_out):
    rows = frames.shape[0]
    pix = frames.shape[2]
    depth = enc_out.shape[1]
    heads = w_step.shape[1]
    head_dim = w_pair.shape[1] // (2 * heads)
    width = w_keys.shape[1] // 2
    flat = heads * head_dim // 2
    count = flat // CHUNK
    peers = lax.axis_size("tm")
    here = lax.axis_index("tm").astype(jnp.int32).reshape(1)
    row = lambda v: v.reshape(1, -1)
    cost = lambda macs: pl.CostEstimate(flops=2 * macs, bytes_accessed=4 * 2**20, transcendentals=0)
    far = lambda v: pltpu.with_memory_space_constraint(v, pltpu.HBM)
    near = lambda shape, dtype=BF: pltpu.VMEM(shape, dtype)
    sems = lambda n: pltpu.SemaphoreType.DMA((n,))
    pair = lambda by: [(i, i ^ by) for i in range(peers)]

    def call(kernel, name, outs, ins, scratch=(), macs=0):
        specs = [spec for spec, _ in ins]
        return pl.pallas_call(kernel, out_shape=tuple(outs), in_specs=specs, out_specs=(VM,) * len(outs),
                              scratch_shapes=list(scratch), compiler_params=params(24), name=name,
                              cost_estimate=cost(macs))(*[v for _, v in ins])

    vm = lambda *vs: [(VM, v) for v in vs]
    hbm = lambda *vs: [(pl.BlockSpec(memory_space=pltpu.HBM), far(v)) for v in vs]
    where = [(SM, here)]
    w_pair, w_out, gain_row = far(w_pair), far(w_out), row(out_gain)

    halves, message = near((rows, flat)), near((width + EXTRA, flat))
    encoded, normed, keys, b_t, grow, fall, x_o, xs_o, s_o = call(
        functools.partial(encode_kernel, heads, head_dim), "encode",
        (near((rows, depth)), near((rows, depth)), near((rows, 2 * width)), near((width, rows)),
         near((rows, 2 * heads)), near((rows, 2 * heads)), halves, halves, message),
        where + [(SM, patch_cell)] + hbm(frames.reshape(rows, pix), enc_in, row(enc_bias), enc_out, pos_table, row(norm_gain),
                                         w_keys, w_step.T, row(step_bias), row(decay_code), w_pair),
        [near((rows, pix)), near((pix, depth)), near((1, depth), F32), near((depth, depth)), near((EXTRA, depth)),
         near((1, depth), F32), near((depth, 2 * width)), near((heads, depth)), near((1, heads), F32),
         near((1, heads), jnp.int32), near((count, depth, 2 * CHUNK)), sems(10), sems(count)],
        rows * depth * depth)
    got_first = lax.ppermute(s_o, "tm", pair(1))
    x_m, xs_m, s_m = call(
        functools.partial(second_kernel, heads, head_dim), "project", (halves, halves, message),
        where + vm(normed, b_t, grow, fall) + hbm(w_pair),
        [near((count, depth, 2 * CHUNK)), sems(count)], rows * depth * flat)
    total, = call(total_kernel, "total", (message,), where + vm(s_m, got_first))

    sg_m, sg_o = call(gate_kernel, "gate", (halves, halves), where + vm(normed) + hbm(w_pair),
                      [near((2 * count, depth, 2 * CHUNK)), sems(2 * count)], 2 * rows * depth * flat)
    u_m, u_o, v_m, v_o = call(
        functools.partial(inner_kernel, heads, head_dim), "inner", (halves,) * 4,
        where + vm(keys, fall) + hbm(row(skip_gain)) + vm(x_m, x_o, xs_m, xs_o, sg_m, sg_o),
        [near((1, heads), F32), pltpu.SemaphoreType.DMA], rows * rows * flat * 2)

    before = total
    ready = [sg_m, u_m]
    reach = 2
    while reach * 2 < peers:
        got = lax.ppermute(total, "tm", pair(reach))
        if ready:
            got, _ = lax.optimization_barrier((got, ready.pop(0)))
        before, total = call(functools.partial(step_kernel, reach == 2, reach), "step", (message, message),
                             where + vm(total, got, before))
        reach *= 2
    got = lax.ppermute(total, "tm", pair(reach))
    for value in ready:
        got, _ = lax.optimization_barrier((got, value))
    state_m, send = call(functools.partial(last_kernel, reach), "last", (near((width, flat)),) * 2,
                         where + vm(got, before, s_m, got_first))
    state_o = lax.ppermute(send, "tm", pair(1))

    def mixed(last, state, u, v, base, kind):
        return call(functools.partial(mix_kernel, head_dim, last), "mix",
                    (sds((rows, depth), kind) if last else near((rows, depth), kind),),
                    where + vm(keys, state, u, v, base) + hbm(gain_row, w_out),
                    [near((1, flat), F32), near((flat, depth)), sems(2)], rows * depth * flat)[0]

    partial = mixed(False, state_m, u_m, v_m, encoded, F32)
    return mixed(True, state_o, u_o, v_o, partial, BF).reshape(rows, 1, depth)


def solution(mesh):
    placed = (P("tm", "space", None), P("space")) + (P(),) * 13
    return jax.shard_map(body, mesh=mesh, in_specs=placed, out_specs=P("tm", "space", None), check_vma=False)
```

time: 77.9 us -> 42.6 us (0.55)
  local copies, waits for them, and re-layouts: 22.8 us -> 0 us
  waiting for transfers between devices: 15 us -> 4.6 us
  other arithmetic: 6.69 us -> 0 us
  Pallas kernels: 26.9 us -> 31.8 us
    unnamed x48 -> x0, local copies, waits for them, and re-layouts: 22.7 us -> none
    ppermute x4, waiting for transfers between devices: 15 us -> 4.6 us  [the longest x2 4.59 us: body(): got = lax.ppermute(total, 'tm', pair(reach))]
    pallas_call x6 -> x9, Pallas kernels: 26.9 us -> 31.8 us  [call(): pl.pallas_call(kernel, out_shape=tuple(outs), in_specs=specs, out_specs=(...]
    convert_element_type x5 -> x0, other arithmetic: 3.06 us -> none  [the longest x2 2.23 us: closed(): state.astype(BF)]
    select_n x3 -> x0, other arithmetic: 2.03 us -> none  [the longest x1 1.17 us: body(): state_m = jnp.where(odd, at_odd, at_even)]
    concatenate x2 -> x0, other arithmetic: 0.94 us -> none  [closed(): jnp.concatenate([state.astype(BF), high, low, jnp.zeros((EXTRA - 2, flat)...]
  transfers between devices with their start and end apart: 4 -> 4, of which waited for: 2 -> 2; matrix products, arithmetic and copies ran while one was open for 0% -> 0% of each run, Pallas kernels for 21% -> 43%
where the time goes in v3:
time: 42.6 us; the launch traced here: 42.3 us
  Pallas kernels  31.8 us (75%)
  starting transfers between devices  5 us (12%)
  waiting for transfers between devices  4.6 us (11%)
  between operations  0.89 us (2%)
    pallas_call x9, Pallas kernels, call(): pl.pallas_call(kernel, out_shape=tuple(outs), in_specs=specs, out_specs=(...  31.8 us
    ppermute x2, waiting for transfers between devices, body(): got = lax.ppermute(total, 'tm', pair(reach))  4.59 us
    ppermute x2, starting transfers between devices, body(): got = lax.ppermute(total, 'tm', pair(reach))  4.42 us
  transfers between devices with their start and end apart: 4, of which 2 were waited for; matrix products, arithmetic and copies ran while one was open for 0% of the time, Pallas kernels for 43%

profile of v3, /device:TPU:0, one launch (start us, length us, event | category | flops | bytes accessed | tf_op | source)
XLA Modules:
  0.0 42.3 jit_solution(193661591935513394)
XLA Ops:
  0.7 9.0 %encode.1 = (bf16[512,1024]{1,0:T(8,128)(2,1)S(1)}, bf16[512,1024]{1,0:T(8,128)(2,1)S(1)}, bf16[512,256]{1,0:T(8,128)(2,1)S(1)}, bf16[128,512]{1,0:T(8,128)(2,1)...) custom-call(s32[1]{0:T(128)} %bitcast.here_ref, ...), custom_call_target="tpu_custom_call" | custom-call | flops 1073741824 | bytes 4194304 | tf_op jit(solution)/shard_map/encode/pallas_call | solution.py:324
  9.7 0.5 %collective-permute-start = (bf16[144,1024]{1,0:T(8,128)(2,1)S(1)}, bf16[144,1024]{1,0:T(8,128)(2,1)S(1)}, u32[]{:S(2)}, u32[]{:S(2)}) collective-permute-start(bf16[144,1024]{1,0:T(8,128)(2,1)S(1)} %get-tuple-element.35), channel_id=1, source_target_pairs={{0,4},{4,0},{8,12},{12,8},{16,20},{20,16},{24,28},{28,24},{1,5},{5... | collective-permute-start | bytes 884744 | tf_op jit(solution)/shard_map/ppermute | solution.py:344
  10.2 5.0 %project.1 = (bf16[512,1024]{1,0:T(8,128)(2,1)S(1)}, bf16[512,1024]{1,0:T(8,128)(2,1)S(1)}, bf16[144,1024]{1,0:T(8,128)(2,1)S(1)}) custom-call(s32[1]{0:T(128)} %bitcast.here_ref, bf16[512,1024]{1,0:T(8,128)(2,1)S(1)} %get-tuple-element.30.normed, bf16[128,512]{1,0:T(8,128)(2,1)S(1)} %get-tuple-element.31.b_t, bf16[512,64]{1,0:T(8,128)(2,1)S(1)} %get-tuple-element.32.grow, ...), custom_call_target="tpu_custom_call" | custom-call | flops 1073741824 | bytes 4194304 | tf_op jit(solution)/shard_map/project/pallas_call | solution.py:324
  15.2 0.0 collective-permute-done.got_ref.first_ref
  15.2 0.3 total.1.total_ref.before_ref
  15.5 2.6 %collective-permute-start.1 = (bf16[144,1024]{1,0:T(8,128)(2,1)S(1)}, bf16[144,1024]{1,0:T(8,128)(2,1)S(1)}, u32[]{:S(2)}, u32[]{:S(2)}) collective-permute-start(bf16[144,1024]{1,0:T(8,128)(2,1)S(1)} %total.1.total_ref.before_ref), channel_id=1, source_target_pairs={{0,8},{4,12},{8,0},{12,4},{16,24},{20,28},{24,16},{28,20},{1,9},{5... | collective-permute-start | bytes 884744 | tf_op jit(solution)/shard_map/ppermute | solution.py:362
  18.1 7.5 %gate.1 = (bf16[512,1024]{1,0:T(8,128)(2,1)S(1)}, bf16[512,1024]{1,0:T(8,128)(2,1)S(1)}) custom-call(s32[1]{0:T(128)} %bitcast.here_ref, bf16[512,1024]{1,0:T(8,128)(2,1)S(1)} %get-tuple-element.30.normed, bf16[1024,4096]{1,0:T(8,128)(2,1)} %w_pair_any.5), custom_call_target="tpu_custom_call" | custom-call | flops 2147483648 | bytes 4194304 | tf_op jit(solution)/shard_map/gate/pallas_call | solution.py:324
  25.7 0.1 collective-permute-done.1.got_ref
  25.8 0.1 step.1
  25.9 1.8 %collective-permute-start.2 = (bf16[144,1024]{1,0:T(8,128)(2,1)S(1)}, bf16[144,1024]{1,0:T(8,128)(2,1)S(1)}, u32[]{:S(2)}, u32[]{:S(2)}) collective-permute-start(bf16[144,1024]{1,0:T(8,128)(2,1)S(1)} %get-tuple-element.38), channel_id=1, source_target_pairs={{0,16},{4,20},{8,24},{12,28},{16,0},{20,4},{24,8},{28,12},{1,17},{... | collective-permute-start | bytes 884744 | tf_op jit(solution)/shard_map/ppermute | solution.py:368
  27.8 2.8 %inner.1 = (bf16[512,1024]{1,0:T(8,128)(2,1)S(1)}, bf16[512,1024]{1,0:T(8,128)(2,1)S(1)}, bf16[512,1024]{1,0:T(8,128)(2,1)S(1)}, bf16[512,1024]{1,0:T(8,128)(2,1)S(1)}) custom-call(s32[1]{0:T(128)} %bitcast.here_ref, bf16[512,256]{1,0:T(8,128)(2,1)S(1)} %get-tuple-element.29.keys, bf16[512,64]{1,0:T(8,128)(2,1)S(1)} %get-tuple-element.33.fall, ...), custom_call_target="tpu_custom_call" | custom-call | flops 1073741824 | bytes 4194304 | tf_op jit(solution)/shard_map/inner/pallas_call | solution.py:324
  30.5 4.5 %collective-permute-done.2.got_ref = bf16[144,1024]{1,0:T(8,128)(2,1)S(1)} collective-permute-done((bf16[144,1024]{1,0:T(8,128)(2,1)S(1)}, bf16[144,1024]{1,0:T(8,128)(2,1)S(1)}, u32[]{:S(2)}, u32[]{:S(2)}) %collective-permute-start.2) | collective-permute-done | bytes 294944 | tf_op jit(solution)/shard_map/ppermute | solution.py:368
  35.0 0.2 last.1
  35.2 0.1 collective-permute-start.3
  35.3 2.9 %mix.2.base = f32[512,1024]{1,0:T(8,128)S(1)} custom-call(s32[1]{0:T(128)} %bitcast.here_ref, bf16[512,256]{1,0:T(8,128)(2,1)S(1)} %get-tuple-element.29.keys, bf16[128,1024]{1,0:T(8,128)(2,1)S(1)} %get-tuple-element.50.state, bf16[512,1024]{1,0:T(8,128)(2,1)S(1)} %get-tuple-element.44.u, bf16[512,1024]{1,0:T(8,128)(2,1)S(1)} %get-tuple-element.51.v, ...), custom_call_target="tpu_custom_call" | custom-call | flops 1073741824 | bytes 4194304 | tf_op jit(solution)/shard_map/mix/pallas_call | solution.py:324
  38.2 0.0 collective-permute-done.3.state
  38.2 3.9 %mix.3 = bf16[512,1024]{1,0:T(8,128)(2,1)} custom-call(s32[1]{0:T(128)} %bitcast.here_ref, bf16[512,256]{1,0:T(8,128)(2,1)S(1)} %get-tuple-element.29.keys, bf16[128,1024]{1,0:T(8,128)(2,1)S(1)} %collective-permute-done.3.state, bf16[512,1024]{1,0:T(8,128)(2,1)S(1)} %get-tuple-element.48.u, bf16[512,1024]{1,0:T(8,128)(2,1)S(1)} %get-tuple-element.49.v, ...), custom_call_target="tpu_custom_call" | custom-call | flops 1073741824 | bytes 4194304 | tf_op jit(solution)/shard_map/mix/pallas_call | solution.py:324
Async XLA Ops:
  9.7 5.5 %collective-permute-start = (bf16[144,1024]{1,0:T(8,128)(2,1)S(1)}, bf16[144,1024]{1,0:T(8,128)(2,1)S(1)}, u32[]{:S(2)}, u32[]{:S(2)}) collective-permute-start(bf16[144,1024]{1,0:T(8,128)(2,1)S(1)} %get-tuple-element.35), channel_id=1, source_target_pairs={{0,4},{4,0},{8,12},{12,8},{16,20},{20,16},{24,28},{28,24},{1,5},{5... | collective-permute-start | bytes 884744 | tf_op jit(solution)/shard_map/ppermute | solution.py:344
  15.5 10.2 %collective-permute-start.1 = (bf16[144,1024]{1,0:T(8,128)(2,1)S(1)}, bf16[144,1024]{1,0:T(8,128)(2,1)S(1)}, u32[]{:S(2)}, u32[]{:S(2)}) collective-permute-start(bf16[144,1024]{1,0:T(8,128)(2,1)S(1)} %total.1.total_ref.before_ref), channel_id=1, source_target_pairs={{0,8},{4,12},{8,0},{12,4},{16,24},{20,28},{24,16},{28,20},{1,9},{5... | collective-permute-start | bytes 884744 | tf_op jit(solution)/shard_map/ppermute | solution.py:362
  25.9 9.1 %collective-permute-start.2 = (bf16[144,1024]{1,0:T(8,128)(2,1)S(1)}, bf16[144,1024]{1,0:T(8,128)(2,1)S(1)}, u32[]{:S(2)}, u32[]{:S(2)}) collective-permute-start(bf16[144,1024]{1,0:T(8,128)(2,1)S(1)} %get-tuple-element.38), channel_id=1, source_target_pairs={{0,16},{4,20},{8,24},{12,28},{16,0},{20,4},{24,8},{28,12},{1,17},{... | collective-permute-start | bytes 884744 | tf_op jit(solution)/shard_map/ppermute | solution.py:368
  35.2 3.0 %collective-permute-start.3 = (bf16[128,1024]{1,0:T(8,128)(2,1)S(1)}, bf16[128,1024]{1,0:T(8,128)(2,1)S(1)}, u32[]{:S(2)}, u32[]{:S(2)}) collective-permute-start(bf16[128,1024]{1,0:T(8,128)(2,1)S(1)} %get-tuple-element.47), channel_id=1, source_target_pairs={{0,4},{4,0},{8,12},{12,8},{16,20},{20,16},{24,28},{28,24},{1,5},{5... | collective-permute-start | bytes 786440 | tf_op jit(solution)/shard_map/ppermute | solution.py:373

commit v4 on v3

v4 whole, which is shorter than its diff:
```python
import functools

import jax
import jax.numpy as jnp
from jax import lax
from jax.experimental import pallas as pl
from jax.experimental.pallas import tpu as pltpu
from jax.sharding import PartitionSpec as P

BF = jnp.bfloat16
F32 = jnp.float32
VM = pl.BlockSpec(memory_space=pltpu.VMEM)
SM = pl.BlockSpec(memory_space=pltpu.SMEM)
ANY = pl.BlockSpec(memory_space=pl.ANY)
LANES = 128
CHUNK = 256
EXTRA = 16


def dot(a, b):
    return jnp.dot(a, b, preferred_element_type=F32)


def dot_t(a, b):
    return lax.dot_general(a, b, (((1,), (1,)), ((), ())), preferred_element_type=F32)


def iota(shape, axis):
    return lax.broadcasted_iota(jnp.int32, shape, axis)


def params(mib):
    return pltpu.CompilerParams(vmem_limit_bytes=mib * 2**20)


def sds(shape, dtype):
    return jax.ShapeDtypeStruct(shape, dtype)


def spread_heads(first_head, heads, head_dim):
    row = iota((2 * heads, CHUNK), 0)
    lane = iota((2 * heads, CHUNK), 1)
    row = jnp.where(row < heads, row, row - heads)
    return (row == first_head + lane // head_dim).astype(F32).astype(BF)


def split_two(value, heads):
    high = value.astype(BF).astype(F32)
    return jnp.where(iota(value.shape, 1) < heads, high, value - high).astype(BF)


def pick_half(tile_a, tile_b, part):
    half = LANES // 2
    low = iota(tile_a.shape, 1) < half
    if part == 0:
        return jnp.where(low, tile_a, pltpu.roll(tile_b, half, 1))
    return jnp.where(low, pltpu.roll(tile_a, half, 1), tile_b)


def compact(ref, j, part):
    start = j * 2 * CHUNK
    tiles = [ref[:, start + i:start + i + LANES] for i in range(0, 2 * CHUNK, LANES)]
    pairs = [pick_half(tiles[i], tiles[i + 1], part) for i in range(0, len(tiles), 2)]
    return jnp.concatenate(pairs, axis=1)


def project(half, group, heads, head_dim, w, normed, b_t, grow, fall_end, x_ref, xs_ref, s_ref):
    width = b_t.shape[0]
    size = x_ref.shape[1]
    first = (half * 2 + group) * (size // head_dim)
    for j in range(size // CHUNK):
        cols = slice(j * CHUNK, (j + 1) * CHUNK)
        spread = spread_heads(first + j * (CHUNK // head_dim), heads, head_dim)
        x = dot(normed[...], compact(w, j, 0)).astype(BF)
        scaled = (x.astype(F32) * dot(grow, spread)).astype(BF)
        x_ref[:, cols] = x
        xs_ref[:, cols] = scaled
        decay = dot(fall_end, spread)[EXTRA - 1:EXTRA]
        s_ref[0:width, cols] = (dot(b_t, scaled) * decay).astype(BF)
        s_ref[width:width + EXTRA, cols] = decay_rows(decay)


def decay_rows(decay):
    high = decay.astype(BF).astype(F32)
    row = iota((EXTRA, decay.shape[1]), 0)
    return jnp.where(row == 0, high, jnp.where(row == 1, decay - high, 0.0)).astype(BF)


def start_all(pairs, sem):
    copies = [pltpu.make_async_copy(src, dst, sem.at[i]) for i, (src, dst) in enumerate(pairs)]
    for c in copies:
        c.start()
    return copies


def encode_kernel(heads, head_dim, here_ref, cell_ref, frames_any, enc_in_any, bias_any, enc_out_any, pos_any, gain_any,
                  w_keys_any, w_step_any, step_bias_any, code_any, w_pair_any,
                  encoded, normed, keys, b_t, grow, fall, x_ref, xs_ref, s_ref, w_o1, w_o2, w_m1, w_m2,
                  frames, enc_in, bias, enc_out, pos, norm_gain, w_keys, w_step, step_bias, code, sem, wsem):
    half = 1 - here_ref[0] % 2
    cell = cell_ref[0]
    base = pl.multiple_of((cell // EXTRA) * EXTRA, EXTRA)
    small = start_all([(frames_any, frames), (enc_in_any, enc_in), (bias_any, bias), (enc_out_any, enc_out),
                       (pos_any.at[pl.ds(base, EXTRA), :], pos), (gain_any, norm_gain), (w_keys_any, w_keys),
                       (w_step_any, w_step), (step_bias_any, step_bias), (code_any, code)], sem)
    size = w_o1.shape[1]
    columns = lambda which, group: w_pair_any.at[:, pl.ds(pl.multiple_of((which * 2 + group) * size, size), size)]
    rows, depth = encoded.shape
    lower = (iota((rows, rows), 0) >= iota((rows, rows), 1)).astype(F32).astype(BF)
    for c in small[:3]:
        c.wait()
    big = start_all([(columns(half, 0), w_o1), (columns(1 - half, 0), w_m1), (columns(half, 1), w_o2),
                     (columns(1 - half, 1), w_m2)], wsem)
    hidden = []
    for j in range(depth // CHUNK):
        cols = slice(j * CHUNK, (j + 1) * CHUNK)
        h = dot(frames[...], enc_in[:, cols]) + bias[:, cols]
        hidden.append(jax.nn.gelu(h, approximate=True).astype(BF))
    hidden = jnp.concatenate(hidden, axis=1)
    for c in small[3:]:
        c.wait()
    row = jnp.sum(jnp.where(iota(pos.shape, 0) == cell - base, pos[...].astype(F32), 0.0), axis=0, keepdims=True)
    square = jnp.zeros((rows, 1), F32)
    for j in range(depth // CHUNK):
        cols = slice(j * CHUNK, (j + 1) * CHUNK)
        e = (dot(hidden, enc_out[:, cols]) + row[:, cols]).astype(BF)
        encoded[:, cols] = e
        e = e.astype(F32)
        square += jnp.sum(e * e, axis=1, keepdims=True)
    inv = lax.rsqrt(square / depth + 1e-05)
    for j in range(depth // CHUNK):
        cols = slice(j * CHUNK, (j + 1) * CHUNK)
        normed[:, cols] = (encoded[:, cols].astype(F32) * inv * norm_gain[:, cols]).astype(BF)
    k = dot(normed[...], w_keys[...]).astype(BF)
    keys[...] = k
    b_t[...] = k[:, :k.shape[1] // 2].T
    ws = w_step[...]
    twice = lambda v: jnp.concatenate([v, v], axis=1)
    raw = dot_t(normed[...], jnp.concatenate([ws, ws], axis=0)) + twice(step_bias[...])
    step = jax.nn.sigmoid(raw).astype(BF)
    cum = dot(lower, step) * twice(-0.0005 - 0.003 * code[...].astype(F32))
    g = split_two(jnp.exp(-cum), heads)
    f = split_two(jnp.exp(cum), heads)
    grow[...] = g
    fall[...] = f
    big[0].wait()
    project(half, 0, heads, head_dim, w_o1, normed, b_t[...], g, f[rows - EXTRA:], x_ref, xs_ref, s_ref)
    for c in big[1:]:
        c.wait()


def project_kernel(heads, head_dim, own, group, here_ref, normed, b_t, grow, fall, w, x_ref, xs_ref, s_ref):
    half = (here_ref[0] + 1 - own) % 2
    rows = normed.shape[0]
    project(half, group, heads, head_dim, w, normed, b_t[...], grow[...], fall[rows - EXTRA:], x_ref, xs_ref, s_ref)


def opened(ref):
    width = ref.shape[0] - EXTRA
    tail = ref[width:, :].astype(F32)
    return ref[:width, :].astype(F32), tail[0:1] + tail[1:2]


def close(ref, state, decay):
    width = ref.shape[0] - EXTRA
    ref[:width, :] = state.astype(BF)
    ref[width:, :] = decay_rows(decay)


def total_kernel(here_ref, mine_ref, got_ref, total_ref):
    mine, mine_decay = opened(mine_ref)
    got, got_decay = opened(got_ref)

    @pl.when(here_ref[0] % 2 == 1)
    def _():
        close(total_ref, mine_decay * got + mine, mine_decay * got_decay)

    @pl.when(here_ref[0] % 2 == 0)
    def _():
        close(total_ref, got_decay * mine + got, mine_decay * got_decay)


def step_kernel(first, reach, here_ref, total_ref, got_ref, before_ref, new_before_ref, new_total_ref):
    later = (here_ref[0] // reach) % 2 == 1
    got, got_decay = opened(got_ref)
    total, total_decay = opened(total_ref)

    @pl.when(later)
    def _():
        if first:
            close(new_before_ref, got, got_decay)
        else:
            before, before_decay = opened(before_ref)
            close(new_before_ref, before + before_decay * got, before_decay * got_decay)
        close(new_total_ref, total_decay * got + total, total_decay * got_decay)

    @pl.when(jnp.logical_not(later))
    def _():
        if first:
            close(new_before_ref, jnp.zeros_like(got), jnp.ones_like(got_decay))
        else:
            new_before_ref[...] = before_ref[...]
        close(new_total_ref, got_decay * total + got, total_decay * got_decay)


def last_kernel(reach, here_ref, got_ref, before_ref, mine_ref, first_ref, keep_ref, send_ref):
    width = keep_ref.shape[0]
    later = (here_ref[0] // reach) % 2 == 1
    got, _ = opened(got_ref)
    before, before_decay = opened(before_ref)
    before = before + jnp.where(later, before_decay, 0.0) * got

    @pl.when(here_ref[0] % 2 == 1)
    def _():
        state, decay = opened(first_ref)
        keep_ref[...] = (decay * before + state).astype(BF)
        send_ref[...] = before.astype(BF)

    @pl.when(here_ref[0] % 2 == 0)
    def _():
        state, decay = opened(mine_ref)
        send_ref[...] = (decay * before + state).astype(BF)
        keep_ref[...] = before.astype(BF)


def inner_kernel(heads, head_dim, own, group, here_ref, normed, keys, fall, skip_any, w_out_any, w, x, xs,
                 u, v, w_rows, skip, sem):
    half = (here_ref[0] + 1 - own) % 2
    rows = keys.shape[0]
    width = keys.shape[1] // 2
    size = x.shape[1]
    start = pl.multiple_of((half * 2 + group) * size, size)
    copies = start_all([(skip_any, skip), (w_out_any.at[pl.ds(start, size), :], w_rows)], sem)
    scores = dot_t(keys[:, width:], keys[:, :width])
    scores = jnp.where(iota((rows, rows), 0) >= iota((rows, rows), 1), scores, 0.0).astype(BF)
    mid = rows // 2
    copies[0].wait()
    both = jnp.broadcast_to(jnp.concatenate([skip[...], skip[...]], axis=1), (EXTRA, 2 * heads))
    skip_two = split_two(both, heads)
    first = (half * 2 + group) * (size // head_dim)
    for j in range(size // CHUNK):
        cols = slice(j * CHUNK, (j + 1) * CHUNK)
        z = dot(normed[...], compact(w, j, 1)).astype(BF).astype(F32)
        gate = z * jax.nn.sigmoid(z)
        spread = spread_heads(first + j * (CHUNK // head_dim), heads, head_dim)
        gain = dot(skip_two, spread)[0:1]
        grown = dot(fall[...], spread)
        u[:, cols] = (grown * gate).astype(BF)
        top = dot(scores[:mid, :mid], xs[:mid, cols])
        low = dot(scores[mid:], xs[:, cols])
        for part, inner in ((slice(0, mid), top), (slice(mid, rows), low)):
            v[part, cols] = ((grown[part] * inner + gain * x[part, cols].astype(F32)) * gate[part]).astype(BF)
    copies[1].wait()


def mix_kernel(head_dim, places, here_ref, keys, base, gain_any, *refs):
    many = len(places)
    states, us, vs, ws = (refs[i * many:(i + 1) * many] for i in range(4))
    out, gain_ref, sem = refs[4 * many:]
    width = keys.shape[1] // 2
    size = us[0].shape[1]
    starts = [((here_ref[0] + 1 - own) % 2 * 2 + group) * size for own, group in places]
    copies = start_all([(gain_any.at[:, pl.ds(pl.multiple_of(s, size), size)], gain_ref.at[pl.ds(i, 1), :])
                        for i, s in enumerate(starts)], sem)
    same = (iota((CHUNK, CHUNK), 0) // head_dim) == (iota((CHUNK, CHUNK), 1) // head_dim)
    mean = jnp.where(same, 1.0 / head_dim, 0.0).astype(BF)
    work = []
    for state, u, v in zip(states, us, vs):
        for j in range(size // CHUNK):
            cols = slice(j * CHUNK, (j + 1) * CHUNK)
            carried = dot(keys[:, width:], state[:, cols])
            g = v[:, cols].astype(F32) + u[:, cols].astype(F32) * carried
            work.append((g, dot((g * g).astype(BF), mean)))
    for c in copies:
        c.wait()
    mixed = []
    for i in range(many):
        row = gain_ref[i:i + 1, :]
        parts = []
        for j in range(size // CHUNK):
            g, m = work[i * (size // CHUNK) + j]
            parts.append((g * lax.rsqrt(m + 1e-05) * row[:, j * CHUNK:(j + 1) * CHUNK]).astype(BF))
        mixed.append(jnp.concatenate(parts, axis=1))
    for n in range(out.shape[1] // CHUNK):
        cols = slice(n * CHUNK, (n + 1) * CHUNK)
        total = base[:, cols].astype(F32)
        for part, w in zip(mixed, ws):
            total = total + dot(part, w[:, cols])
        out[:, cols] = total.astype(out.dtype)


def body(frames, patch_cell, enc_in, enc_bias, enc_out, pos_table, norm_gain, w_pair, w_keys, w_step,
         step_bias, decay_code, skip_gain, out_gain, w_out):
    rows = frames.shape[0]
    pix = frames.shape[2]
    depth = enc_out.shape[1]
    heads = w_step.shape[1]
    head_dim = w_pair.shape[1] // (2 * heads)
    width = w_keys.shape[1] // 2
    size = heads * head_dim // 4
    peers = lax.axis_size("tm")
    here = lax.axis_index("tm").astype(jnp.int32).reshape(1)
    row = lambda v: v.reshape(1, -1)
    far = lambda v: pltpu.with_memory_space_constraint(v, pltpu.HBM)
    near = lambda shape, dtype=BF: pltpu.VMEM(shape, dtype)
    sems = lambda n: pltpu.SemaphoreType.DMA((n,))
    pair = lambda by: [(i, i ^ by) for i in range(peers)]
    after = lambda value, *first: lax.optimization_barrier((value,) + first)[0]

    def call(kernel, name, outs, ins, scratch=(), macs=0):
        specs = [spec for spec, _ in ins]
        cost = pl.CostEstimate(flops=2 * macs, bytes_accessed=4 * 2**20, transcendentals=0)
        return pl.pallas_call(kernel, out_shape=tuple(outs), in_specs=specs, out_specs=(VM,) * len(outs),
                              scratch_shapes=list(scratch), compiler_params=params(24), name=name,
                              cost_estimate=cost)(*[v for _, v in ins])

    vm = lambda *vs: [(VM, v) for v in vs]
    hbm = lambda *vs: [(pl.BlockSpec(memory_space=pltpu.HBM), far(v)) for v in vs]
    where = [(SM, here)]

    part, message, weight = near((rows, size)), near((width + EXTRA, size)), near((depth, 2 * size))
    encoded, normed, keys, b_t, grow, fall, x_o1, xs_o1, s_o1, w_o1, w_o2, w_m1, w_m2 = call(
        functools.partial(encode_kernel, heads, head_dim), "encode",
        (near((rows, depth)), near((rows, depth)), near((rows, 2 * width)), near((width, rows)),
         near((rows, 2 * heads)), near((rows, 2 * heads)), part, part, message) + (weight,) * 4,
        where + [(SM, patch_cell)] + hbm(frames.reshape(rows, pix), enc_in, row(enc_bias), enc_out, pos_table, row(norm_gain),
                                         w_keys, w_step.T, row(step_bias), row(decay_code), w_pair),
        [near((rows, pix)), near((pix, depth)), near((1, depth), F32), near((depth, depth)), near((EXTRA, depth)),
         near((1, depth), F32), near((depth, 2 * width)), near((heads, depth)), near((1, heads), F32),
         near((1, heads), jnp.int32), sems(10), sems(4)],
        rows * depth * depth)

    def projected(own, group, w):
        return call(functools.partial(project_kernel, heads, head_dim, own, group), "project", (part, part, message),
                    where + vm(normed, b_t, grow, fall, w), (), rows * depth * size)

    def inner(own, group, w, x, xs):
        return call(functools.partial(inner_kernel, heads, head_dim, own, group), "inner",
                    (part, part, near((size, depth))),
                    where + vm(normed, keys, fall) + hbm(skip_row, w_out) + vm(w, x, xs),
                    [near((1, heads), F32), sems(2)], rows * depth * size)

    def mixed(places, base, kind, *groups):
        states, us, vs, ws = zip(*groups)
        last = kind == BF
        return call(functools.partial(mix_kernel, head_dim, places), "mix",
                    (sds((rows, depth), kind) if last else near((rows, depth), kind),),
                    where + vm(keys, base) + hbm(gain_row) + vm(*states, *us, *vs, *ws),
                    [near((len(places), size), F32), sems(len(places))], len(places) * rows * depth * size)[0]

    skip_row, gain_row = row(skip_gain), row(out_gain)
    got_1 = lax.ppermute(s_o1, "tm", pair(1))
    x_m1, xs_m1, s_m1 = projected(1, 0, w_m1)
    total_1, = call(total_kernel, "total", (message,), where + vm(s_m1, got_1))
    x_o2, xs_o2, s_o2 = projected(0, 1, after(w_o2, total_1))
    got_2 = lax.ppermute(s_o2, "tm", pair(1))
    x_m2, xs_m2, s_m2 = projected(1, 1, w_m2)
    total_2, = call(total_kernel, "total", (message,), where + vm(s_m2, got_2))

    todo = [(0, 0, w_o1, x_o1, xs_o1), (1, 0, w_m1, x_m1, xs_m1), (1, 1, w_m2, x_m2, xs_m2), (0, 1, w_o2, x_o2, xs_o2)]
    done = {}
    totals, befores = [total_1, total_2], [total_1, total_2]
    gots = [lax.ppermute(total_1, "tm", pair(2)), lax.ppermute(total_2, "tm", pair(2))]
    stamp = total_2
    reach = 2
    while reach * 2 < peers:
        for i in range(2):
            if todo:
                own, group, w, x, xs = todo.pop(0)
                done[own, group] = inner(own, group, w, after(x, stamp), xs)
                gots[i] = after(gots[i], done[own, group][0])
            befores[i], totals[i] = call(functools.partial(step_kernel, reach == 2, reach), "step", (message, message),
                                         where + vm(totals[i], gots[i], befores[i]))
            stamp = totals[i]
            gots[i] = lax.ppermute(totals[i], "tm", pair(2 * reach))
        reach *= 2
    for own, group, w, x, xs in todo:
        done[own, group] = inner(own, group, w, after(x, stamp), xs)
        stamp = done[own, group][0]

    def last(i, got, mine, first):
        keep, send = call(functools.partial(last_kernel, reach), "last", (near((width, size)),) * 2,
                          where + vm(got, befores[i], mine, first))
        return keep, lax.ppermute(send, "tm", pair(1))

    keep_1, sent_1 = last(0, after(gots[0], stamp), s_m1, got_1)
    mix_1 = mixed(((1, 0),), encoded, F32, (keep_1, *done[1, 0]))
    keep_2, sent_2 = last(1, after(gots[1], mix_1), s_m2, got_2)
    mix_2 = mixed(((0, 0), (1, 1)), mix_1, F32, (sent_1, *done[0, 0]), (keep_2, *done[1, 1]))
    return mixed(((0, 1),), mix_2, BF, (sent_2, *done[0, 1])).reshape(rows, 1, depth)


def solution(mesh):
    placed = (P("tm", "space", None), P("space")) + (P(),) * 13
    return jax.shard_map(body, mesh=mesh, in_specs=placed, out_specs=P("tm", "space", None), check_vma=False)
```

time: 42.6 us -> 35.5 us (0.83)
  Pallas kernels: 31.8 us -> 26.7 us
  waiting for transfers between devices: 4.6 us -> 0.47 us
  starting transfers between devices: 5 us -> 7.1 us
    pallas_call x9 -> x17, Pallas kernels: 31.8 us -> 26.7 us  [call(): pl.pallas_call(kernel, out_shape=tuple(outs), in_specs=specs, out_specs=(...]
    ppermute x4 -> x8, waiting for transfers between devices: 4.6 us -> 0.47 us  [the longest x1 0.45 us: body(): lax.ppermute(total_1, 'tm', pair(2))]
    ppermute x4 -> x8, starting transfers between devices: 5 us -> 7.1 us  [the longest x1 2.94 us: body(): lax.ppermute(total_1, 'tm', pair(2))]
  transfers between devices with their start and end apart: 4 -> 8, of which waited for: 2 -> 1; matrix products, arithmetic and copies ran while one was open for 0% -> 0% of each run, Pallas kernels for 43% -> 45%
where the time goes in v4:
time: 35.5 us; the launch traced here: 35.2 us
  Pallas kernels  26.7 us (75%)
  starting transfers between devices  7.1 us (20%)
  between operations  0.99 us (3%)
  waiting for transfers between devices  0.47 us (1%)
    pallas_call x17, Pallas kernels, call(): pl.pallas_call(kernel, out_shape=tuple(outs), in_specs=specs, out_specs=(...  26.7 us
    ppermute x1, starting transfers between devices, body(): lax.ppermute(total_1, 'tm', pair(2))  2.94 us
    ppermute x2, starting transfers between devices, body(): gots[i] = lax.ppermute(totals[i], 'tm', pair(2 * reach))  2.81 us
  transfers between devices with their start and end apart: 8, of which 1 were waited for; matrix products, arithmetic and copies ran while one was open for 0% of the time, Pallas kernels for 45%

profile of v4, /device:TPU:0, one launch (start us, length us, event | category | flops | bytes accessed | tf_op | source)
XLA Modules:
  0.0 35.2 jit_solution(9891004419686397017)
XLA Ops:
  0.7 6.3 %encode.1 = (bf16[512,1024]{1,0:T(8,128)(2,1)S(1)}, bf16[512,1024]{1,0:T(8,128)(2,1)S(1)}, bf16[512,256]{1,0:T(8,128)(2,1)S(1)}, bf16[128,512]{1,0:T(8,128)(2,1)...) custom-call(s32[1]{0:T(128)} %bitcast.here_ref, ...), custom_call_target="tpu_custom_call" | custom-call | flops 1073741824 | bytes 4194304 | tf_op jit(solution)/shard_map/encode/pallas_call | solution.py:313
  6.9 0.5 %collective-permute-start = (bf16[144,512]{1,0:T(8,128)(2,1)S(1)}, bf16[144,512]{1,0:T(8,128)(2,1)S(1)}, u32[]{:S(2)}, u32[]{:S(2)}) collective-permute-start(bf16[144,512]{1,0:T(8,128)(2,1)S(1)} %get-tuple-element.64), channel_id=1, source_target_pairs={{0,4},{4,0},{8,12},{12,8},{16,20},{20,16},{24,28},{28,24},{1,5},{5... | collective-permute-start | bytes 442376 | tf_op jit(solution)/shard_map/ppermute | solution.py:352
  7.5 1.6 %project.3 = (bf16[512,512]{1,0:T(8,128)(2,1)S(1)}, bf16[512,512]{1,0:T(8,128)(2,1)S(1)}, bf16[144,512]{1,0:T(8,128)(2,1)S(1)}) custom-call(s32[1]{0:T(128)} %bitcast.here_ref, bf16[512,1024]{1,0:T(8,128)(2,1)S(1)} %get-tuple-element.58.normed, bf16[128,512]{1,0:T(8,128)(2,1)S(1)} %get-tuple-element.59.b_t, bf16[512,64]{1,0:T(8,128)(2,1)S(1)} %get-tuple-element.60.grow, ...), custom_call_target="tpu_custom_call" | custom-call | flops 536870912 | bytes 4194304 | tf_op jit(solution)/shard_map/project/pallas_call | solution.py:313
  9.1 0.0 collective-permute-done.got_ref.first_ref
  9.1 0.1 total.2.total_ref.before_ref
  9.2 1.6 %project.5 = (bf16[512,512]{1,0:T(8,128)(2,1)S(1)}, bf16[512,512]{1,0:T(8,128)(2,1)S(1)}, bf16[144,512]{1,0:T(8,128)(2,1)S(1)}) custom-call(s32[1]{0:T(128)} %bitcast.here_ref, bf16[512,1024]{1,0:T(8,128)(2,1)S(1)} %get-tuple-element.58.normed, bf16[128,512]{1,0:T(8,128)(2,1)S(1)} %get-tuple-element.59.b_t, bf16[512,64]{1,0:T(8,128)(2,1)S(1)} %get-tuple-element.60.grow, ...), custom_call_target="tpu_custom_call" | custom-call | flops 536870912 | bytes 4194304 | tf_op jit(solution)/shard_map/project/pallas_call | solution.py:313
  10.8 0.1 collective-permute-start.2
  11.0 2.9 %collective-permute-start.1 = (bf16[144,512]{1,0:T(8,128)(2,1)S(1)}, bf16[144,512]{1,0:T(8,128)(2,1)S(1)}, u32[]{:S(2)}, u32[]{:S(2)}) collective-permute-start(bf16[144,512]{1,0:T(8,128)(2,1)S(1)} %total.2.total_ref.before_ref), channel_id=1, source_target_pairs={{0,8},{4,12},{8,0},{12,4},{16,24},{20,28},{24,16},{28,20},{1,9},{5... | collective-permute-start | bytes 442376 | tf_op jit(solution)/shard_map/ppermute | solution.py:363
  13.9 1.6 %project.4 = (bf16[512,512]{1,0:T(8,128)(2,1)S(1)}, bf16[512,512]{1,0:T(8,128)(2,1)S(1)}, bf16[144,512]{1,0:T(8,128)(2,1)S(1)}) custom-call(s32[1]{0:T(128)} %bitcast.here_ref, bf16[512,1024]{1,0:T(8,128)(2,1)S(1)} %get-tuple-element.58.normed, bf16[128,512]{1,0:T(8,128)(2,1)S(1)} %get-tuple-element.59.b_t, bf16[512,64]{1,0:T(8,128)(2,1)S(1)} %get-tuple-element.60.grow, ...), custom_call_target="tpu_custom_call" | custom-call | flops 536870912 | bytes 4194304 | tf_op jit(solution)/shard_map/project/pallas_call | solution.py:313
  15.5 0.0 collective-permute-done.2.got_ref.first_ref
  15.6 0.1 total.3.total_ref.before_ref
  15.6 0.1 collective-permute-start.4
  15.7 2.0 %inner.4 = (bf16[512,512]{1,0:T(8,128)(2,1)S(1)}, bf16[512,512]{1,0:T(8,128)(2,1)S(1)}, bf16[512,1024]{1,0:T(8,128)(2,1)S(1)}) custom-call(s32[1]{0:T(128)} %bitcast.here_ref, bf16[512,1024]{1,0:T(8,128)(2,1)S(1)} %get-tuple-element.58.normed, bf16[512,256]{1,0:T(8,128)(2,1)S(1)} %get-tuple-element.56.keys, bf16[512,64]{1,0:T(8,128)(2,1)S(1)} %get-tuple-element.61.fall, ...), custom_call_target="tpu_custom_call" | custom-call | flops 536870912 | bytes 4194304 | tf_op jit(solution)/shard_map/inner/pallas_call | solution.py:313
  17.7 0.5 %collective-permute-done.1.got_ref = bf16[144,512]{1,0:T(8,128)(2,1)S(1)} collective-permute-done((bf16[144,512]{1,0:T(8,128)(2,1)S(1)}, bf16[144,512]{1,0:T(8,128)(2,1)S(1)}, u32[]{:S(2)}, u32[]{:S(2)}) %collective-permute-start.1) | collective-permute-done | bytes 147488 | tf_op jit(solution)/shard_map/ppermute | solution.py:363
  18.1 0.1 step.2
  18.2 1.8 %collective-permute-start.3 = (bf16[144,512]{1,0:T(8,128)(2,1)S(1)}, bf16[144,512]{1,0:T(8,128)(2,1)S(1)}, u32[]{:S(2)}, u32[]{:S(2)}) collective-permute-start(bf16[144,512]{1,0:T(8,128)(2,1)S(1)} %get-tuple-element.76), channel_id=1, source_target_pairs={{0,16},{4,20},{8,24},{12,28},{16,0},{20,4},{24,8},{28,12},{1,17},{... | collective-permute-start | bytes 442376 | tf_op jit(solution)/shard_map/ppermute | solution.py:375
  20.0 2.0 %inner.5 = (bf16[512,512]{1,0:T(8,128)(2,1)S(1)}, bf16[512,512]{1,0:T(8,128)(2,1)S(1)}, bf16[512,1024]{1,0:T(8,128)(2,1)S(1)}) custom-call(s32[1]{0:T(128)} %bitcast.here_ref, bf16[512,1024]{1,0:T(8,128)(2,1)S(1)} %get-tuple-element.58.normed, bf16[512,256]{1,0:T(8,128)(2,1)S(1)} %get-tuple-element.56.keys, bf16[512,64]{1,0:T(8,128)(2,1)S(1)} %get-tuple-element.61.fall, ...), custom_call_target="tpu_custom_call" | custom-call | flops 536870912 | bytes 4194304 | tf_op jit(solution)/shard_map/inner/pallas_call | solution.py:313
  21.9 0.0 collective-permute-done.4.got_ref
  22.0 0.3 step.3
  22.2 1.0 %collective-permute-start.6 = (bf16[144,512]{1,0:T(8,128)(2,1)S(1)}, bf16[144,512]{1,0:T(8,128)(2,1)S(1)}, u32[]{:S(2)}, u32[]{:S(2)}) collective-permute-start(bf16[144,512]{1,0:T(8,128)(2,1)S(1)} %get-tuple-element.84), channel_id=1, source_target_pairs={{0,16},{4,20},{8,24},{12,28},{16,0},{20,4},{24,8},{28,12},{1,17},{... | collective-permute-start | bytes 442376 | tf_op jit(solution)/shard_map/ppermute | solution.py:375
  23.2 1.9 %inner.6 = (bf16[512,512]{1,0:T(8,128)(2,1)S(1)}, bf16[512,512]{1,0:T(8,128)(2,1)S(1)}, bf16[512,1024]{1,0:T(8,128)(2,1)S(1)}) custom-call(s32[1]{0:T(128)} %bitcast.here_ref, bf16[512,1024]{1,0:T(8,128)(2,1)S(1)} %get-tuple-element.58.normed, bf16[512,256]{1,0:T(8,128)(2,1)S(1)} %get-tuple-element.56.keys, bf16[512,64]{1,0:T(8,128)(2,1)S(1)} %get-tuple-element.61.fall, ...), custom_call_target="tpu_custom_call" | custom-call | flops 536870912 | bytes 4194304 | tf_op jit(solution)/shard_map/inner/pallas_call | solution.py:313
  25.2 1.9 %inner.7 = (bf16[512,512]{1,0:T(8,128)(2,1)S(1)}, bf16[512,512]{1,0:T(8,128)(2,1)S(1)}, bf16[512,1024]{1,0:T(8,128)(2,1)S(1)}) custom-call(s32[1]{0:T(128)} %bitcast.here_ref, bf16[512,1024]{1,0:T(8,128)(2,1)S(1)} %get-tuple-element.58.normed, bf16[512,256]{1,0:T(8,128)(2,1)S(1)} %get-tuple-element.56.keys, bf16[512,64]{1,0:T(8,128)(2,1)S(1)} %get-tuple-element.61.fall, ...), custom_call_target="tpu_custom_call" | custom-call | flops 536870912 | bytes 4194304 | tf_op jit(solution)/shard_map/inner/pallas_call | solution.py:313
  27.2 0.0 collective-permute-done.3.got_ref
  27.2 0.1 last.2
  27.3 0.1 collective-permute-start.5
  27.4 1.6 %mix.3.base = f32[512,1024]{1,0:T(8,128)S(1)} custom-call(s32[1]{0:T(128)} %bitcast.here_ref, bf16[512,256]{1,0:T(8,128)(2,1)S(1)} %get-tuple-element.56.keys, bf16[512,1024]{1,0:T(8,128)(2,1)S(1)} %get-tuple-element.57.base, f32[1,2048]{1,0:T(1,128)} %bitcast.11, bf16[128,512]{1,0:T(8,128)(2,1)S(1)} %get-tuple-element.93.refs_0_, ...), custom_call_target="tpu_custom_call" | custom-call | flops 536870912 | bytes 4194304 | tf_op jit(solution)/shard_map/mix/pallas_call | solution.py:313
  29.0 0.0 collective-permute-done.6.got_ref
  29.0 0.1 last.3
  29.1 0.6 %collective-permute-start.7 = (bf16[128,512]{1,0:T(8,128)(2,1)S(1)}, bf16[128,512]{1,0:T(8,128)(2,1)S(1)}, u32[]{:S(2)}, u32[]{:S(2)}) collective-permute-start(bf16[128,512]{1,0:T(8,128)(2,1)S(1)} %get-tuple-element.104), channel_id=1, source_target_pairs={{0,4},{4,0},{8,12},{12,8},{16,20},{20,16},{24,28},{28,24},{1,5},{5... | collective-permute-start | bytes 393224 | tf_op jit(solution)/shard_map/ppermute | solution.py:384
  29.7 0.0 collective-permute-done.5.refs_0_
  29.7 2.7 %mix.4.base = f32[512,1024]{1,0:T(8,128)S(1)} custom-call(s32[1]{0:T(128)} %bitcast.here_ref, bf16[512,256]{1,0:T(8,128)(2,1)S(1)} %get-tuple-element.56.keys, f32[512,1024]{1,0:T(8,128)S(1)} %mix.3.base, f32[1,2048]{1,0:T(1,128)} %bitcast.12, bf16[128,512]{1,0:T(8,128)(2,1)S(1)} %collective-permute-done.5.refs_0_, ...), custom_call_target="tpu_custom_call" | custom-call | flops 1073741824 | bytes 4194304 | tf_op jit(solution)/shard_map/mix/pallas_call | solution.py:313
  32.3 0.0 collective-permute-done.7.refs_0_
  32.3 2.7 %mix.5 = bf16[512,1024]{1,0:T(8,128)(2,1)} custom-call(s32[1]{0:T(128)} %bitcast.here_ref, bf16[512,256]{1,0:T(8,128)(2,1)S(1)} %get-tuple-element.56.keys, f32[512,1024]{1,0:T(8,128)S(1)} %mix.4.base, f32[1,2048]{1,0:T(1,128)} %bitcast.13, bf16[128,512]{1,0:T(8,128)(2,1)S(1)} %collective-permute-done.7.refs_0_, ...), custom_call_target="tpu_custom_call" | custom-call | flops 536870912 | bytes 4194304 | tf_op jit(solution)/shard_map/mix/pallas_call | solution.py:313
Async XLA Ops:
  6.9 2.2 %collective-permute-start = (bf16[144,512]{1,0:T(8,128)(2,1)S(1)}, bf16[144,512]{1,0:T(8,128)(2,1)S(1)}, u32[]{:S(2)}, u32[]{:S(2)}) collective-permute-start(bf16[144,512]{1,0:T(8,128)(2,1)S(1)} %get-tuple-element.64), channel_id=1, source_target_pairs={{0,4},{4,0},{8,12},{12,8},{16,20},{20,16},{24,28},{28,24},{1,5},{5... | collective-permute-start | bytes 442376 | tf_op jit(solution)/shard_map/ppermute | solution.py:352
  10.8 4.7 %collective-permute-start.2 = (bf16[144,512]{1,0:T(8,128)(2,1)S(1)}, bf16[144,512]{1,0:T(8,128)(2,1)S(1)}, u32[]{:S(2)}, u32[]{:S(2)}) collective-permute-start(bf16[144,512]{1,0:T(8,128)(2,1)S(1)} %get-tuple-element.71), channel_id=1, source_target_pairs={{0,4},{4,0},{8,12},{12,8},{16,20},{20,16},{24,28},{28,24},{1,5},{5... | collective-permute-start | bytes 442376 | tf_op jit(solution)/shard_map/ppermute | solution.py:356
  11.0 7.2 %collective-permute-start.1 = (bf16[144,512]{1,0:T(8,128)(2,1)S(1)}, bf16[144,512]{1,0:T(8,128)(2,1)S(1)}, u32[]{:S(2)}, u32[]{:S(2)}) collective-permute-start(bf16[144,512]{1,0:T(8,128)(2,1)S(1)} %total.2.total_ref.before_ref), channel_id=1, source_target_pairs={{0,8},{4,12},{8,0},{12,4},{16,24},{20,28},{24,16},{28,20},{1,9},{5... | collective-permute-start | bytes 442376 | tf_op jit(solution)/shard_map/ppermute | solution.py:363
  15.6 6.3 %collective-permute-start.4 = (bf16[144,512]{1,0:T(8,128)(2,1)S(1)}, bf16[144,512]{1,0:T(8,128)(2,1)S(1)}, u32[]{:S(2)}, u32[]{:S(2)}) collective-permute-start(bf16[144,512]{1,0:T(8,128)(2,1)S(1)} %total.3.total_ref.before_ref), channel_id=1, source_target_pairs={{0,8},{4,12},{8,0},{12,4},{16,24},{20,28},{24,16},{28,20},{1,9},{5... | collective-permute-start | bytes 442376 | tf_op jit(solution)/shard_map/ppermute | solution.py:363
  18.2 9.0 %collective-permute-start.3 = (bf16[144,512]{1,0:T(8,128)(2,1)S(1)}, bf16[144,512]{1,0:T(8,128)(2,1)S(1)}, u32[]{:S(2)}, u32[]{:S(2)}) collective-permute-start(bf16[144,512]{1,0:T(8,128)(2,1)S(1)} %get-tuple-element.76), channel_id=1, source_target_pairs={{0,16},{4,20},{8,24},{12,28},{16,0},{20,4},{24,8},{28,12},{1,17},{... | collective-permute-start | bytes 442376 | tf_op jit(solution)/shard_map/ppermute | solution.py:375
  22.2 6.8 %collective-permute-start.6 = (bf16[144,512]{1,0:T(8,128)(2,1)S(1)}, bf16[144,512]{1,0:T(8,128)(2,1)S(1)}, u32[]{:S(2)}, u32[]{:S(2)}) collective-permute-start(bf16[144,512]{1,0:T(8,128)(2,1)S(1)} %get-tuple-element.84), channel_id=1, source_target_pairs={{0,16},{4,20},{8,24},{12,28},{16,0},{20,4},{24,8},{28,12},{1,17},{... | collective-permute-start | bytes 442376 | tf_op jit(solution)/shard_map/ppermute | solution.py:375
  27.3 2.4 %collective-permute-start.5 = (bf16[128,512]{1,0:T(8,128)(2,1)S(1)}, bf16[128,512]{1,0:T(8,128)(2,1)S(1)}, u32[]{:S(2)}, u32[]{:S(2)}) collective-permute-start(bf16[128,512]{1,0:T(8,128)(2,1)S(1)} %get-tuple-element.96), channel_id=1, source_target_pairs={{0,4},{4,0},{8,12},{12,8},{16,20},{20,16},{24,28},{28,24},{1,5},{5... | collective-permute-start | bytes 393224 | tf_op jit(solution)/shard_map/ppermute | solution.py:384
  29.1 3.2 %collective-permute-start.7 = (bf16[128,512]{1,0:T(8,128)(2,1)S(1)}, bf16[128,512]{1,0:T(8,128)(2,1)S(1)}, u32[]{:S(2)}, u32[]{:S(2)}) collective-permute-start(bf16[128,512]{1,0:T(8,128)(2,1)S(1)} %get-tuple-element.104), channel_id=1, source_target_pairs={{0,4},{4,0},{8,12},{12,8},{16,20},{20,16},{24,28},{28,24},{1,5},{5... | collective-permute-start | bytes 393224 | tf_op jit(solution)/shard_map/ppermute | solution.py:384

commit v5 on v4

--- a/solution.py
+++ b/solution.py
@@ -68,6 +68,7 @@
     width = b_t.shape[0]
     size = x_ref.shape[1]
     first = (half * 2 + group) * (size // head_dim)
+    later = []
     for j in range(size // CHUNK):
         cols = slice(j * CHUNK, (j + 1) * CHUNK)
         spread = spread_heads(first + j * (CHUNK // head_dim), heads, head_dim)
@@ -76,8 +77,10 @@
         x_ref[:, cols] = x
         xs_ref[:, cols] = scaled
         decay = dot(fall_end, spread)[EXTRA - 1:EXTRA]
+        s_ref[width:width + EXTRA, cols] = decay_rows(decay)
+        later.append((cols, scaled, decay))
+    for cols, scaled, decay in later:
         s_ref[0:width, cols] = (dot(b_t, scaled) * decay).astype(BF)
-        s_ref[width:width + EXTRA, cols] = decay_rows(decay)
 
 
 def decay_rows(decay):
@@ -86,67 +89,114 @@
     return jnp.where(row == 0, high, jnp.where(row == 1, decay - high, 0.0)).astype(BF)
 
 
-def start_all(pairs, sem):
-    copies = [pltpu.make_async_copy(src, dst, sem.at[i]) for i, (src, dst) in enumerate(pairs)]
-    for c in copies:
-        c.start()
-    return copies
+def in_pieces(src, dst, sem, slot):
+    block = dst.shape[0] // 2
+
+    def piece(i):
+        part = pl.ds(pl.multiple_of(i * block, block), block)
+        return pltpu.make_async_copy(src.at[part, :], dst.at[part, :], sem.at[slot, i])
+
+    return piece
+
+
+def start_pieces(pieces):
+    def go(i, carry):
+        for piece in pieces:
+            piece(i).start()
+        return carry
+
+    lax.fori_loop(0, 2, go, 0)
+
+
+def wait_pieces(pieces):
+    def go(i, carry):
+        for piece in pieces:
+            piece(i).wait()
+        return carry
+
+    lax.fori_loop(0, 2, go, 0)
 
 
 def encode_kernel(heads, head_dim, here_ref, cell_ref, frames_any, enc_in_any, bias_any, enc_out_any, pos_any, gain_any,
-                  w_keys_any, w_step_any, step_bias_any, code_any, w_pair_any,
-                  encoded, normed, keys, b_t, grow, fall, x_ref, xs_ref, s_ref, w_o1, w_o2, w_m1, w_m2,
+                  w_keys_any, w_step_any, step_bias_any, code_any, skip_any, out_gain_any, w_pair_any,
+                  encoded, normed, keys, b_t, grow, fall, skip, out_gain, x_ref, xs_ref, s_ref, w_o1, w_m1, w_o2, w_m2,
                   frames, enc_in, bias, enc_out, pos, norm_gain, w_keys, w_step, step_bias, code, sem, wsem):
     half = 1 - here_ref[0] % 2
     cell = cell_ref[0]
     base = pl.multiple_of((cell // EXTRA) * EXTRA, EXTRA)
-    small = start_all([(frames_any, frames), (enc_in_any, enc_in), (bias_any, bias), (enc_out_any, enc_out),
-                       (pos_any.at[pl.ds(base, EXTRA), :], pos), (gain_any, norm_gain), (w_keys_any, w_keys),
-                       (w_step_any, w_step), (step_bias_any, step_bias), (code_any, code)], sem)
-    size = w_o1.shape[1]
-    columns = lambda which, group: w_pair_any.at[:, pl.ds(pl.multiple_of((which * 2 + group) * size, size), size)]
+    small = [pltpu.make_async_copy(src, dst, sem.at[i]) for i, (src, dst) in enumerate((
+        (bias_any, bias), (pos_any.at[pl.ds(base, EXTRA), :], pos), (gain_any, norm_gain), (step_bias_any, step_bias),
+        (code_any, code), (skip_any, skip), (out_gain_any, out_gain)))]
+    first = [in_pieces(src, dst, wsem, i) for i, (src, dst) in enumerate((
+        (frames_any, frames), (enc_in_any, enc_in), (enc_out_any, enc_out), (w_keys_any, w_keys), (w_step_any, w_step)))]
+    big = [in_pieces(group_columns(w_pair_any, dst, which, group), dst, wsem, 5 + i) for i, (which, group, dst) in enumerate((
+        (half, 0, w_o1), (1 - half, 0, w_m1), (half, 1, w_o2), (1 - half, 1, w_m2)))]
+    start_pieces(first[:2])
+    for c in small:
+        c.start()
+    start_pieces(first[2:])
     rows, depth = encoded.shape
+    block = rows // 2
     lower = (iota((rows, rows), 0) >= iota((rows, rows), 1)).astype(F32).astype(BF)
-    for c in small[:3]:
+    small[0].wait()
+    wait_pieces(first[:2])
+    start_pieces(big)
+    twice = lambda v: jnp.concatenate([v, v], axis=1)
+    columns = [slice(j, j + CHUNK) for j in range(0, depth, CHUNK)]
+
+    def hide(part):
+        pieces = []
+        for cols in columns:
+            h = dot(frames[part, :], enc_in[:, cols]) + bias[:, cols]
+            pieces.append(jax.nn.gelu(h, approximate=True).astype(BF))
+        return jnp.concatenate(pieces, axis=1)
+
+    def encode(part, hidden, row):
+        square = jnp.zeros((block, 1), F32)
+        for cols in columns:
+            e = (dot(hidden, enc_out[:, cols]) + row[:, cols]).astype(BF)
+            encoded[part, cols] = e
+            e = e.astype(F32)
+            square += jnp.sum(e * e, axis=1, keepdims=True)
+        inv = lax.rsqrt(square / depth + 1e-05)
+        pieces = []
+        for cols in columns:
+            piece = (encoded[part, cols].astype(F32) * inv * norm_gain[:, cols]).astype(BF)
+            normed[part, cols] = piece
+            pieces.append(piece)
+        return jnp.concatenate(pieces, axis=1)
+
+    def read_out(part, wide):
+        k = dot(wide, w_keys[...]).astype(BF)
+        keys[part, :] = k
+        b_t[:, part] = k[:, :k.shape[1] // 2].T
+        ws = w_step[...]
+        raw = dot_t(wide, jnp.concatenate([ws, ws], axis=0)) + twice(step_bias[...])
+        return jax.nn.sigmoid(raw).astype(BF)
+
+    top, low = slice(0, block), slice(block, rows)
+    hidden_top = hide(top)
+    hidden_low = hide(low)
+    for c in small[1:]:
         c.wait()
-    big = start_all([(columns(half, 0), w_o1), (columns(1 - half, 0), w_m1), (columns(half, 1), w_o2),
-                     (columns(1 - half, 1), w_m2)], wsem)
-    hidden = []
-    for j in range(depth // CHUNK):
-        cols = slice(j * CHUNK, (j + 1) * CHUNK)
-        h = dot(frames[...], enc_in[:, cols]) + bias[:, cols]
-        hidden.append(jax.nn.gelu(h, approximate=True).astype(BF))
-    hidden = jnp.concatenate(hidden, axis=1)
-    for c in small[3:]:
-        c.wait()
+    wait_pieces(first[2:])
     row = jnp.sum(jnp.where(iota(pos.shape, 0) == cell - base, pos[...].astype(F32), 0.0), axis=0, keepdims=True)
-    square = jnp.zeros((rows, 1), F32)
-    for j in range(depth // CHUNK):
-        cols = slice(j * CHUNK, (j + 1) * CHUNK)
-        e = (dot(hidden, enc_out[:, cols]) + row[:, cols]).astype(BF)
-        encoded[:, cols] = e
-        e = e.astype(F32)
-        square += jnp.sum(e * e, axis=1, keepdims=True)
-    inv = lax.rsqrt(square / depth + 1e-05)
-    for j in range(depth // CHUNK):
-        cols = slice(j * CHUNK, (j + 1) * CHUNK)
-        normed[:, cols] = (encoded[:, cols].astype(F32) * inv * norm_gain[:, cols]).astype(BF)
-    k = dot(normed[...], w_keys[...]).astype(BF)
-    keys[...] = k
-    b_t[...] = k[:, :k.shape[1] // 2].T
-    ws = w_step[...]
-    twice = lambda v: jnp.concatenate([v, v], axis=1)
-    raw = dot_t(normed[...], jnp.concatenate([ws, ws], axis=0)) + twice(step_bias[...])
-    step = jax.nn.sigmoid(raw).astype(BF)
+    wide_top = encode(top, hidden_top, row)
+    wide_low = encode(low, hidden_low, row)
+    step = jnp.concatenate([read_out(top, wide_top), read_out(low, wide_low)], axis=0)
     cum = dot(lower, step) * twice(-0.0005 - 0.003 * code[...].astype(F32))
     g = split_two(jnp.exp(-cum), heads)
     f = split_two(jnp.exp(cum), heads)
     grow[...] = g
     fall[...] = f
-    big[0].wait()
+    wait_pieces(big[:1])
     project(half, 0, heads, head_dim, w_o1, normed, b_t[...], g, f[rows - EXTRA:], x_ref, xs_ref, s_ref)
-    for c in big[1:]:
-        c.wait()
+    wait_pieces(big[1:])
+
+
+def group_columns(w_any, like, half, group):
+    size = like.shape[1]
+    return w_any.at[:, pl.ds(pl.multiple_of((half * 2 + group) * size, size), size)]
 
 
 def project_kernel(heads, head_dim, own, group, here_ref, normed, b_t, grow, fall, w, x_ref, xs_ref, s_ref):
@@ -223,18 +273,23 @@
         keep_ref[...] = before.astype(BF)
 
 
-def inner_kernel(heads, head_dim, own, group, here_ref, normed, keys, fall, skip_any, w_out_any, w, x, xs,
-                 u, v, w_rows, skip, sem):
+def inner_kernel(heads, head_dim, own, group, fresh, here_ref, normed, keys, fall, skip, w_out_any, w, x, xs, *refs):
     half = (here_ref[0] + 1 - own) % 2
     rows = keys.shape[0]
     width = keys.shape[1] // 2
     size = x.shape[1]
+    if fresh:
+        u, v, w_rows, scores_ref, sem = refs
+    else:
+        scores_ref, u, v, w_rows, sem = refs
     start = pl.multiple_of((half * 2 + group) * size, size)
-    copies = start_all([(skip_any, skip), (w_out_any.at[pl.ds(start, size), :], w_rows)], sem)
-    scores = dot_t(keys[:, width:], keys[:, :width])
-    scores = jnp.where(iota((rows, rows), 0) >= iota((rows, rows), 1), scores, 0.0).astype(BF)
+    copies = [in_pieces(w_out_any.at[pl.ds(start, size), :], w_rows, sem, 0)]
+    start_pieces(copies)
+    if fresh:
+        scores = dot_t(keys[:, width:], keys[:, :width])
+        scores_ref[...] = jnp.where(iota((rows, rows), 0) >= iota((rows, rows), 1), scores, 0.0).astype(BF)
+    scores = scores_ref[...]
     mid = rows // 2
-    copies[0].wait()
     both = jnp.broadcast_to(jnp.concatenate([skip[...], skip[...]], axis=1), (EXTRA, 2 * heads))
     skip_two = split_two(both, heads)
     first = (half * 2 + group) * (size // head_dim)
@@ -250,18 +305,16 @@
         low = dot(scores[mid:], xs[:, cols])
         for part, inner in ((slice(0, mid), top), (slice(mid, rows), low)):
             v[part, cols] = ((grown[part] * inner + gain * x[part, cols].astype(F32)) * gate[part]).astype(BF)
-    copies[1].wait()
-
-
-def mix_kernel(head_dim, places, here_ref, keys, base, gain_any, *refs):
+    wait_pieces(copies)
+
+
+def mix_kernel(head_dim, places, last, here_ref, keys, base, gain, *refs):
     many = len(places)
     states, us, vs, ws = (refs[i * many:(i + 1) * many] for i in range(4))
-    out, gain_ref, sem = refs[4 * many:]
+    out = refs[4 * many]
     width = keys.shape[1] // 2
     size = us[0].shape[1]
     starts = [((here_ref[0] + 1 - own) % 2 * 2 + group) * size for own, group in places]
-    copies = start_all([(gain_any.at[:, pl.ds(pl.multiple_of(s, size), size)], gain_ref.at[pl.ds(i, 1), :])
-                        for i, s in enumerate(starts)], sem)
     same = (iota((CHUNK, CHUNK), 0) // head_dim) == (iota((CHUNK, CHUNK), 1) // head_dim)
     mean = jnp.where(same, 1.0 / head_dim, 0.0).astype(BF)
     work = []
@@ -271,22 +324,29 @@
             carried = dot(keys[:, width:], state[:, cols])
             g = v[:, cols].astype(F32) + u[:, cols].astype(F32) * carried
             work.append((g, dot((g * g).astype(BF), mean)))
-    for c in copies:
-        c.wait()
     mixed = []
     for i in range(many):
-        row = gain_ref[i:i + 1, :]
         parts = []
         for j in range(size // CHUNK):
             g, m = work[i * (size // CHUNK) + j]
-            parts.append((g * lax.rsqrt(m + 1e-05) * row[:, j * CHUNK:(j + 1) * CHUNK]).astype(BF))
+            row = gain[:, pl.ds(pl.multiple_of(starts[i] + j * CHUNK, CHUNK), CHUNK)]
+            parts.append((g * lax.rsqrt(m + 1e-05) * row).astype(BF))
         mixed.append(jnp.concatenate(parts, axis=1))
-    for n in range(out.shape[1] // CHUNK):
+    copies = []
+    for n in range(base.shape[1] // CHUNK):
         cols = slice(n * CHUNK, (n + 1) * CHUNK)
         total = base[:, cols].astype(F32)
         for part, w in zip(mixed, ws):
             total = total + dot(part, w[:, cols])
-        out[:, cols] = total.astype(out.dtype)
+        if last:
+            buf, sem = refs[4 * many + 1:]
+            buf[:, cols] = total.astype(buf.dtype)
+            copies.append(pltpu.make_async_copy(buf.at[:, cols], out.at[:, cols], sem.at[n]))
+            copies[-1].start()
+        else:
+            out[:, cols] = total.astype(out.dtype)
+    for c in copies:
+        c.wait()
 
 
 def body(frames, patch_cell, enc_in, enc_bias, enc_out, pos_table, norm_gain, w_pair, w_keys, w_step,
@@ -307,10 +367,10 @@
     pair = lambda by: [(i, i ^ by) for i in range(peers)]
     after = lambda value, *first: lax.optimization_barrier((value,) + first)[0]
 
-    def call(kernel, name, outs, ins, scratch=(), macs=0):
+    def call(kernel, name, outs, ins, scratch=(), macs=0, out_spec=VM):
         specs = [spec for spec, _ in ins]
-        cost = pl.CostEstimate(flops=2 * macs, bytes_accessed=4 * 2**20, transcendentals=0)
-        return pl.pallas_call(kernel, out_shape=tuple(outs), in_specs=specs, out_specs=(VM,) * len(outs),
+        cost = pl.CostEstimate(flops=macs // 4, bytes_accessed=2**20, transcendentals=0)
+        return pl.pallas_call(kernel, out_shape=tuple(outs), in_specs=specs, out_specs=(out_spec,) * len(outs),
                               scratch_shapes=list(scratch), compiler_params=params(24), name=name,
                               cost_estimate=cost)(*[v for _, v in ins])
 
@@ -319,36 +379,41 @@
     where = [(SM, here)]
 
     part, message, weight = near((rows, size)), near((width + EXTRA, size)), near((depth, 2 * size))
-    encoded, normed, keys, b_t, grow, fall, x_o1, xs_o1, s_o1, w_o1, w_o2, w_m1, w_m2 = call(
+    encoded, normed, keys, b_t, grow, fall, skip, gain, x_o1, xs_o1, s_o1, w_o1, w_m1, w_o2, w_m2 = call(
         functools.partial(encode_kernel, heads, head_dim), "encode",
         (near((rows, depth)), near((rows, depth)), near((rows, 2 * width)), near((width, rows)),
-         near((rows, 2 * heads)), near((rows, 2 * heads)), part, part, message) + (weight,) * 4,
+         near((rows, 2 * heads)), near((rows, 2 * heads)), near((1, heads), F32), near((1, heads * head_dim), F32),
+         part, part, message) + (weight,) * 4,
         where + [(SM, patch_cell)] + hbm(frames.reshape(rows, pix), enc_in, row(enc_bias), enc_out, pos_table, row(norm_gain),
-                                         w_keys, w_step.T, row(step_bias), row(decay_code), w_pair),
+                                         w_keys, w_step.T, row(step_bias), row(decay_code), row(skip_gain), row(out_gain),
+                                         w_pair),
         [near((rows, pix)), near((pix, depth)), near((1, depth), F32), near((depth, depth)), near((EXTRA, depth)),
          near((1, depth), F32), near((depth, 2 * width)), near((heads, depth)), near((1, heads), F32),
-         near((1, heads), jnp.int32), sems(10), sems(4)],
+         near((1, heads), jnp.int32), sems(7), pltpu.SemaphoreType.DMA((9, 2))],
         rows * depth * depth)
 
     def projected(own, group, w):
-        return call(functools.partial(project_kernel, heads, head_dim, own, group), "project", (part, part, message),
-                    where + vm(normed, b_t, grow, fall, w), (), rows * depth * size)
+        return call(functools.partial(project_kernel, heads, head_dim, own, group), "project",
+                    (part, part, message), where + vm(normed, b_t, grow, fall, w), (), rows * depth * size)
+
+    scores = []
 
     def inner(own, group, w, x, xs):
-        return call(functools.partial(inner_kernel, heads, head_dim, own, group), "inner",
-                    (part, part, near((size, depth))),
-                    where + vm(normed, keys, fall) + hbm(skip_row, w_out) + vm(w, x, xs),
-                    [near((1, heads), F32), sems(2)], rows * depth * size)
-
-    def mixed(places, base, kind, *groups):
+        outs = call(functools.partial(inner_kernel, heads, head_dim, own, group, not scores), "inner",
+                    (part, part, near((size, depth))) + (() if scores else (near((rows, rows)),)),
+                    where + vm(normed, keys, fall, skip) + hbm(w_out) + vm(w, x, xs, *scores),
+                    [pltpu.SemaphoreType.DMA((1, 2))], rows * depth * size)
+        scores.extend(outs[3:])
+        return outs[:3]
+
+    def mixed(places, base, last, *groups):
         states, us, vs, ws = zip(*groups)
-        last = kind == BF
-        return call(functools.partial(mix_kernel, head_dim, places), "mix",
-                    (sds((rows, depth), kind) if last else near((rows, depth), kind),),
-                    where + vm(keys, base) + hbm(gain_row) + vm(*states, *us, *vs, *ws),
-                    [near((len(places), size), F32), sems(len(places))], len(places) * rows * depth * size)[0]
-
-    skip_row, gain_row = row(skip_gain), row(out_gain)
+        shape = sds((rows, depth), BF) if last else near((rows, depth), F32)
+        return call(functools.partial(mix_kernel, head_dim, places, last), "mix", (shape,),
+                    where + vm(keys, base, gain, *states, *us, *vs, *ws),
+                    [near((rows, depth)), sems(depth // CHUNK)] if last else [], len(places) * rows * depth * size,
+                    ANY if last else VM)[0]
+
     got_1 = lax.ppermute(s_o1, "tm", pair(1))
     x_m1, xs_m1, s_m1 = projected(1, 0, w_m1)
     total_1, = call(total_kernel, "total", (message,), where + vm(s_m1, got_1))
@@ -384,10 +449,10 @@
         return keep, lax.ppermute(send, "tm", pair(1))
 
     keep_1, sent_1 = last(0, after(gots[0], stamp), s_m1, got_1)
-    mix_1 = mixed(((1, 0),), encoded, F32, (keep_1, *done[1, 0]))
+    mix_1 = mixed(((1, 0),), encoded, False, (keep_1, *done[1, 0]))
     keep_2, sent_2 = last(1, after(gots[1], mix_1), s_m2, got_2)
-    mix_2 = mixed(((0, 0), (1, 1)), mix_1, F32, (sent_1, *done[0, 0]), (keep_2, *done[1, 1]))
-    return mixed(((0, 1),), mix_2, BF, (sent_2, *done[0, 1])).reshape(rows, 1, depth)
+    mix_2 = mixed(((0, 0), (1, 1)), mix_1, False, (sent_1, *done[0, 0]), (keep_2, *done[1, 1]))
+    return mixed(((0, 1),), mix_2, True, (sent_2, *done[0, 1])).reshape(rows, 1, depth)
 
 
 def solution(mesh):

time: 35.5 us -> 30.4 us (0.86)
  Pallas kernels: 26.7 us -> 19.5 us
  waiting for transfers between devices: 0.47 us -> 2.28 us
  starting transfers between devices: 7.1 us -> 7.46 us
    pallas_call x17, Pallas kernels: 26.7 us -> 19.5 us  [call(): pl.pallas_call(kernel, out_shape=tuple(outs), in_specs=specs, out_specs=(...]
    ppermute x1, waiting for transfers between devices: 0.45 us -> 2.01 us  [body(): lax.ppermute(total_1, 'tm', pair(2))]
    ppermute x2, starting transfers between devices: 2.81 us -> 3.37 us  [body(): gots[i] = lax.ppermute(totals[i], 'tm', pair(2 * reach))]
  transfers between devices with their start and end apart: 8 -> 8, of which waited for: 1 -> 2; matrix products, arithmetic and copies ran while one was open for 0% -> 0% of each run, Pallas kernels for 45% -> 36%
where the time goes in v5:
time: 30.4 us; the launch traced here: 30.2 us
  Pallas kernels  19.5 us (64%)
  starting transfers between devices  7.46 us (25%)
  waiting for transfers between devices  2.28 us (7%)
  between operations  0.96 us (3%)
    pallas_call x17, Pallas kernels, call(): pl.pallas_call(kernel, out_shape=tuple(outs), in_specs=specs, out_specs=(...  19.5 us
    ppermute x2, starting transfers between devices, body(): gots[i] = lax.ppermute(totals[i], 'tm', pair(2 * reach))  3.37 us
    ppermute x1, starting transfers between devices, body(): lax.ppermute(total_1, 'tm', pair(2))  2.71 us
    ppermute x1, waiting for transfers between devices, body(): lax.ppermute(total_1, 'tm', pair(2))  2.01 us
  transfers between devices with their start and end apart: 8, of which 2 were waited for; matrix products, arithmetic and copies ran while one was open for 0% of the time, Pallas kernels for 36%

profile of v5, /device:TPU:0, one launch (start us, length us, event | category | flops | bytes accessed | tf_op | source)
XLA Modules:
  0.0 30.2 jit_solution(4774934227278154573)
XLA Ops:
  0.7 5.7 %encode.1 = (bf16[512,1024]{1,0:T(8,128)(2,1)S(1)}, bf16[512,1024]{1,0:T(8,128)(2,1)S(1)}, bf16[512,256]{1,0:T(8,128)(2,1)S(1)}, bf16[128,512]{1,0:T(8,128)(2,1)...) custom-call(s32[1]{0:T(128)} %bitcast.here_ref, ...), custom_call_target="tpu_custom_call" | custom-call | flops 134217728 | bytes 1048576 | tf_op jit(solution)/shard_map/encode/pallas_call | solution.py:373
  6.3 0.5 %collective-permute-start = (bf16[144,512]{1,0:T(8,128)(2,1)S(1)}, bf16[144,512]{1,0:T(8,128)(2,1)S(1)}, u32[]{:S(2)}, u32[]{:S(2)}) collective-permute-start(bf16[144,512]{1,0:T(8,128)(2,1)S(1)} %get-tuple-element.68), channel_id=1, source_target_pairs={{0,4},{4,0},{8,12},{12,8},{16,20},{20,16},{24,28},{28,24},{1,5},{5... | collective-permute-start | bytes 442376 | tf_op jit(solution)/shard_map/ppermute | solution.py:417
  6.8 1.1 %project.3 = (bf16[512,512]{1,0:T(8,128)(2,1)S(1)}, bf16[512,512]{1,0:T(8,128)(2,1)S(1)}, bf16[144,512]{1,0:T(8,128)(2,1)S(1)}) custom-call(s32[1]{0:T(128)} %bitcast.here_ref, bf16[512,1024]{1,0:T(8,128)(2,1)S(1)} %get-tuple-element.62.normed, bf16[128,512]{1,0:T(8,128)(2,1)S(1)} %get-tuple-element.63.b_t, bf16[512,64]{1,0:T(8,128)(2,1)S(1)} %get-tuple-element.64.grow, ...), custom_call_target="tpu_custom_call" | custom-call | flops 67108864 | bytes 1048576 | tf_op jit(solution)/shard_map/project/pallas_call | solution.py:373
  7.9 0.0 collective-permute-done.got_ref.first_ref
  7.9 0.1 total.2.total_ref.before_ref
  8.0 1.1 %project.5 = (bf16[512,512]{1,0:T(8,128)(2,1)S(1)}, bf16[512,512]{1,0:T(8,128)(2,1)S(1)}, bf16[144,512]{1,0:T(8,128)(2,1)S(1)}) custom-call(s32[1]{0:T(128)} %bitcast.here_ref, bf16[512,1024]{1,0:T(8,128)(2,1)S(1)} %get-tuple-element.62.normed, bf16[128,512]{1,0:T(8,128)(2,1)S(1)} %get-tuple-element.63.b_t, bf16[512,64]{1,0:T(8,128)(2,1)S(1)} %get-tuple-element.64.grow, ...), custom_call_target="tpu_custom_call" | custom-call | flops 67108864 | bytes 1048576 | tf_op jit(solution)/shard_map/project/pallas_call | solution.py:373
  9.1 0.4 %collective-permute-start.2 = (bf16[144,512]{1,0:T(8,128)(2,1)S(1)}, bf16[144,512]{1,0:T(8,128)(2,1)S(1)}, u32[]{:S(2)}, u32[]{:S(2)}) collective-permute-start(bf16[144,512]{1,0:T(8,128)(2,1)S(1)} %get-tuple-element.76), channel_id=1, source_target_pairs={{0,4},{4,0},{8,12},{12,8},{16,20},{20,16},{24,28},{28,24},{1,5},{5... | collective-permute-start | bytes 442376 | tf_op jit(solution)/shard_map/ppermute | solution.py:421
  9.4 2.7 %collective-permute-start.1 = (bf16[144,512]{1,0:T(8,128)(2,1)S(1)}, bf16[144,512]{1,0:T(8,128)(2,1)S(1)}, u32[]{:S(2)}, u32[]{:S(2)}) collective-permute-start(bf16[144,512]{1,0:T(8,128)(2,1)S(1)} %total.2.total_ref.before_ref), channel_id=1, source_target_pairs={{0,8},{4,12},{8,0},{12,4},{16,24},{20,28},{24,16},{28,20},{1,9},{5... | collective-permute-start | bytes 442376 | tf_op jit(solution)/shard_map/ppermute | solution.py:428
  12.1 1.1 %project.4 = (bf16[512,512]{1,0:T(8,128)(2,1)S(1)}, bf16[512,512]{1,0:T(8,128)(2,1)S(1)}, bf16[144,512]{1,0:T(8,128)(2,1)S(1)}) custom-call(s32[1]{0:T(128)} %bitcast.here_ref, bf16[512,1024]{1,0:T(8,128)(2,1)S(1)} %get-tuple-element.62.normed, bf16[128,512]{1,0:T(8,128)(2,1)S(1)} %get-tuple-element.63.b_t, bf16[512,64]{1,0:T(8,128)(2,1)S(1)} %get-tuple-element.64.grow, ...), custom_call_target="tpu_custom_call" | custom-call | flops 67108864 | bytes 1048576 | tf_op jit(solution)/shard_map/project/pallas_call | solution.py:373
  13.2 0.0 collective-permute-done.2.got_ref.first_ref
  13.2 0.1 total.3.total_ref.before_ref
  13.3 0.1 collective-permute-start.4
  13.4 1.3 %inner.4 = (bf16[512,512]{1,0:T(8,128)(2,1)S(1)}, bf16[512,512]{1,0:T(8,128)(2,1)S(1)}, bf16[512,1024]{1,0:T(8,128)(2,1)S(1)}, bf16[512,512]{1,0:T(8,128)(2,1)S(1)}) custom-call(s32[1]{0:T(128)} %bitcast.here_ref, bf16[512,1024]{1,0:T(8,128)(2,1)S(1)} %get-tuple-element.62.normed, bf16[512,256]{1,0:T(8,128)(2,1)S(1)} %get-tuple-element.59.keys, ...), custom_call_target="tpu_custom_call" | custom-call | flops 67108864 | bytes 1048576 | tf_op jit(solution)/shard_map/inner/pallas_call | solution.py:373
  14.7 2.0 %collective-permute-done.1.got_ref = bf16[144,512]{1,0:T(8,128)(2,1)S(1)} collective-permute-done((bf16[144,512]{1,0:T(8,128)(2,1)S(1)}, bf16[144,512]{1,0:T(8,128)(2,1)S(1)}, u32[]{:S(2)}, u32[]{:S(2)}) %collective-permute-start.1) | collective-permute-done | bytes 147488 | tf_op jit(solution)/shard_map/ppermute | solution.py:428
  16.7 0.1 step.2
  16.8 2.2 %collective-permute-start.3 = (bf16[144,512]{1,0:T(8,128)(2,1)S(1)}, bf16[144,512]{1,0:T(8,128)(2,1)S(1)}, u32[]{:S(2)}, u32[]{:S(2)}) collective-permute-start(bf16[144,512]{1,0:T(8,128)(2,1)S(1)} %get-tuple-element.81), channel_id=1, source_target_pairs={{0,16},{4,20},{8,24},{12,28},{16,0},{20,4},{24,8},{28,12},{1,17},{... | collective-permute-start | bytes 442376 | tf_op jit(solution)/shard_map/ppermute | solution.py:440
  19.0 1.2 %inner.5 = (bf16[512,512]{1,0:T(8,128)(2,1)S(1)}, bf16[512,512]{1,0:T(8,128)(2,1)S(1)}, bf16[512,1024]{1,0:T(8,128)(2,1)S(1)}) custom-call(s32[1]{0:T(128)} %bitcast.here_ref, bf16[512,1024]{1,0:T(8,128)(2,1)S(1)} %get-tuple-element.62.normed, bf16[512,256]{1,0:T(8,128)(2,1)S(1)} %get-tuple-element.59.keys, bf16[512,64]{1,0:T(8,128)(2,1)S(1)} %get-tuple-element.65.fall, ...), custom_call_target="tpu_custom_call" | custom-call | flops 67108864 | bytes 1048576 | tf_op jit(solution)/shard_map/inner/pallas_call | solution.py:373
  20.2 0.0 collective-permute-done.4.got_ref
  20.2 0.3 step.3
  20.5 1.2 %collective-permute-start.6 = (bf16[144,512]{1,0:T(8,128)(2,1)S(1)}, bf16[144,512]{1,0:T(8,128)(2,1)S(1)}, u32[]{:S(2)}, u32[]{:S(2)}) collective-permute-start(bf16[144,512]{1,0:T(8,128)(2,1)S(1)} %get-tuple-element.90), channel_id=1, source_target_pairs={{0,16},{4,20},{8,24},{12,28},{16,0},{20,4},{24,8},{28,12},{1,17},{... | collective-permute-start | bytes 442376 | tf_op jit(solution)/shard_map/ppermute | solution.py:440
  21.7 1.2 %inner.6 = (bf16[512,512]{1,0:T(8,128)(2,1)S(1)}, bf16[512,512]{1,0:T(8,128)(2,1)S(1)}, bf16[512,1024]{1,0:T(8,128)(2,1)S(1)}) custom-call(s32[1]{0:T(128)} %bitcast.here_ref, bf16[512,1024]{1,0:T(8,128)(2,1)S(1)} %get-tuple-element.62.normed, bf16[512,256]{1,0:T(8,128)(2,1)S(1)} %get-tuple-element.59.keys, bf16[512,64]{1,0:T(8,128)(2,1)S(1)} %get-tuple-element.65.fall, ...), custom_call_target="tpu_custom_call" | custom-call | flops 67108864 | bytes 1048576 | tf_op jit(solution)/shard_map/inner/pallas_call | solution.py:373
  22.9 1.2 %inner.7 = (bf16[512,512]{1,0:T(8,128)(2,1)S(1)}, bf16[512,512]{1,0:T(8,128)(2,1)S(1)}, bf16[512,1024]{1,0:T(8,128)(2,1)S(1)}) custom-call(s32[1]{0:T(128)} %bitcast.here_ref, bf16[512,1024]{1,0:T(8,128)(2,1)S(1)} %get-tuple-element.62.normed, bf16[512,256]{1,0:T(8,128)(2,1)S(1)} %get-tuple-element.59.keys, bf16[512,64]{1,0:T(8,128)(2,1)S(1)} %get-tuple-element.65.fall, ...), custom_call_target="tpu_custom_call" | custom-call | flops 67108864 | bytes 1048576 | tf_op jit(solution)/shard_map/inner/pallas_call | solution.py:373
  24.1 0.0 collective-permute-done.3.got_ref
  24.2 0.1 last.2
  24.3 0.1 collective-permute-start.5
  24.4 1.1 %mix.3.base = f32[512,1024]{1,0:T(8,128)S(1)} custom-call(s32[1]{0:T(128)} %bitcast.here_ref, bf16[512,256]{1,0:T(8,128)(2,1)S(1)} %get-tuple-element.59.keys, bf16[512,1024]{1,0:T(8,128)(2,1)S(1)} %get-tuple-element.60.base, f32[1,2048]{1,0:T(1,128)S(1)} %get-tuple-element.61.gain, bf16[128,512]{1,0:T(8,128)(2,1)S(1)} %get-tuple-element.99.refs_0_, ...), custom_call_target="tpu_custom_call" | custom-call | flops 67108864 | bytes 1048576 | tf_op jit(solution)/shard_map/mix/pallas_call | solution.py:373
  25.4 0.3 collective-permute-done.6.got_ref
  25.7 0.1 last.3
  25.8 0.3 %collective-permute-start.7 = (bf16[128,512]{1,0:T(8,128)(2,1)S(1)}, bf16[128,512]{1,0:T(8,128)(2,1)S(1)}, u32[]{:S(2)}, u32[]{:S(2)}) collective-permute-start(bf16[128,512]{1,0:T(8,128)(2,1)S(1)} %get-tuple-element.110), channel_id=1, source_target_pairs={{0,4},{4,0},{8,12},{12,8},{16,20},{20,16},{24,28},{28,24},{1,5},{5... | collective-permute-start | bytes 393224 | tf_op jit(solution)/shard_map/ppermute | solution.py:449
  26.1 0.0 collective-permute-done.5.refs_0_
  26.1 2.0 %mix.4.base = f32[512,1024]{1,0:T(8,128)S(1)} custom-call(s32[1]{0:T(128)} %bitcast.here_ref, bf16[512,256]{1,0:T(8,128)(2,1)S(1)} %get-tuple-element.59.keys, f32[512,1024]{1,0:T(8,128)S(1)} %mix.3.base, f32[1,2048]{1,0:T(1,128)S(1)} %get-tuple-element.61.gain, bf16[128,512]{1,0:T(8,128)(2,1)S(1)} %collective-permute-done.5.refs_0_, ...), custom_call_target="tpu_custom_call" | custom-call | flops 134217728 | bytes 1048576 | tf_op jit(solution)/shard_map/mix/pallas_call | solution.py:373
  28.1 0.0 collective-permute-done.7.refs_0_
  28.1 1.9 %mix.5 = bf16[512,1024]{1,0:T(8,128)(2,1)} custom-call(s32[1]{0:T(128)} %bitcast.here_ref, bf16[512,256]{1,0:T(8,128)(2,1)S(1)} %get-tuple-element.59.keys, f32[512,1024]{1,0:T(8,128)S(1)} %mix.4.base, f32[1,2048]{1,0:T(1,128)S(1)} %get-tuple-element.61.gain, bf16[128,512]{1,0:T(8,128)(2,1)S(1)} %collective-permute-done.7.refs_0_, ...), custom_call_target="tpu_custom_call" | custom-call | flops 67108864 | bytes 1048576 | tf_op jit(solution)/shard_map/mix/pallas_call | solution.py:373
Async XLA Ops:
  6.3 1.6 %collective-permute-start = (bf16[144,512]{1,0:T(8,128)(2,1)S(1)}, bf16[144,512]{1,0:T(8,128)(2,1)S(1)}, u32[]{:S(2)}, u32[]{:S(2)}) collective-permute-start(bf16[144,512]{1,0:T(8,128)(2,1)S(1)} %get-tuple-element.68), channel_id=1, source_target_pairs={{0,4},{4,0},{8,12},{12,8},{16,20},{20,16},{24,28},{28,24},{1,5},{5... | collective-permute-start | bytes 442376 | tf_op jit(solution)/shard_map/ppermute | solution.py:417
  9.1 4.1 %collective-permute-start.2 = (bf16[144,512]{1,0:T(8,128)(2,1)S(1)}, bf16[144,512]{1,0:T(8,128)(2,1)S(1)}, u32[]{:S(2)}, u32[]{:S(2)}) collective-permute-start(bf16[144,512]{1,0:T(8,128)(2,1)S(1)} %get-tuple-element.76), channel_id=1, source_target_pairs={{0,4},{4,0},{8,12},{12,8},{16,20},{20,16},{24,28},{28,24},{1,5},{5... | collective-permute-start | bytes 442376 | tf_op jit(solution)/shard_map/ppermute | solution.py:421
  9.4 7.3 %collective-permute-start.1 = (bf16[144,512]{1,0:T(8,128)(2,1)S(1)}, bf16[144,512]{1,0:T(8,128)(2,1)S(1)}, u32[]{:S(2)}, u32[]{:S(2)}) collective-permute-start(bf16[144,512]{1,0:T(8,128)(2,1)S(1)} %total.2.total_ref.before_ref), channel_id=1, source_target_pairs={{0,8},{4,12},{8,0},{12,4},{16,24},{20,28},{24,16},{28,20},{1,9},{5... | collective-permute-start | bytes 442376 | tf_op jit(solution)/shard_map/ppermute | solution.py:428
  13.3 6.9 %collective-permute-start.4 = (bf16[144,512]{1,0:T(8,128)(2,1)S(1)}, bf16[144,512]{1,0:T(8,128)(2,1)S(1)}, u32[]{:S(2)}, u32[]{:S(2)}) collective-permute-start(bf16[144,512]{1,0:T(8,128)(2,1)S(1)} %total.3.total_ref.before_ref), channel_id=1, source_target_pairs={{0,8},{4,12},{8,0},{12,4},{16,24},{20,28},{24,16},{28,20},{1,9},{5... | collective-permute-start | bytes 442376 | tf_op jit(solution)/shard_map/ppermute | solution.py:428
  16.8 7.3 %collective-permute-start.3 = (bf16[144,512]{1,0:T(8,128)(2,1)S(1)}, bf16[144,512]{1,0:T(8,128)(2,1)S(1)}, u32[]{:S(2)}, u32[]{:S(2)}) collective-permute-start(bf16[144,512]{1,0:T(8,128)(2,1)S(1)} %get-tuple-element.81), channel_id=1, source_target_pairs={{0,16},{4,20},{8,24},{12,28},{16,0},{20,4},{24,8},{28,12},{1,17},{... | collective-permute-start | bytes 442376 | tf_op jit(solution)/shard_map/ppermute | solution.py:440
  20.5 5.2 %collective-permute-start.6 = (bf16[144,512]{1,0:T(8,128)(2,1)S(1)}, bf16[144,512]{1,0:T(8,128)(2,1)S(1)}, u32[]{:S(2)}, u32[]{:S(2)}) collective-permute-start(bf16[144,512]{1,0:T(8,128)(2,1)S(1)} %get-tuple-element.90), channel_id=1, source_target_pairs={{0,16},{4,20},{8,24},{12,28},{16,0},{20,4},{24,8},{28,12},{1,17},{... | collective-permute-start | bytes 442376 | tf_op jit(solution)/shard_map/ppermute | solution.py:440
  24.3 1.8 %collective-permute-start.5 = (bf16[128,512]{1,0:T(8,128)(2,1)S(1)}, bf16[128,512]{1,0:T(8,128)(2,1)S(1)}, u32[]{:S(2)}, u32[]{:S(2)}) collective-permute-start(bf16[128,512]{1,0:T(8,128)(2,1)S(1)} %get-tuple-element.102), channel_id=1, source_target_pairs={{0,4},{4,0},{8,12},{12,8},{16,20},{20,16},{24,28},{28,24},{1,5},{5... | collective-permute-start | bytes 393224 | tf_op jit(solution)/shard_map/ppermute | solution.py:449
  25.8 2.4 %collective-permute-start.7 = (bf16[128,512]{1,0:T(8,128)(2,1)S(1)}, bf16[128,512]{1,0:T(8,128)(2,1)S(1)}, u32[]{:S(2)}, u32[]{:S(2)}) collective-permute-start(bf16[128,512]{1,0:T(8,128)(2,1)S(1)} %get-tuple-element.110), channel_id=1, source_target_pairs={{0,4},{4,0},{8,12},{12,8},{16,20},{20,16},{24,28},{28,24},{1,5},{5... | collective-permute-start | bytes 393224 | tf_op jit(solution)/shard_map/ppermute | solution.py:449

commit v6 on v5

--- a/solution.py
+++ b/solution.py
@@ -64,22 +64,21 @@
     return jnp.concatenate(pairs, axis=1)
 
 
-def project(half, group, heads, head_dim, w, normed, b_t, grow, fall_end, x_ref, xs_ref, s_ref):
+def project(jobs, heads, head_dim, normed, b_t, grow, fall_end):
     width = b_t.shape[0]
-    size = x_ref.shape[1]
-    first = (half * 2 + group) * (size // head_dim)
     later = []
-    for j in range(size // CHUNK):
-        cols = slice(j * CHUNK, (j + 1) * CHUNK)
-        spread = spread_heads(first + j * (CHUNK // head_dim), heads, head_dim)
-        x = dot(normed[...], compact(w, j, 0)).astype(BF)
-        scaled = (x.astype(F32) * dot(grow, spread)).astype(BF)
-        x_ref[:, cols] = x
-        xs_ref[:, cols] = scaled
-        decay = dot(fall_end, spread)[EXTRA - 1:EXTRA]
-        s_ref[width:width + EXTRA, cols] = decay_rows(decay)
-        later.append((cols, scaled, decay))
-    for cols, scaled, decay in later:
+    for first, w, x_ref, xs_ref, s_ref in jobs:
+        for j in range(x_ref.shape[1] // CHUNK):
+            cols = slice(j * CHUNK, (j + 1) * CHUNK)
+            spread = spread_heads(first + j * (CHUNK // head_dim), heads, head_dim)
+            x = dot(normed[...], compact(w, j, 0)).astype(BF)
+            scaled = (x.astype(F32) * dot(grow, spread)).astype(BF)
+            x_ref[:, cols] = x
+            xs_ref[:, cols] = scaled
+            decay = dot(fall_end, spread)[EXTRA - 1:EXTRA]
+            s_ref[width:width + EXTRA, cols] = decay_rows(decay)
+            later.append((s_ref, cols, scaled, decay))
+    for s_ref, cols, scaled, decay in later:
         s_ref[0:width, cols] = (dot(b_t, scaled) * decay).astype(BF)
 
 
@@ -119,7 +118,7 @@
 
 def encode_kernel(heads, head_dim, here_ref, cell_ref, frames_any, enc_in_any, bias_any, enc_out_any, pos_any, gain_any,
                   w_keys_any, w_step_any, step_bias_any, code_any, skip_any, out_gain_any, w_pair_any,
-                  encoded, normed, keys, b_t, grow, fall, skip, out_gain, x_ref, xs_ref, s_ref, w_o1, w_m1, w_o2, w_m2,
+                  encoded, normed, keys, b_t, grow, fall, skip, out_gain, x_o1, xs_o1, x_o2, xs_o2, s_o, w_o1, w_m1, w_o2, w_m2,
                   frames, enc_in, bias, enc_out, pos, norm_gain, w_keys, w_step, step_bias, code, sem, wsem):
     half = 1 - here_ref[0] % 2
     cell = cell_ref[0]
@@ -130,7 +129,7 @@
     first = [in_pieces(src, dst, wsem, i) for i, (src, dst) in enumerate((
         (frames_any, frames), (enc_in_any, enc_in), (enc_out_any, enc_out), (w_keys_any, w_keys), (w_step_any, w_step)))]
     big = [in_pieces(group_columns(w_pair_any, dst, which, group), dst, wsem, 5 + i) for i, (which, group, dst) in enumerate((
-        (half, 0, w_o1), (1 - half, 0, w_m1), (half, 1, w_o2), (1 - half, 1, w_m2)))]
+        (half, 0, w_o1), (half, 1, w_o2), (1 - half, 0, w_m1), (1 - half, 1, w_m2)))]
     start_pieces(first[:2])
     for c in small:
         c.start()
@@ -189,9 +188,12 @@
     f = split_two(jnp.exp(cum), heads)
     grow[...] = g
     fall[...] = f
-    wait_pieces(big[:1])
-    project(half, 0, heads, head_dim, w_o1, normed, b_t[...], g, f[rows - EXTRA:], x_ref, xs_ref, s_ref)
-    wait_pieces(big[1:])
+    wait_pieces(big[:2])
+    size = x_o1.shape[1]
+    per = size // head_dim
+    project([(half * 2 * per, w_o1, x_o1, xs_o1, s_o.at[:, :size]), (half * 2 * per + per, w_o2, x_o2, xs_o2, s_o.at[:, size:])],
+            heads, head_dim, normed, b_t[...], g, f[rows - EXTRA:])
+    wait_pieces(big[2:])
 
 
 def group_columns(w_any, like, half, group):
@@ -202,7 +204,8 @@
 def project_kernel(heads, head_dim, own, group, here_ref, normed, b_t, grow, fall, w, x_ref, xs_ref, s_ref):
     half = (here_ref[0] + 1 - own) % 2
     rows = normed.shape[0]
-    project(half, group, heads, head_dim, w, normed, b_t[...], grow[...], fall[rows - EXTRA:], x_ref, xs_ref, s_ref)
+    first = (half * 2 + group) * (x_ref.shape[1] // head_dim)
+    project([(first, w, x_ref, xs_ref, s_ref)], heads, head_dim, normed, b_t[...], grow[...], fall[rows - EXTRA:])
 
 
 def opened(ref):
@@ -217,9 +220,10 @@
     ref[width:, :] = decay_rows(decay)
 
 
-def total_kernel(here_ref, mine_ref, got_ref, total_ref):
+def total_kernel(group, here_ref, mine_ref, got_ref, total_ref):
+    size = mine_ref.shape[1]
     mine, mine_decay = opened(mine_ref)
-    got, got_decay = opened(got_ref)
+    got, got_decay = opened(got_ref.at[:, group * size:(group + 1) * size])
 
     @pl.when(here_ref[0] % 2 == 1)
     def _():
@@ -230,10 +234,16 @@
         close(total_ref, got_decay * mine + got, mine_decay * got_decay)
 
 
-def step_kernel(first, reach, here_ref, total_ref, got_ref, before_ref, new_before_ref, new_total_ref):
+def step_kernel(first, final, reach, here_ref, total_ref, got_ref, before_ref, new_before_ref, new_total_ref):
     later = (here_ref[0] // reach) % 2 == 1
     got, got_decay = opened(got_ref)
     total, total_decay = opened(total_ref)
+
+    def put_total(value):
+        if final:
+            new_total_ref[...] = value.astype(BF)
+        else:
+            close(new_total_ref, value, total_decay * got_decay)
 
     @pl.when(later)
     def _():
@@ -242,7 +252,7 @@
         else:
             before, before_decay = opened(before_ref)
             close(new_before_ref, before + before_decay * got, before_decay * got_decay)
-        close(new_total_ref, total_decay * got + total, total_decay * got_decay)
+        put_total(total_decay * got + total)
 
     @pl.when(jnp.logical_not(later))
     def _():
@@ -250,19 +260,19 @@
             close(new_before_ref, jnp.zeros_like(got), jnp.ones_like(got_decay))
         else:
             new_before_ref[...] = before_ref[...]
-        close(new_total_ref, got_decay * total + got, total_decay * got_decay)
-
-
-def last_kernel(reach, here_ref, got_ref, before_ref, mine_ref, first_ref, keep_ref, send_ref):
-    width = keep_ref.shape[0]
+        put_total(got_decay * total + got)
+
+
+def last_kernel(reach, group, here_ref, got_ref, before_ref, mine_ref, first_ref, keep_ref, send_ref):
+    state_size = keep_ref.shape[1]
     later = (here_ref[0] // reach) % 2 == 1
-    got, _ = opened(got_ref)
+    got = got_ref[:keep_ref.shape[0], :].astype(F32)
     before, before_decay = opened(before_ref)
     before = before + jnp.where(later, before_decay, 0.0) * got
 
     @pl.when(here_ref[0] % 2 == 1)
     def _():
-        state, decay = opened(first_ref)
+        state, decay = opened(first_ref.at[:, group * state_size:(group + 1) * state_size])
         keep_ref[...] = (decay * before + state).astype(BF)
         send_ref[...] = before.astype(BF)
 
@@ -379,11 +389,11 @@
     where = [(SM, here)]
 
     part, message, weight = near((rows, size)), near((width + EXTRA, size)), near((depth, 2 * size))
-    encoded, normed, keys, b_t, grow, fall, skip, gain, x_o1, xs_o1, s_o1, w_o1, w_m1, w_o2, w_m2 = call(
+    encoded, normed, keys, b_t, grow, fall, skip, gain, x_o1, xs_o1, x_o2, xs_o2, s_o, w_o1, w_m1, w_o2, w_m2 = call(
         functools.partial(encode_kernel, heads, head_dim), "encode",
         (near((rows, depth)), near((rows, depth)), near((rows, 2 * width)), near((width, rows)),
          near((rows, 2 * heads)), near((rows, 2 * heads)), near((1, heads), F32), near((1, heads * head_dim), F32),
-         part, part, message) + (weight,) * 4,
+         part, part, part, part, near((width + EXTRA, 2 * size))) + (weight,) * 4,
         where + [(SM, patch_cell)] + hbm(frames.reshape(rows, pix), enc_in, row(enc_bias), enc_out, pos_table, row(norm_gain),
                                          w_keys, w_step.T, row(step_bias), row(decay_code), row(skip_gain), row(out_gain),
                                          w_pair),
@@ -414,45 +424,51 @@
                     [near((rows, depth)), sems(depth // CHUNK)] if last else [], len(places) * rows * depth * size,
                     ANY if last else VM)[0]
 
-    got_1 = lax.ppermute(s_o1, "tm", pair(1))
+    totals, befores, arriving = [None, None], [None, None], [None, None]
+    done = {}
+
+    def work(own, group, w, x, xs, stamp):
+        done[own, group] = inner(own, group, w, after(x, stamp), xs)
+        return done[own, group][0]
+
+    def start_total(i, mine):
+        totals[i], = call(functools.partial(total_kernel, i), "total", (message,), where + vm(mine, got))
+        befores[i] = totals[i]
+        arriving[i] = lax.ppermute(totals[i], "tm", pair(2))
+
+    def advance(i, reach, arrived):
+        final = reach * 4 >= peers
+        befores[i], totals[i] = call(
+            functools.partial(step_kernel, reach == 2, final, reach), "step",
+            (message, near((width, size)) if final else message), where + vm(totals[i], arrived, befores[i]))
+        arriving[i] = lax.ppermute(totals[i], "tm", pair(2 * reach))
+
+    def finish(i, arrived, mine):
+        keep, send = call(functools.partial(last_kernel, peers // 2, i), "last", (near((width, size)),) * 2,
+                          where + vm(arrived, befores[i], mine, got))
+        return keep, lax.ppermute(send, "tm", pair(1))
+
+    got = lax.ppermute(s_o, "tm", pair(1))
     x_m1, xs_m1, s_m1 = projected(1, 0, w_m1)
-    total_1, = call(total_kernel, "total", (message,), where + vm(s_m1, got_1))
-    x_o2, xs_o2, s_o2 = projected(0, 1, after(w_o2, total_1))
-    got_2 = lax.ppermute(s_o2, "tm", pair(1))
-    x_m2, xs_m2, s_m2 = projected(1, 1, w_m2)
-    total_2, = call(total_kernel, "total", (message,), where + vm(s_m2, got_2))
-
-    todo = [(0, 0, w_o1, x_o1, xs_o1), (1, 0, w_m1, x_m1, xs_m1), (1, 1, w_m2, x_m2, xs_m2), (0, 1, w_o2, x_o2, xs_o2)]
-    done = {}
-    totals, befores = [total_1, total_2], [total_1, total_2]
-    gots = [lax.ppermute(total_1, "tm", pair(2)), lax.ppermute(total_2, "tm", pair(2))]
-    stamp = total_2
-    reach = 2
+    start_total(0, s_m1)
+    x_m2, xs_m2, s_m2 = projected(1, 1, after(w_m2, totals[0]))
+    stamp = work(0, 0, w_o1, x_o1, xs_o1, s_m2)
+    start_total(1, after(s_m2, stamp))
+    advance(0, 2, after(arriving[0], totals[1]))
+    stamp = work(1, 0, w_m1, x_m1, xs_m1, befores[0])
+    stamp = work(1, 1, w_m2, x_m2, xs_m2, stamp)
+    advance(1, 2, after(arriving[1], stamp))
+    reach = 4
     while reach * 2 < peers:
         for i in range(2):
-            if todo:
-                own, group, w, x, xs = todo.pop(0)
-                done[own, group] = inner(own, group, w, after(x, stamp), xs)
-                gots[i] = after(gots[i], done[own, group][0])
-            befores[i], totals[i] = call(functools.partial(step_kernel, reach == 2, reach), "step", (message, message),
-                                         where + vm(totals[i], gots[i], befores[i]))
-            stamp = totals[i]
-            gots[i] = lax.ppermute(totals[i], "tm", pair(2 * reach))
+            advance(i, reach, arriving[i])
         reach *= 2
-    for own, group, w, x, xs in todo:
-        done[own, group] = inner(own, group, w, after(x, stamp), xs)
-        stamp = done[own, group][0]
-
-    def last(i, got, mine, first):
-        keep, send = call(functools.partial(last_kernel, reach), "last", (near((width, size)),) * 2,
-                          where + vm(got, befores[i], mine, first))
-        return keep, lax.ppermute(send, "tm", pair(1))
-
-    keep_1, sent_1 = last(0, after(gots[0], stamp), s_m1, got_1)
-    mix_1 = mixed(((1, 0),), encoded, False, (keep_1, *done[1, 0]))
-    keep_2, sent_2 = last(1, after(gots[1], mix_1), s_m2, got_2)
-    mix_2 = mixed(((0, 0), (1, 1)), mix_1, False, (sent_1, *done[0, 0]), (keep_2, *done[1, 1]))
-    return mixed(((0, 1),), mix_2, True, (sent_2, *done[0, 1])).reshape(rows, 1, depth)
+    keep_1, sent_1 = finish(0, after(arriving[0], befores[1]), s_m1)
+    stamp = work(0, 1, w_o2, x_o2, xs_o2, keep_1)
+    mixing = mixed(((1, 0),), after(encoded, stamp), False, (keep_1, *done[1, 0]))
+    keep_2, sent_2 = finish(1, after(arriving[1], mixing), s_m2)
+    mixing = mixed(((0, 0), (1, 1)), after(mixing, keep_2), False, (sent_1, *done[0, 0]), (keep_2, *done[1, 1]))
+    return mixed(((0, 1),), mixing, True, (sent_2, *done[0, 1])).reshape(rows, 1, depth)
 
 
 def solution(mesh):

time: 30.4 us -> 30.2 us (level)
  starting transfers between devices: 7.46 us -> 6.75 us
  waiting for transfers between devices: 2.28 us -> 2.8 us
    ppermute x8 -> x7, starting transfers between devices: 7.46 us -> 6.75 us  [the longest x2 3.09 us: advance(): arriving[i] = lax.ppermute(totals[i], 'tm', pair(2 * reach))]
    ppermute x8 -> x7, waiting for transfers between devices: 2.28 us -> 2.8 us  [the longest x2 1.55 us: start_total(): arriving[i] = lax.ppermute(totals[i], 'tm', pair(2))]
    pallas_call x17 -> x16, Pallas kernels: 19.5 us -> 19.4 us  [call(): pl.pallas_call(kernel, out_shape=tuple(outs), in_specs=specs, out_specs=(...]
  transfers between devices with their start and end apart: 8 -> 7, of which waited for: 2 -> 3; matrix products, arithmetic and copies ran while one was open for 0% -> 0% of each run, Pallas kernels for 36% -> 36%
where the time goes in v6:
time: 30.2 us; the launch traced here: 30 us
  Pallas kernels  19.4 us (64%)
  starting transfers between devices  6.75 us (22%)
  waiting for transfers between devices  2.8 us (9%)
  between operations  0.95 us (3%)
    pallas_call x16, Pallas kernels, call(): pl.pallas_call(kernel, out_shape=tuple(outs), in_specs=specs, out_specs=(...  19.4 us
    ppermute x2, starting transfers between devices, advance(): arriving[i] = lax.ppermute(totals[i], 'tm', pair(2 * reach))  3.09 us
    ppermute x2, starting transfers between devices, start_total(): arriving[i] = lax.ppermute(totals[i], 'tm', pair(2))  3.01 us
    ppermute x2, waiting for transfers between devices, start_total(): arriving[i] = lax.ppermute(totals[i], 'tm', pair(2))  1.55 us
    ppermute x2, waiting for transfers between devices, advance(): arriving[i] = lax.ppermute(totals[i], 'tm', pair(2 * reach))  1.1 us
  transfers between devices with their start and end apart: 7, of which 3 were waited for; matrix products, arithmetic and copies ran while one was open for 0% of the time, Pallas kernels for 36%

profile of v6, /device:TPU:0, one launch (start us, length us, event | category | flops | bytes accessed | tf_op | source)
XLA Modules:
  0.0 30.0 jit_solution(13174611371316694656)
XLA Ops:
  0.7 6.6 %encode.1 = (bf16[512,1024]{1,0:T(8,128)(2,1)S(1)}, bf16[512,1024]{1,0:T(8,128)(2,1)S(1)}, bf16[512,256]{1,0:T(8,128)(2,1)S(1)}, bf16[128,512]{1,0:T(8,128)(2,1)...) custom-call(s32[1]{0:T(128)} %bitcast.here_ref, ...), custom_call_target="tpu_custom_call" | custom-call | flops 134217728 | bytes 1048576 | tf_op jit(solution)/shard_map/encode/pallas_call | solution.py:383
  7.2 0.5 %collective-permute-start = (bf16[144,1024]{1,0:T(8,128)(2,1)S(1)}, bf16[144,1024]{1,0:T(8,128)(2,1)S(1)}, u32[]{:S(2)}, u32[]{:S(2)}) collective-permute-start(bf16[144,1024]{1,0:T(8,128)(2,1)S(1)} %get-tuple-element.72), channel_id=1, source_target_pairs={{0,4},{4,0},{8,12},{12,8},{16,20},{20,16},{24,28},{28,24},{1,5},{5... | collective-permute-start | bytes 884744 | tf_op jit(solution)/shard_map/ppermute | solution.py:451
  7.8 1.1 %project.2 = (bf16[512,512]{1,0:T(8,128)(2,1)S(1)}, bf16[512,512]{1,0:T(8,128)(2,1)S(1)}, bf16[144,512]{1,0:T(8,128)(2,1)S(1)}) custom-call(s32[1]{0:T(128)} %bitcast.here_ref, bf16[512,1024]{1,0:T(8,128)(2,1)S(1)} %get-tuple-element.63.normed, bf16[128,512]{1,0:T(8,128)(2,1)S(1)} %get-tuple-element.68.b_t, bf16[512,64]{1,0:T(8,128)(2,1)S(1)} %get-tuple-element.69.grow, ...), custom_call_target="tpu_custom_call" | custom-call | flops 67108864 | bytes 1048576 | tf_op jit(solution)/shard_map/project/pallas_call | solution.py:383
  8.8 0.1 collective-permute-done.got_ref.first_ref
  9.0 0.1 total.2.total_ref.before_ref
  9.1 2.9 %collective-permute-start.1 = (bf16[144,512]{1,0:T(8,128)(2,1)S(1)}, bf16[144,512]{1,0:T(8,128)(2,1)S(1)}, u32[]{:S(2)}, u32[]{:S(2)}) collective-permute-start(bf16[144,512]{1,0:T(8,128)(2,1)S(1)} %total.2.total_ref.before_ref), channel_id=1, source_target_pairs={{0,8},{4,12},{8,0},{12,4},{16,24},{20,28},{24,16},{28,20},{1,9},{5... | collective-permute-start | bytes 442376 | tf_op jit(solution)/shard_map/ppermute | solution.py:437
  12.0 1.1 %project.3 = (bf16[512,512]{1,0:T(8,128)(2,1)S(1)}, bf16[512,512]{1,0:T(8,128)(2,1)S(1)}, bf16[144,512]{1,0:T(8,128)(2,1)S(1)}) custom-call(s32[1]{0:T(128)} %bitcast.here_ref, bf16[512,1024]{1,0:T(8,128)(2,1)S(1)} %get-tuple-element.63.normed, bf16[128,512]{1,0:T(8,128)(2,1)S(1)} %get-tuple-element.68.b_t, bf16[512,64]{1,0:T(8,128)(2,1)S(1)} %get-tuple-element.69.grow, ...), custom_call_target="tpu_custom_call" | custom-call | flops 67108864 | bytes 1048576 | tf_op jit(solution)/shard_map/project/pallas_call | solution.py:383
  13.0 1.4 %inner.4 = (bf16[512,512]{1,0:T(8,128)(2,1)S(1)}, bf16[512,512]{1,0:T(8,128)(2,1)S(1)}, bf16[512,1024]{1,0:T(8,128)(2,1)S(1)}, bf16[512,512]{1,0:T(8,128)(2,1)S(1)}) custom-call(s32[1]{0:T(128)} %bitcast.here_ref, bf16[512,1024]{1,0:T(8,128)(2,1)S(1)} %get-tuple-element.63.normed, bf16[512,256]{1,0:T(8,128)(2,1)S(1)} %get-tuple-element.61.keys, ...), custom_call_target="tpu_custom_call" | custom-call | flops 67108864 | bytes 1048576 | tf_op jit(solution)/shard_map/inner/pallas_call | solution.py:383
  14.4 0.1 total.3.total_ref.before_ref
  14.5 0.1 collective-permute-start.3
  14.6 1.5 %collective-permute-done.1.got_ref = bf16[144,512]{1,0:T(8,128)(2,1)S(1)} collective-permute-done((bf16[144,512]{1,0:T(8,128)(2,1)S(1)}, bf16[144,512]{1,0:T(8,128)(2,1)S(1)}, u32[]{:S(2)}, u32[]{:S(2)}) %collective-permute-start.1) | collective-permute-done | bytes 147488 | tf_op jit(solution)/shard_map/ppermute | solution.py:437
  16.1 0.1 step.2
  16.2 1.8 %collective-permute-start.2 = (bf16[128,512]{1,0:T(8,128)(2,1)S(1)}, bf16[128,512]{1,0:T(8,128)(2,1)S(1)}, u32[]{:S(2)}, u32[]{:S(2)}) collective-permute-start(bf16[128,512]{1,0:T(8,128)(2,1)S(1)} %get-tuple-element.83), channel_id=1, source_target_pairs={{0,16},{4,20},{8,24},{12,28},{16,0},{20,4},{24,8},{28,12},{1,17},{... | collective-permute-start | bytes 393224 | tf_op jit(solution)/shard_map/ppermute | solution.py:444
  18.0 1.2 %inner.5 = (bf16[512,512]{1,0:T(8,128)(2,1)S(1)}, bf16[512,512]{1,0:T(8,128)(2,1)S(1)}, bf16[512,1024]{1,0:T(8,128)(2,1)S(1)}) custom-call(s32[1]{0:T(128)} %bitcast.here_ref, bf16[512,1024]{1,0:T(8,128)(2,1)S(1)} %get-tuple-element.63.normed, bf16[512,256]{1,0:T(8,128)(2,1)S(1)} %get-tuple-element.61.keys, bf16[512,64]{1,0:T(8,128)(2,1)S(1)} %get-tuple-element.64.fall, ...), custom_call_target="tpu_custom_call" | custom-call | flops 67108864 | bytes 1048576 | tf_op jit(solution)/shard_map/inner/pallas_call | solution.py:383
  19.2 1.2 %inner.6 = (bf16[512,512]{1,0:T(8,128)(2,1)S(1)}, bf16[512,512]{1,0:T(8,128)(2,1)S(1)}, bf16[512,1024]{1,0:T(8,128)(2,1)S(1)}) custom-call(s32[1]{0:T(128)} %bitcast.here_ref, bf16[512,1024]{1,0:T(8,128)(2,1)S(1)} %get-tuple-element.63.normed, bf16[512,256]{1,0:T(8,128)(2,1)S(1)} %get-tuple-element.61.keys, bf16[512,64]{1,0:T(8,128)(2,1)S(1)} %get-tuple-element.64.fall, ...), custom_call_target="tpu_custom_call" | custom-call | flops 67108864 | bytes 1048576 | tf_op jit(solution)/shard_map/inner/pallas_call | solution.py:383
  20.5 0.0 collective-permute-done.3.got_ref
  20.5 0.1 step.3
  20.6 1.3 %collective-permute-start.4 = (bf16[128,512]{1,0:T(8,128)(2,1)S(1)}, bf16[128,512]{1,0:T(8,128)(2,1)S(1)}, u32[]{:S(2)}, u32[]{:S(2)}) collective-permute-start(bf16[128,512]{1,0:T(8,128)(2,1)S(1)} %get-tuple-element.105), channel_id=1, source_target_pairs={{0,16},{4,20},{8,24},{12,28},{16,0},{20,4},{24,8},{28,12},{1,17},{... | collective-permute-start | bytes 393224 | tf_op jit(solution)/shard_map/ppermute | solution.py:444
  21.8 0.0 collective-permute-done.2.got_ref
  21.8 0.3 last.2
  22.1 0.1 collective-permute-start.5
  22.2 1.2 %inner.7 = (bf16[512,512]{1,0:T(8,128)(2,1)S(1)}, bf16[512,512]{1,0:T(8,128)(2,1)S(1)}, bf16[512,1024]{1,0:T(8,128)(2,1)S(1)}) custom-call(s32[1]{0:T(128)} %bitcast.here_ref, bf16[512,1024]{1,0:T(8,128)(2,1)S(1)} %get-tuple-element.63.normed, bf16[512,256]{1,0:T(8,128)(2,1)S(1)} %get-tuple-element.61.keys, bf16[512,64]{1,0:T(8,128)(2,1)S(1)} %get-tuple-element.64.fall, ...), custom_call_target="tpu_custom_call" | custom-call | flops 67108864 | bytes 1048576 | tf_op jit(solution)/shard_map/inner/pallas_call | solution.py:383
  23.4 1.1 %mix.3.base = f32[512,1024]{1,0:T(8,128)S(1)} custom-call(s32[1]{0:T(128)} %bitcast.here_ref, bf16[512,256]{1,0:T(8,128)(2,1)S(1)} %get-tuple-element.61.keys, bf16[512,1024]{1,0:T(8,128)(2,1)S(1)} %get-tuple-element.101.base, f32[1,2048]{1,0:T(1,128)S(1)} %get-tuple-element.102.gain, bf16[128,512]{1,0:T(8,128)(2,1)S(1)} %get-tuple-element.97.refs_0_, ...), custom_call_target="tpu_custom_call" | custom-call | flops 67108864 | bytes 1048576 | tf_op jit(solution)/shard_map/mix/pallas_call | solution.py:383
  24.5 1.1 %collective-permute-done.4.got_ref = bf16[128,512]{1,0:T(8,128)(2,1)S(1)} collective-permute-done((bf16[128,512]{1,0:T(8,128)(2,1)S(1)}, bf16[128,512]{1,0:T(8,128)(2,1)S(1)}, u32[]{:S(2)}, u32[]{:S(2)}) %collective-permute-start.4) | collective-permute-done | bytes 131104 | tf_op jit(solution)/shard_map/ppermute | solution.py:444
  25.6 0.1 last.3
  25.7 0.1 collective-permute-start.6
  25.8 0.0 collective-permute-done.5.refs_0_
  25.8 2.0 %mix.4.base = f32[512,1024]{1,0:T(8,128)S(1)} custom-call(s32[1]{0:T(128)} %bitcast.here_ref, bf16[512,256]{1,0:T(8,128)(2,1)S(1)} %get-tuple-element.61.keys, f32[512,1024]{1,0:T(8,128)S(1)} %mix.3.base, f32[1,2048]{1,0:T(1,128)S(1)} %get-tuple-element.102.gain, bf16[128,512]{1,0:T(8,128)(2,1)S(1)} %collective-permute-done.5.refs_0_, ...), custom_call_target="tpu_custom_call" | custom-call | flops 134217728 | bytes 1048576 | tf_op jit(solution)/shard_map/mix/pallas_call | solution.py:383
  27.8 0.0 collective-permute-done.6.refs_0_
  27.9 1.9 %mix.5 = bf16[512,1024]{1,0:T(8,128)(2,1)} custom-call(s32[1]{0:T(128)} %bitcast.here_ref, bf16[512,256]{1,0:T(8,128)(2,1)S(1)} %get-tuple-element.61.keys, f32[512,1024]{1,0:T(8,128)S(1)} %mix.4.base, f32[1,2048]{1,0:T(1,128)S(1)} %get-tuple-element.102.gain, bf16[128,512]{1,0:T(8,128)(2,1)S(1)} %collective-permute-done.6.refs_0_, ...), custom_call_target="tpu_custom_call" | custom-call | flops 67108864 | bytes 1048576 | tf_op jit(solution)/shard_map/mix/pallas_call | solution.py:383
Async XLA Ops:
  7.2 1.7 %collective-permute-start = (bf16[144,1024]{1,0:T(8,128)(2,1)S(1)}, bf16[144,1024]{1,0:T(8,128)(2,1)S(1)}, u32[]{:S(2)}, u32[]{:S(2)}) collective-permute-start(bf16[144,1024]{1,0:T(8,128)(2,1)S(1)} %get-tuple-element.72), channel_id=1, source_target_pairs={{0,4},{4,0},{8,12},{12,8},{16,20},{20,16},{24,28},{28,24},{1,5},{5... | collective-permute-start | bytes 884744 | tf_op jit(solution)/shard_map/ppermute | solution.py:451
  9.1 7.1 %collective-permute-start.1 = (bf16[144,512]{1,0:T(8,128)(2,1)S(1)}, bf16[144,512]{1,0:T(8,128)(2,1)S(1)}, u32[]{:S(2)}, u32[]{:S(2)}) collective-permute-start(bf16[144,512]{1,0:T(8,128)(2,1)S(1)} %total.2.total_ref.before_ref), channel_id=1, source_target_pairs={{0,8},{4,12},{8,0},{12,4},{16,24},{20,28},{24,16},{28,20},{1,9},{5... | collective-permute-start | bytes 442376 | tf_op jit(solution)/shard_map/ppermute | solution.py:437
  14.5 6.0 %collective-permute-start.3 = (bf16[144,512]{1,0:T(8,128)(2,1)S(1)}, bf16[144,512]{1,0:T(8,128)(2,1)S(1)}, u32[]{:S(2)}, u32[]{:S(2)}) collective-permute-start(bf16[144,512]{1,0:T(8,128)(2,1)S(1)} %total.3.total_ref.before_ref), channel_id=1, source_target_pairs={{0,8},{4,12},{8,0},{12,4},{16,24},{20,28},{24,16},{28,20},{1,9},{5... | collective-permute-start | bytes 442376 | tf_op jit(solution)/shard_map/ppermute | solution.py:437
  16.2 5.6 %collective-permute-start.2 = (bf16[128,512]{1,0:T(8,128)(2,1)S(1)}, bf16[128,512]{1,0:T(8,128)(2,1)S(1)}, u32[]{:S(2)}, u32[]{:S(2)}) collective-permute-start(bf16[128,512]{1,0:T(8,128)(2,1)S(1)} %get-tuple-element.83), channel_id=1, source_target_pairs={{0,16},{4,20},{8,24},{12,28},{16,0},{20,4},{24,8},{28,12},{1,17},{... | collective-permute-start | bytes 393224 | tf_op jit(solution)/shard_map/ppermute | solution.py:444
  20.6 5.0 %collective-permute-start.4 = (bf16[128,512]{1,0:T(8,128)(2,1)S(1)}, bf16[128,512]{1,0:T(8,128)(2,1)S(1)}, u32[]{:S(2)}, u32[]{:S(2)}) collective-permute-start(bf16[128,512]{1,0:T(8,128)(2,1)S(1)} %get-tuple-element.105), channel_id=1, source_target_pairs={{0,16},{4,20},{8,24},{12,28},{16,0},{20,4},{24,8},{28,12},{1,17},{... | collective-permute-start | bytes 393224 | tf_op jit(solution)/shard_map/ppermute | solution.py:444
  22.1 3.7 %collective-permute-start.5 = (bf16[128,512]{1,0:T(8,128)(2,1)S(1)}, bf16[128,512]{1,0:T(8,128)(2,1)S(1)}, u32[]{:S(2)}, u32[]{:S(2)}) collective-permute-start(bf16[128,512]{1,0:T(8,128)(2,1)S(1)} %get-tuple-element.109), channel_id=1, source_target_pairs={{0,4},{4,0},{8,12},{12,8},{16,20},{20,16},{24,28},{28,24},{1,5},{5... | collective-permute-start | bytes 393224 | tf_op jit(solution)/shard_map/ppermute | solution.py:449
  25.7 2.1 %collective-permute-start.6 = (bf16[128,512]{1,0:T(8,128)(2,1)S(1)}, bf16[128,512]{1,0:T(8,128)(2,1)S(1)}, u32[]{:S(2)}, u32[]{:S(2)}) collective-permute-start(bf16[128,512]{1,0:T(8,128)(2,1)S(1)} %get-tuple-element.114), channel_id=1, source_target_pairs={{0,4},{4,0},{8,12},{12,8},{16,20},{20,16},{24,28},{28,24},{1,5},{5... | collective-permute-start | bytes 393224 | tf_op jit(solution)/shard_map/ppermute | solution.py:449

commit v7 on v6

--- a/solution.py
+++ b/solution.py
@@ -64,21 +64,19 @@
     return jnp.concatenate(pairs, axis=1)
 
 
-def project(jobs, heads, head_dim, normed, b_t, grow, fall_end):
+def project(first, w, xs_ref, s_ref, heads, head_dim, normed, b_t, grow, fall_end):
     width = b_t.shape[0]
     later = []
-    for first, w, x_ref, xs_ref, s_ref in jobs:
-        for j in range(x_ref.shape[1] // CHUNK):
-            cols = slice(j * CHUNK, (j + 1) * CHUNK)
-            spread = spread_heads(first + j * (CHUNK // head_dim), heads, head_dim)
-            x = dot(normed[...], compact(w, j, 0)).astype(BF)
-            scaled = (x.astype(F32) * dot(grow, spread)).astype(BF)
-            x_ref[:, cols] = x
-            xs_ref[:, cols] = scaled
-            decay = dot(fall_end, spread)[EXTRA - 1:EXTRA]
-            s_ref[width:width + EXTRA, cols] = decay_rows(decay)
-            later.append((s_ref, cols, scaled, decay))
-    for s_ref, cols, scaled, decay in later:
+    for j in range(xs_ref.shape[1] // CHUNK):
+        cols = slice(j * CHUNK, (j + 1) * CHUNK)
+        spread = spread_heads(first + j * (CHUNK // head_dim), heads, head_dim)
+        x = dot(normed[...], compact(w, j, 0)).astype(BF)
+        scaled = (x.astype(F32) * dot(grow, spread)).astype(BF)
+        xs_ref[:, cols] = scaled
+        decay = dot(fall_end, spread)[EXTRA - 1:EXTRA]
+        s_ref[width:width + EXTRA, cols] = decay_rows(decay)
+        later.append((cols, scaled, decay))
+    for cols, scaled, decay in later:
         s_ref[0:width, cols] = (dot(b_t, scaled) * decay).astype(BF)
 
 
@@ -118,7 +116,7 @@
 
 def encode_kernel(heads, head_dim, here_ref, cell_ref, frames_any, enc_in_any, bias_any, enc_out_any, pos_any, gain_any,
                   w_keys_any, w_step_any, step_bias_any, code_any, skip_any, out_gain_any, w_pair_any,
-                  encoded, normed, keys, b_t, grow, fall, skip, out_gain, x_o1, xs_o1, x_o2, xs_o2, s_o, w_o1, w_m1, w_o2, w_m2,
+                  encoded, normed, keys, b_t, grow, fall, skip, out_gain, xs_o1, s_o1, w_o1, w_m1, w_o2, w_m2,
                   frames, enc_in, bias, enc_out, pos, norm_gain, w_keys, w_step, step_bias, code, sem, wsem):
     half = 1 - here_ref[0] % 2
     cell = cell_ref[0]
@@ -129,7 +127,7 @@
     first = [in_pieces(src, dst, wsem, i) for i, (src, dst) in enumerate((
         (frames_any, frames), (enc_in_any, enc_in), (enc_out_any, enc_out), (w_keys_any, w_keys), (w_step_any, w_step)))]
     big = [in_pieces(group_columns(w_pair_any, dst, which, group), dst, wsem, 5 + i) for i, (which, group, dst) in enumerate((
-        (half, 0, w_o1), (half, 1, w_o2), (1 - half, 0, w_m1), (1 - half, 1, w_m2)))]
+        (half, 0, w_o1), (1 - half, 0, w_m1), (half, 1, w_o2), (1 - half, 1, w_m2)))]
     start_pieces(first[:2])
     for c in small:
         c.start()
@@ -188,12 +186,9 @@
     f = split_two(jnp.exp(cum), heads)
     grow[...] = g
     fall[...] = f
-    wait_pieces(big[:2])
-    size = x_o1.shape[1]
-    per = size // head_dim
-    project([(half * 2 * per, w_o1, x_o1, xs_o1, s_o.at[:, :size]), (half * 2 * per + per, w_o2, x_o2, xs_o2, s_o.at[:, size:])],
-            heads, head_dim, normed, b_t[...], g, f[rows - EXTRA:])
-    wait_pieces(big[2:])
+    wait_pieces(big[:1])
+    project(half * (heads // 2), w_o1, xs_o1, s_o1, heads, head_dim, normed, b_t[...], g, f[rows - EXTRA:])
+    wait_pieces(big[1:])
 
 
 def group_columns(w_any, like, half, group):
@@ -201,11 +196,11 @@
     return w_any.at[:, pl.ds(pl.multiple_of((half * 2 + group) * size, size), size)]
 
 
-def project_kernel(heads, head_dim, own, group, here_ref, normed, b_t, grow, fall, w, x_ref, xs_ref, s_ref):
+def project_kernel(heads, head_dim, own, group, here_ref, normed, b_t, grow, fall, w, xs_ref, s_ref):
     half = (here_ref[0] + 1 - own) % 2
     rows = normed.shape[0]
-    first = (half * 2 + group) * (x_ref.shape[1] // head_dim)
-    project([(first, w, x_ref, xs_ref, s_ref)], heads, head_dim, normed, b_t[...], grow[...], fall[rows - EXTRA:])
+    first = (half * 2 + group) * (xs_ref.shape[1] // head_dim)
+    project(first, w, xs_ref, s_ref, heads, head_dim, normed, b_t[...], grow[...], fall[rows - EXTRA:])
 
 
 def opened(ref):
@@ -220,10 +215,9 @@
     ref[width:, :] = decay_rows(decay)
 
 
-def total_kernel(group, here_ref, mine_ref, got_ref, total_ref):
-    size = mine_ref.shape[1]
+def total_kernel(here_ref, mine_ref, got_ref, total_ref):
     mine, mine_decay = opened(mine_ref)
-    got, got_decay = opened(got_ref.at[:, group * size:(group + 1) * size])
+    got, got_decay = opened(got_ref)
 
     @pl.when(here_ref[0] % 2 == 1)
     def _():
@@ -263,8 +257,7 @@
         put_total(got_decay * total + got)
 
 
-def last_kernel(reach, group, here_ref, got_ref, before_ref, mine_ref, first_ref, keep_ref, send_ref):
-    state_size = keep_ref.shape[1]
+def last_kernel(reach, here_ref, got_ref, before_ref, mine_ref, first_ref, keep_ref, send_ref):
     later = (here_ref[0] // reach) % 2 == 1
     got = got_ref[:keep_ref.shape[0], :].astype(F32)
     before, before_decay = opened(before_ref)
@@ -272,7 +265,7 @@
 
     @pl.when(here_ref[0] % 2 == 1)
     def _():
-        state, decay = opened(first_ref.at[:, group * state_size:(group + 1) * state_size])
+        state, decay = opened(first_ref)
         keep_ref[...] = (decay * before + state).astype(BF)
         send_ref[...] = before.astype(BF)
 
@@ -283,11 +276,11 @@
         keep_ref[...] = before.astype(BF)
 
 
-def inner_kernel(heads, head_dim, own, group, fresh, here_ref, normed, keys, fall, skip, w_out_any, w, x, xs, *refs):
+def inner_kernel(heads, head_dim, own, group, fresh, here_ref, normed, keys, fall, skip, w_out_any, w, xs, *refs):
     half = (here_ref[0] + 1 - own) % 2
     rows = keys.shape[0]
     width = keys.shape[1] // 2
-    size = x.shape[1]
+    size = xs.shape[1]
     if fresh:
         u, v, w_rows, scores_ref, sem = refs
     else:
@@ -310,11 +303,12 @@
         spread = spread_heads(first + j * (CHUNK // head_dim), heads, head_dim)
         gain = dot(skip_two, spread)[0:1]
         grown = dot(fall[...], spread)
-        u[:, cols] = (grown * gate).astype(BF)
+        grown = grown * gate
+        u[:, cols] = grown.astype(BF)
         top = dot(scores[:mid, :mid], xs[:mid, cols])
         low = dot(scores[mid:], xs[:, cols])
         for part, inner in ((slice(0, mid), top), (slice(mid, rows), low)):
-            v[part, cols] = ((grown[part] * inner + gain * x[part, cols].astype(F32)) * gate[part]).astype(BF)
+            v[part, cols] = (grown[part] * (inner + gain * xs[part, cols].astype(F32))).astype(BF)
     wait_pieces(copies)
 
 
@@ -377,9 +371,9 @@
     pair = lambda by: [(i, i ^ by) for i in range(peers)]
     after = lambda value, *first: lax.optimization_barrier((value,) + first)[0]
 
-    def call(kernel, name, outs, ins, scratch=(), macs=0, out_spec=VM):
+    def call(kernel, name, outs, ins, scratch=(), flops=0, out_spec=VM):
         specs = [spec for spec, _ in ins]
-        cost = pl.CostEstimate(flops=macs // 4, bytes_accessed=2**20, transcendentals=0)
+        cost = pl.CostEstimate(flops=flops, bytes_accessed=2**20, transcendentals=0)
         return pl.pallas_call(kernel, out_shape=tuple(outs), in_specs=specs, out_specs=(out_spec,) * len(outs),
                               scratch_shapes=list(scratch), compiler_params=params(24), name=name,
                               cost_estimate=cost)(*[v for _, v in ins])
@@ -389,11 +383,11 @@
     where = [(SM, here)]
 
     part, message, weight = near((rows, size)), near((width + EXTRA, size)), near((depth, 2 * size))
-    encoded, normed, keys, b_t, grow, fall, skip, gain, x_o1, xs_o1, x_o2, xs_o2, s_o, w_o1, w_m1, w_o2, w_m2 = call(
+    encoded, normed, keys, b_t, grow, fall, skip, gain, xs_o1, s_o1, w_o1, w_m1, w_o2, w_m2 = call(
         functools.partial(encode_kernel, heads, head_dim), "encode",
         (near((rows, depth)), near((rows, depth)), near((rows, 2 * width)), near((width, rows)),
          near((rows, 2 * heads)), near((rows, 2 * heads)), near((1, heads), F32), near((1, heads * head_dim), F32),
-         part, part, part, part, near((width + EXTRA, 2 * size))) + (weight,) * 4,
+         part, message) + (weight,) * 4,
         where + [(SM, patch_cell)] + hbm(frames.reshape(rows, pix), enc_in, row(enc_bias), enc_out, pos_table, row(norm_gain),
                                          w_keys, w_step.T, row(step_bias), row(decay_code), row(skip_gain), row(out_gain),
                                          w_pair),
@@ -402,17 +396,19 @@
          near((1, heads), jnp.int32), sems(7), pltpu.SemaphoreType.DMA((9, 2))],
         rows * depth * depth)
 
+    long, short = 8 * rows * depth * size, rows * depth * size // 4
+
     def projected(own, group, w):
         return call(functools.partial(project_kernel, heads, head_dim, own, group), "project",
-                    (part, part, message), where + vm(normed, b_t, grow, fall, w), (), rows * depth * size)
+                    (part, message), where + vm(normed, b_t, grow, fall, w), (), long)
 
     scores = []
 
-    def inner(own, group, w, x, xs):
+    def inner(own, group, w, xs, flops):
         outs = call(functools.partial(inner_kernel, heads, head_dim, own, group, not scores), "inner",
                     (part, part, near((size, depth))) + (() if scores else (near((rows, rows)),)),
-                    where + vm(normed, keys, fall, skip) + hbm(w_out) + vm(w, x, xs, *scores),
-                    [pltpu.SemaphoreType.DMA((1, 2))], rows * depth * size)
+                    where + vm(normed, keys, fall, skip) + hbm(w_out) + vm(w, xs, *scores),
+                    [pltpu.SemaphoreType.DMA((1, 2))], flops)
         scores.extend(outs[3:])
         return outs[:3]
 
@@ -421,18 +417,18 @@
         shape = sds((rows, depth), BF) if last else near((rows, depth), F32)
         return call(functools.partial(mix_kernel, head_dim, places, last), "mix", (shape,),
                     where + vm(keys, base, gain, *states, *us, *vs, *ws),
-                    [near((rows, depth)), sems(depth // CHUNK)] if last else [], len(places) * rows * depth * size,
+                    [near((rows, depth)), sems(depth // CHUNK)] if last else [], short,
                     ANY if last else VM)[0]
 
     totals, befores, arriving = [None, None], [None, None], [None, None]
     done = {}
 
-    def work(own, group, w, x, xs, stamp):
-        done[own, group] = inner(own, group, w, after(x, stamp), xs)
+    def work(own, group, w, xs, stamp, flops):
+        done[own, group] = inner(own, group, w, after(xs, stamp), flops)
         return done[own, group][0]
 
-    def start_total(i, mine):
-        totals[i], = call(functools.partial(total_kernel, i), "total", (message,), where + vm(mine, got))
+    def start_total(i, mine, theirs):
+        totals[i], = call(total_kernel, "total", (message,), where + vm(mine, theirs))
         befores[i] = totals[i]
         arriving[i] = lax.ppermute(totals[i], "tm", pair(2))
 
@@ -443,30 +439,32 @@
             (message, near((width, size)) if final else message), where + vm(totals[i], arrived, befores[i]))
         arriving[i] = lax.ppermute(totals[i], "tm", pair(2 * reach))
 
-    def finish(i, arrived, mine):
-        keep, send = call(functools.partial(last_kernel, peers // 2, i), "last", (near((width, size)),) * 2,
-                          where + vm(arrived, befores[i], mine, got))
+    def finish(i, arrived, mine, theirs):
+        keep, send = call(functools.partial(last_kernel, peers // 2), "last", (near((width, size)),) * 2,
+                          where + vm(arrived, befores[i], mine, theirs))
         return keep, lax.ppermute(send, "tm", pair(1))
 
-    got = lax.ppermute(s_o, "tm", pair(1))
-    x_m1, xs_m1, s_m1 = projected(1, 0, w_m1)
-    start_total(0, s_m1)
-    x_m2, xs_m2, s_m2 = projected(1, 1, after(w_m2, totals[0]))
-    stamp = work(0, 0, w_o1, x_o1, xs_o1, s_m2)
-    start_total(1, after(s_m2, stamp))
-    advance(0, 2, after(arriving[0], totals[1]))
-    stamp = work(1, 0, w_m1, x_m1, xs_m1, befores[0])
-    stamp = work(1, 1, w_m2, x_m2, xs_m2, stamp)
+    got_1 = lax.ppermute(s_o1, "tm", pair(1))
+    xs_m1, s_m1 = projected(1, 0, w_m1)
+    start_total(0, s_m1, got_1)
+    xs_o2, s_o2 = projected(0, 1, after(w_o2, totals[0]))
+    got_2 = lax.ppermute(s_o2, "tm", pair(1))
+    xs_m2, s_m2 = projected(1, 1, after(w_m2, s_o2))
+    start_total(1, s_m2, got_2)
+    stamp = work(0, 0, w_o1, xs_o1, totals[1], long)
+    advance(0, 2, after(arriving[0], stamp))
+    stamp = work(1, 0, w_m1, xs_m1, befores[0], short)
+    stamp = work(1, 1, w_m2, xs_m2, stamp, short)
     advance(1, 2, after(arriving[1], stamp))
     reach = 4
     while reach * 2 < peers:
         for i in range(2):
             advance(i, reach, arriving[i])
         reach *= 2
-    keep_1, sent_1 = finish(0, after(arriving[0], befores[1]), s_m1)
-    stamp = work(0, 1, w_o2, x_o2, xs_o2, keep_1)
+    keep_1, sent_1 = finish(0, after(arriving[0], befores[1]), s_m1, got_1)
+    stamp = work(0, 1, w_o2, xs_o2, keep_1, short)
     mixing = mixed(((1, 0),), after(encoded, stamp), False, (keep_1, *done[1, 0]))
-    keep_2, sent_2 = finish(1, after(arriving[1], mixing), s_m2)
+    keep_2, sent_2 = finish(1, after(arriving[1], mixing), s_m2, got_2)
     mixing = mixed(((0, 0), (1, 1)), after(mixing, keep_2), False, (sent_1, *done[0, 0]), (keep_2, *done[1, 1]))
     return mixed(((0, 1),), mixing, True, (sent_2, *done[0, 1])).reshape(rows, 1, depth)
 

time: 30.2 us -> 29.2 us (0.967)
  waiting for transfers between devices: 2.8 us -> 1.44 us
  starting transfers between devices: 6.75 us -> 7.08 us
    ppermute x2, waiting for transfers between devices: 1.55 us -> 0.27 us  [start_total(): arriving[i] = lax.ppermute(totals[i], 'tm', pair(2))]
    ppermute x2, starting transfers between devices: 3.09 us -> 3.43 us  [advance(): arriving[i] = lax.ppermute(totals[i], 'tm', pair(2 * reach))]
    pallas_call x16 -> x17, Pallas kernels: 19.4 us -> 19.5 us  [call(): pl.pallas_call(kernel, out_shape=tuple(outs), in_specs=specs, out_specs=(...]
  transfers between devices with their start and end apart: 7 -> 8, of which waited for: 3 -> 3; matrix products, arithmetic and copies ran while one was open for 0% -> 0% of each run, Pallas kernels for 36% -> 41%
where the time goes in v7:
time: 29.2 us; the launch traced here: 29 us
  Pallas kernels  19.5 us (67%)
  starting transfers between devices  7.08 us (24%)
  waiting for transfers between devices  1.44 us (5%)
  between operations  0.96 us (3%)
    pallas_call x17, Pallas kernels, call(): pl.pallas_call(kernel, out_shape=tuple(outs), in_specs=specs, out_specs=(...  19.5 us
    ppermute x2, starting transfers between devices, advance(): arriving[i] = lax.ppermute(totals[i], 'tm', pair(2 * reach))  3.43 us
    ppermute x2, starting transfers between devices, start_total(): arriving[i] = lax.ppermute(totals[i], 'tm', pair(2))  2.92 us
    ppermute x2, waiting for transfers between devices, advance(): arriving[i] = lax.ppermute(totals[i], 'tm', pair(2 * reach))  0.88 us
  transfers between devices with their start and end apart: 8, of which 3 were waited for; matrix products, arithmetic and copies ran while one was open for 0% of the time, Pallas kernels for 41%

profile of v7, /device:TPU:0, one launch (start us, length us, event | category | flops | bytes accessed | tf_op | source)
XLA Modules:
  0.0 29.0 jit_solution(4089038903976663374)
XLA Ops:
  0.7 5.6 %encode.1 = (bf16[512,1024]{1,0:T(8,128)(2,1)S(1)}, bf16[512,1024]{1,0:T(8,128)(2,1)S(1)}, bf16[512,256]{1,0:T(8,128)(2,1)S(1)}, bf16[128,512]{1,0:T(8,128)(2,1)...) custom-call(s32[1]{0:T(128)} %bitcast.here_ref, ...), custom_call_target="tpu_custom_call" | custom-call | flops 536870912 | bytes 1048576 | tf_op jit(solution)/shard_map/encode/pallas_call | solution.py:377
  6.3 0.5 %collective-permute-start = (bf16[144,512]{1,0:T(8,128)(2,1)S(1)}, bf16[144,512]{1,0:T(8,128)(2,1)S(1)}, u32[]{:S(2)}, u32[]{:S(2)}) collective-permute-start(bf16[144,512]{1,0:T(8,128)(2,1)S(1)} %get-tuple-element.68), channel_id=1, source_target_pairs={{0,4},{4,0},{8,12},{12,8},{16,20},{20,16},{24,28},{28,24},{1,5},{5... | collective-permute-start | bytes 442376 | tf_op jit(solution)/shard_map/ppermute | solution.py:447
  6.8 1.1 %project.3 = (bf16[512,512]{1,0:T(8,128)(2,1)S(1)}, bf16[144,512]{1,0:T(8,128)(2,1)S(1)}) custom-call(s32[1]{0:T(128)} %bitcast.here_ref, bf16[512,1024]{1,0:T(8,128)(2,1)S(1)} %get-tuple-element.60.normed, bf16[128,512]{1,0:T(8,128)(2,1)S(1)} %get-tuple-element.64.b_t, bf16[512,64]{1,0:T(8,128)(2,1)S(1)} %get-tuple-element.65.grow, ...), custom_call_target="tpu_custom_call" | custom-call | flops 2147483648 | bytes 1048576 | tf_op jit(solution)/shard_map/project/pallas_call | solution.py:377
  7.9 0.0 collective-permute-done.got_ref.first_ref
  7.9 0.1 total.2.total_ref.before_ref
  8.0 2.8 %collective-permute-start.1 = (bf16[144,512]{1,0:T(8,128)(2,1)S(1)}, bf16[144,512]{1,0:T(8,128)(2,1)S(1)}, u32[]{:S(2)}, u32[]{:S(2)}) collective-permute-start(bf16[144,512]{1,0:T(8,128)(2,1)S(1)} %total.2.total_ref.before_ref), channel_id=1, source_target_pairs={{0,8},{4,12},{8,0},{12,4},{16,24},{20,28},{24,16},{28,20},{1,9},{5... | collective-permute-start | bytes 442376 | tf_op jit(solution)/shard_map/ppermute | solution.py:433
  10.8 1.1 %project.4 = (bf16[512,512]{1,0:T(8,128)(2,1)S(1)}, bf16[144,512]{1,0:T(8,128)(2,1)S(1)}) custom-call(s32[1]{0:T(128)} %bitcast.here_ref, bf16[512,1024]{1,0:T(8,128)(2,1)S(1)} %get-tuple-element.60.normed, bf16[128,512]{1,0:T(8,128)(2,1)S(1)} %get-tuple-element.64.b_t, bf16[512,64]{1,0:T(8,128)(2,1)S(1)} %get-tuple-element.65.grow, ...), custom_call_target="tpu_custom_call" | custom-call | flops 2147483648 | bytes 1048576 | tf_op jit(solution)/shard_map/project/pallas_call | solution.py:377
  11.9 0.1 collective-permute-start.2
  12.0 1.1 %project.5 = (bf16[512,512]{1,0:T(8,128)(2,1)S(1)}, bf16[144,512]{1,0:T(8,128)(2,1)S(1)}) custom-call(s32[1]{0:T(128)} %bitcast.here_ref, bf16[512,1024]{1,0:T(8,128)(2,1)S(1)} %get-tuple-element.60.normed, bf16[128,512]{1,0:T(8,128)(2,1)S(1)} %get-tuple-element.64.b_t, bf16[512,64]{1,0:T(8,128)(2,1)S(1)} %get-tuple-element.65.grow, ...), custom_call_target="tpu_custom_call" | custom-call | flops 2147483648 | bytes 1048576 | tf_op jit(solution)/shard_map/project/pallas_call | solution.py:377
  13.0 0.3 collective-permute-done.2.got_ref.first_ref
  13.3 0.1 total.3.total_ref.before_ref
  13.4 0.1 collective-permute-start.4
  13.5 1.3 %inner.4 = (bf16[512,512]{1,0:T(8,128)(2,1)S(1)}, bf16[512,512]{1,0:T(8,128)(2,1)S(1)}, bf16[512,1024]{1,0:T(8,128)(2,1)S(1)}, bf16[512,512]{1,0:T(8,128)(2,1)S(1)}) custom-call(s32[1]{0:T(128)} %bitcast.here_ref, bf16[512,1024]{1,0:T(8,128)(2,1)S(1)} %get-tuple-element.60.normed, bf16[512,256]{1,0:T(8,128)(2,1)S(1)} %get-tuple-element.58.keys, ...), custom_call_target="tpu_custom_call" | custom-call | flops 2147483648 | bytes 1048576 | tf_op jit(solution)/shard_map/inner/pallas_call | solution.py:377
  14.8 0.3 collective-permute-done.1.got_ref
  15.1 0.1 step.2
  15.1 1.8 %collective-permute-start.3 = (bf16[128,512]{1,0:T(8,128)(2,1)S(1)}, bf16[128,512]{1,0:T(8,128)(2,1)S(1)}, u32[]{:S(2)}, u32[]{:S(2)}) collective-permute-start(bf16[128,512]{1,0:T(8,128)(2,1)S(1)} %get-tuple-element.80), channel_id=1, source_target_pairs={{0,16},{4,20},{8,24},{12,28},{16,0},{20,4},{24,8},{28,12},{1,17},{... | collective-permute-start | bytes 393224 | tf_op jit(solution)/shard_map/ppermute | solution.py:440
  17.0 1.2 %inner.5 = (bf16[512,512]{1,0:T(8,128)(2,1)S(1)}, bf16[512,512]{1,0:T(8,128)(2,1)S(1)}, bf16[512,1024]{1,0:T(8,128)(2,1)S(1)}) custom-call(s32[1]{0:T(128)} %bitcast.here_ref, bf16[512,1024]{1,0:T(8,128)(2,1)S(1)} %get-tuple-element.60.normed, bf16[512,256]{1,0:T(8,128)(2,1)S(1)} %get-tuple-element.58.keys, bf16[512,64]{1,0:T(8,128)(2,1)S(1)} %get-tuple-element.61.fall, ...), custom_call_target="tpu_custom_call" | custom-call | flops 67108864 | bytes 1048576 | tf_op jit(solution)/shard_map/inner/pallas_call | solution.py:377
  18.2 1.2 %inner.6 = (bf16[512,512]{1,0:T(8,128)(2,1)S(1)}, bf16[512,512]{1,0:T(8,128)(2,1)S(1)}, bf16[512,1024]{1,0:T(8,128)(2,1)S(1)}) custom-call(s32[1]{0:T(128)} %bitcast.here_ref, bf16[512,1024]{1,0:T(8,128)(2,1)S(1)} %get-tuple-element.60.normed, bf16[512,256]{1,0:T(8,128)(2,1)S(1)} %get-tuple-element.58.keys, bf16[512,64]{1,0:T(8,128)(2,1)S(1)} %get-tuple-element.61.fall, ...), custom_call_target="tpu_custom_call" | custom-call | flops 67108864 | bytes 1048576 | tf_op jit(solution)/shard_map/inner/pallas_call | solution.py:377
  19.4 0.0 collective-permute-done.4.got_ref
  19.4 0.1 step.3
  19.5 1.6 %collective-permute-start.5 = (bf16[128,512]{1,0:T(8,128)(2,1)S(1)}, bf16[128,512]{1,0:T(8,128)(2,1)S(1)}, u32[]{:S(2)}, u32[]{:S(2)}) collective-permute-start(bf16[128,512]{1,0:T(8,128)(2,1)S(1)} %get-tuple-element.99), channel_id=1, source_target_pairs={{0,16},{4,20},{8,24},{12,28},{16,0},{20,4},{24,8},{28,12},{1,17},{... | collective-permute-start | bytes 393224 | tf_op jit(solution)/shard_map/ppermute | solution.py:440
  21.1 0.0 collective-permute-done.3.got_ref
  21.1 0.3 last.2
  21.4 1.2 %inner.7 = (bf16[512,512]{1,0:T(8,128)(2,1)S(1)}, bf16[512,512]{1,0:T(8,128)(2,1)S(1)}, bf16[512,1024]{1,0:T(8,128)(2,1)S(1)}) custom-call(s32[1]{0:T(128)} %bitcast.here_ref, bf16[512,1024]{1,0:T(8,128)(2,1)S(1)} %get-tuple-element.60.normed, bf16[512,256]{1,0:T(8,128)(2,1)S(1)} %get-tuple-element.58.keys, bf16[512,64]{1,0:T(8,128)(2,1)S(1)} %get-tuple-element.61.fall, ...), custom_call_target="tpu_custom_call" | custom-call | flops 67108864 | bytes 1048576 | tf_op jit(solution)/shard_map/inner/pallas_call | solution.py:377
  22.6 0.1 collective-permute-start.6
  22.7 1.1 %mix.3.base = f32[512,1024]{1,0:T(8,128)S(1)} custom-call(s32[1]{0:T(128)} %bitcast.here_ref, bf16[512,256]{1,0:T(8,128)(2,1)S(1)} %get-tuple-element.58.keys, bf16[512,1024]{1,0:T(8,128)(2,1)S(1)} %get-tuple-element.95.base, f32[1,2048]{1,0:T(1,128)S(1)} %get-tuple-element.96.gain, bf16[128,512]{1,0:T(8,128)(2,1)S(1)} %get-tuple-element.92.refs_0_, ...), custom_call_target="tpu_custom_call" | custom-call | flops 67108864 | bytes 1048576 | tf_op jit(solution)/shard_map/mix/pallas_call | solution.py:377
  23.8 0.9 %collective-permute-done.5.got_ref = bf16[128,512]{1,0:T(8,128)(2,1)S(1)} collective-permute-done((bf16[128,512]{1,0:T(8,128)(2,1)S(1)}, bf16[128,512]{1,0:T(8,128)(2,1)S(1)}, u32[]{:S(2)}, u32[]{:S(2)}) %collective-permute-start.5) | collective-permute-done | bytes 131104 | tf_op jit(solution)/shard_map/ppermute | solution.py:440
  24.6 0.1 last.3
  24.7 0.1 collective-permute-start.7
  24.8 0.0 collective-permute-done.6.refs_0_
  24.8 2.0 %mix.4.base = f32[512,1024]{1,0:T(8,128)S(1)} custom-call(s32[1]{0:T(128)} %bitcast.here_ref, bf16[512,256]{1,0:T(8,128)(2,1)S(1)} %get-tuple-element.58.keys, f32[512,1024]{1,0:T(8,128)S(1)} %mix.3.base, f32[1,2048]{1,0:T(1,128)S(1)} %get-tuple-element.96.gain, bf16[128,512]{1,0:T(8,128)(2,1)S(1)} %collective-permute-done.6.refs_0_, ...), custom_call_target="tpu_custom_call" | custom-call | flops 67108864 | bytes 1048576 | tf_op jit(solution)/shard_map/mix/pallas_call | solution.py:377
  26.9 0.0 collective-permute-done.7.refs_0_
  26.9 1.9 %mix.5 = bf16[512,1024]{1,0:T(8,128)(2,1)} custom-call(s32[1]{0:T(128)} %bitcast.here_ref, bf16[512,256]{1,0:T(8,128)(2,1)S(1)} %get-tuple-element.58.keys, f32[512,1024]{1,0:T(8,128)S(1)} %mix.4.base, f32[1,2048]{1,0:T(1,128)S(1)} %get-tuple-element.96.gain, bf16[128,512]{1,0:T(8,128)(2,1)S(1)} %collective-permute-done.7.refs_0_, ...), custom_call_target="tpu_custom_call" | custom-call | flops 67108864 | bytes 1048576 | tf_op jit(solution)/shard_map/mix/pallas_call | solution.py:377
Async XLA Ops:
  6.3 1.6 %collective-permute-start = (bf16[144,512]{1,0:T(8,128)(2,1)S(1)}, bf16[144,512]{1,0:T(8,128)(2,1)S(1)}, u32[]{:S(2)}, u32[]{:S(2)}) collective-permute-start(bf16[144,512]{1,0:T(8,128)(2,1)S(1)} %get-tuple-element.68), channel_id=1, source_target_pairs={{0,4},{4,0},{8,12},{12,8},{16,20},{20,16},{24,28},{28,24},{1,5},{5... | collective-permute-start | bytes 442376 | tf_op jit(solution)/shard_map/ppermute | solution.py:447
  8.0 7.1 %collective-permute-start.1 = (bf16[144,512]{1,0:T(8,128)(2,1)S(1)}, bf16[144,512]{1,0:T(8,128)(2,1)S(1)}, u32[]{:S(2)}, u32[]{:S(2)}) collective-permute-start(bf16[144,512]{1,0:T(8,128)(2,1)S(1)} %total.2.total_ref.before_ref), channel_id=1, source_target_pairs={{0,8},{4,12},{8,0},{12,4},{16,24},{20,28},{24,16},{28,20},{1,9},{5... | collective-permute-start | bytes 442376 | tf_op jit(solution)/shard_map/ppermute | solution.py:433
  11.9 1.4 %collective-permute-start.2 = (bf16[144,512]{1,0:T(8,128)(2,1)S(1)}, bf16[144,512]{1,0:T(8,128)(2,1)S(1)}, u32[]{:S(2)}, u32[]{:S(2)}) collective-permute-start(bf16[144,512]{1,0:T(8,128)(2,1)S(1)} %get-tuple-element.74), channel_id=1, source_target_pairs={{0,4},{4,0},{8,12},{12,8},{16,20},{20,16},{24,28},{28,24},{1,5},{5... | collective-permute-start | bytes 442376 | tf_op jit(solution)/shard_map/ppermute | solution.py:451
  13.4 6.0 %collective-permute-start.4 = (bf16[144,512]{1,0:T(8,128)(2,1)S(1)}, bf16[144,512]{1,0:T(8,128)(2,1)S(1)}, u32[]{:S(2)}, u32[]{:S(2)}) collective-permute-start(bf16[144,512]{1,0:T(8,128)(2,1)S(1)} %total.3.total_ref.before_ref), channel_id=1, source_target_pairs={{0,8},{4,12},{8,0},{12,4},{16,24},{20,28},{24,16},{28,20},{1,9},{5... | collective-permute-start | bytes 442376 | tf_op jit(solution)/shard_map/ppermute | solution.py:433
  15.1 6.0 %collective-permute-start.3 = (bf16[128,512]{1,0:T(8,128)(2,1)S(1)}, bf16[128,512]{1,0:T(8,128)(2,1)S(1)}, u32[]{:S(2)}, u32[]{:S(2)}) collective-permute-start(bf16[128,512]{1,0:T(8,128)(2,1)S(1)} %get-tuple-element.80), channel_id=1, source_target_pairs={{0,16},{4,20},{8,24},{12,28},{16,0},{20,4},{24,8},{28,12},{1,17},{... | collective-permute-start | bytes 393224 | tf_op jit(solution)/shard_map/ppermute | solution.py:440
  19.5 5.1 %collective-permute-start.5 = (bf16[128,512]{1,0:T(8,128)(2,1)S(1)}, bf16[128,512]{1,0:T(8,128)(2,1)S(1)}, u32[]{:S(2)}, u32[]{:S(2)}) collective-permute-start(bf16[128,512]{1,0:T(8,128)(2,1)S(1)} %get-tuple-element.99), channel_id=1, source_target_pairs={{0,16},{4,20},{8,24},{12,28},{16,0},{20,4},{24,8},{28,12},{1,17},{... | collective-permute-start | bytes 393224 | tf_op jit(solution)/shard_map/ppermute | solution.py:440
  22.6 2.2 %collective-permute-start.6 = (bf16[128,512]{1,0:T(8,128)(2,1)S(1)}, bf16[128,512]{1,0:T(8,128)(2,1)S(1)}, u32[]{:S(2)}, u32[]{:S(2)}) collective-permute-start(bf16[128,512]{1,0:T(8,128)(2,1)S(1)} %get-tuple-element.103), channel_id=1, source_target_pairs={{0,4},{4,0},{8,12},{12,8},{16,20},{20,16},{24,28},{28,24},{1,5},{5... | collective-permute-start | bytes 393224 | tf_op jit(solution)/shard_map/ppermute | solution.py:445
  24.7 2.1 %collective-permute-start.7 = (bf16[128,512]{1,0:T(8,128)(2,1)S(1)}, bf16[128,512]{1,0:T(8,128)(2,1)S(1)}, u32[]{:S(2)}, u32[]{:S(2)}) collective-permute-start(bf16[128,512]{1,0:T(8,128)(2,1)S(1)} %get-tuple-element.108), channel_id=1, source_target_pairs={{0,4},{4,0},{8,12},{12,8},{16,20},{20,16},{24,28},{28,24},{1,5},{5... | collective-permute-start | bytes 393224 | tf_op jit(solution)/shard_map/ppermute | solution.py:445

commit v8 on v7

--- a/solution.py
+++ b/solution.py
@@ -74,16 +74,22 @@
         scaled = (x.astype(F32) * dot(grow, spread)).astype(BF)
         xs_ref[:, cols] = scaled
         decay = dot(fall_end, spread)[EXTRA - 1:EXTRA]
-        s_ref[width:width + EXTRA, cols] = decay_rows(decay)
+        if s_ref.shape[0] > width:
+            next_first = first + (xs_ref.shape[1] + j * CHUNK) // head_dim
+            next_decay = dot(fall_end, spread_heads(next_first, heads, head_dim))[EXTRA - 1:EXTRA]
+            s_ref[width:width + EXTRA, cols] = decay_rows((decay, next_decay))
         later.append((cols, scaled, decay))
     for cols, scaled, decay in later:
         s_ref[0:width, cols] = (dot(b_t, scaled) * decay).astype(BF)
 
 
-def decay_rows(decay):
-    high = decay.astype(BF).astype(F32)
-    row = iota((EXTRA, decay.shape[1]), 0)
-    return jnp.where(row == 0, high, jnp.where(row == 1, decay - high, 0.0)).astype(BF)
+def decay_rows(values):
+    row = iota((EXTRA, values[0].shape[1]), 0)
+    out = jnp.zeros(row.shape, F32)
+    for k, value in enumerate(values):
+        high = value.astype(BF).astype(F32)
+        out = jnp.where(row == 2 * k, high, jnp.where(row == 2 * k + 1, value - high, out))
+    return out.astype(BF)
 
 
 def in_pieces(src, dst, sem, slot):
@@ -203,76 +209,82 @@
     project(first, w, xs_ref, s_ref, heads, head_dim, normed, b_t[...], grow[...], fall[rows - EXTRA:])
 
 
-def opened(ref):
-    width = ref.shape[0] - EXTRA
-    tail = ref[width:, :].astype(F32)
-    return ref[:width, :].astype(F32), tail[0:1] + tail[1:2]
-
-
-def close(ref, state, decay):
-    width = ref.shape[0] - EXTRA
+def state_of(ref, width):
+    return ref[:width, :].astype(F32)
+
+
+def decays_of(ref):
+    tail = ref[ref.shape[0] - EXTRA:, :].astype(F32)
+    return tail[0:1] + tail[1:2], tail[2:3] + tail[3:4]
+
+
+def put(ref, width, state, decays):
     ref[:width, :] = state.astype(BF)
-    ref[width:, :] = decay_rows(decay)
-
-
-def total_kernel(here_ref, mine_ref, got_ref, total_ref):
-    mine, mine_decay = opened(mine_ref)
-    got, got_decay = opened(got_ref)
+    if ref.shape[0] > width:
+        ref[width:, :] = decay_rows(decays)
+
+
+def times(one, other):
+    return one[0] * other[0], one[1] * other[1]
+
+
+def total_kernel(group, width, here_ref, mine_ref, got_ref, mine_first, got_first, total_ref):
+    mine, got = state_of(mine_ref, width), state_of(got_ref, width)
+    mine_decays, got_decays = decays_of(mine_first), decays_of(got_first)
+    both = times(mine_decays, got_decays)
 
     @pl.when(here_ref[0] % 2 == 1)
     def _():
-        close(total_ref, mine_decay * got + mine, mine_decay * got_decay)
+        put(total_ref, width, mine_decays[group] * got + mine, both)
 
     @pl.when(here_ref[0] % 2 == 0)
     def _():
-        close(total_ref, got_decay * mine + got, mine_decay * got_decay)
-
-
-def step_kernel(first, final, reach, here_ref, total_ref, got_ref, before_ref, new_before_ref, new_total_ref):
+        put(total_ref, width, got_decays[group] * mine + got, both)
+
+
+def step_kernel(group, width, reach, here_ref, total_ref, got_ref, total_first, got_first, *refs):
+    begin = len(refs) == 2
+    new_before_ref, new_total_ref = refs[-2:]
     later = (here_ref[0] // reach) % 2 == 1
-    got, got_decay = opened(got_ref)
-    total, total_decay = opened(total_ref)
-
-    def put_total(value):
-        if final:
-            new_total_ref[...] = value.astype(BF)
+    got, total = state_of(got_ref, width), state_of(total_ref, width)
+    got_decays, total_decays = decays_of(got_first), decays_of(total_first)
+    both = times(total_decays, got_decays)
+
+    @pl.when(later)
+    def _():
+        if begin:
+            put(new_before_ref, width, got, got_decays)
         else:
-            close(new_total_ref, value, total_decay * got_decay)
-
-    @pl.when(later)
-    def _():
-        if first:
-            close(new_before_ref, got, got_decay)
+            before_decays = decays_of(refs[1])
+            put(new_before_ref, width, state_of(refs[0], width) + before_decays[group] * got,
+                times(before_decays, got_decays))
+        put(new_total_ref, width, total_decays[group] * got + total, both)
+
+    @pl.when(jnp.logical_not(later))
+    def _():
+        if begin:
+            one = jnp.ones_like(got_decays[0])
+            put(new_before_ref, width, jnp.zeros_like(got), (one, one))
         else:
-            before, before_decay = opened(before_ref)
-            close(new_before_ref, before + before_decay * got, before_decay * got_decay)
-        put_total(total_decay * got + total)
-
-    @pl.when(jnp.logical_not(later))
-    def _():
-        if first:
-            close(new_before_ref, jnp.zeros_like(got), jnp.ones_like(got_decay))
-        else:
-            new_before_ref[...] = before_ref[...]
-        put_total(got_decay * total + got)
-
-
-def last_kernel(reach, here_ref, got_ref, before_ref, mine_ref, first_ref, keep_ref, send_ref):
+            put(new_before_ref, width, state_of(refs[0], width), decays_of(refs[1]))
+        put(new_total_ref, width, got_decays[group] * total + got, both)
+
+
+def last_kernel(group, reach, here_ref, got_ref, before_ref, before_first, mine_ref, theirs_ref, mine_first, theirs_first,
+                keep_ref, send_ref):
+    width = keep_ref.shape[0]
     later = (here_ref[0] // reach) % 2 == 1
-    got = got_ref[:keep_ref.shape[0], :].astype(F32)
-    before, before_decay = opened(before_ref)
-    before = before + jnp.where(later, before_decay, 0.0) * got
+    before_decay = jnp.where(later, decays_of(before_first)[group], 0.0)
+    before = state_of(before_ref, width) + before_decay * state_of(got_ref, width)
 
     @pl.when(here_ref[0] % 2 == 1)
     def _():
-        state, decay = opened(first_ref)
-        keep_ref[...] = (decay * before + state).astype(BF)
+        keep_ref[...] = (decays_of(theirs_first)[group] * before + state_of(theirs_ref, width)).astype(BF)
         send_ref[...] = before.astype(BF)
 
     @pl.when(here_ref[0] % 2 == 0)
     def _():
-        state, decay = opened(mine_ref)
-        send_ref[...] = (decay * before + state).astype(BF)
+        send_ref[...] = (decays_of(mine_first)[group] * before + state_of(mine_ref, width)).astype(BF)
         keep_ref[...] = before.astype(BF)
 
 
@@ -383,6 +395,7 @@
     where = [(SM, here)]
 
     part, message, weight = near((rows, size)), near((width + EXTRA, size)), near((depth, 2 * size))
+    kinds = (message, near((width, size)))
     encoded, normed, keys, b_t, grow, fall, skip, gain, xs_o1, s_o1, w_o1, w_m1, w_o2, w_m2 = call(
         functools.partial(encode_kernel, heads, head_dim), "encode",
         (near((rows, depth)), near((rows, depth)), near((rows, 2 * width)), near((width, rows)),
@@ -400,7 +413,7 @@
 
     def projected(own, group, w):
         return call(functools.partial(project_kernel, heads, head_dim, own, group), "project",
-                    (part, message), where + vm(normed, b_t, grow, fall, w), (), long)
+                    (part, kinds[group]), where + vm(normed, b_t, grow, fall, w), (), long)
 
     scores = []
 
@@ -420,7 +433,7 @@
                     [near((rows, depth)), sems(depth // CHUNK)] if last else [], short,
                     ANY if last else VM)[0]
 
-    totals, befores, arriving = [None, None], [None, None], [None, None]
+    totals, befores, arriving, firsts = [None, None], [None, None], [None, None], {}
     done = {}
 
     def work(own, group, w, xs, stamp, flops):
@@ -428,20 +441,24 @@
         return done[own, group][0]
 
     def start_total(i, mine, theirs):
-        totals[i], = call(total_kernel, "total", (message,), where + vm(mine, theirs))
-        befores[i] = totals[i]
+        totals[i], = call(functools.partial(total_kernel, i, width), "total", (kinds[i],),
+                          where + vm(mine, theirs, s_m1, got_1))
         arriving[i] = lax.ppermute(totals[i], "tm", pair(2))
 
     def advance(i, reach, arrived):
+        if i == 0:
+            firsts[reach] = totals[0], arrived, befores[0]
+        own, theirs, before = firsts[reach]
+        carried = [] if reach == 2 else [befores[i], before]
         final = reach * 4 >= peers
         befores[i], totals[i] = call(
-            functools.partial(step_kernel, reach == 2, final, reach), "step",
-            (message, near((width, size)) if final else message), where + vm(totals[i], arrived, befores[i]))
+            functools.partial(step_kernel, i, width, reach), "step", (kinds[i], kinds[1] if final else kinds[i]),
+            where + vm(totals[i], arrived, own, theirs, *carried))
         arriving[i] = lax.ppermute(totals[i], "tm", pair(2 * reach))
 
     def finish(i, arrived, mine, theirs):
-        keep, send = call(functools.partial(last_kernel, peers // 2), "last", (near((width, size)),) * 2,
-                          where + vm(arrived, befores[i], mine, theirs))
+        keep, send = call(functools.partial(last_kernel, i, peers // 2), "last", (kinds[1],) * 2,
+                          where + vm(arrived, befores[i], befores[0], mine, theirs, s_m1, got_1))
         return keep, lax.ppermute(send, "tm", pair(1))
 
     got_1 = lax.ppermute(s_o1, "tm", pair(1))

time: 29.2 us -> 29.2 us (level)
  starting transfers between devices: 7.08 us -> 6.72 us
  waiting for transfers between devices: 1.44 us -> 1.78 us
    ppermute x2, starting transfers between devices: 3.43 us -> 3.07 us  [advance(): arriving[i] = lax.ppermute(totals[i], 'tm', pair(2 * reach))]
    ppermute x2, waiting for transfers between devices: 0.88 us -> 1.21 us  [advance(): arriving[i] = lax.ppermute(totals[i], 'tm', pair(2 * reach))]
where the time goes in v8:
time: 29.2 us; the launch traced here: 29 us
  Pallas kernels  19.5 us (67%)
  starting transfers between devices  6.72 us (23%)
  waiting for transfers between devices  1.78 us (6%)
  between operations  0.97 us (3%)
    pallas_call x17, Pallas kernels, call(): pl.pallas_call(kernel, out_shape=tuple(outs), in_specs=specs, out_specs=(...  19.5 us
    ppermute x2, starting transfers between devices, advance(): arriving[i] = lax.ppermute(totals[i], 'tm', pair(2 * reach))  3.07 us
    ppermute x2, starting transfers between devices, start_total(): arriving[i] = lax.ppermute(totals[i], 'tm', pair(2))  2.92 us
    ppermute x2, waiting for transfers between devices, advance(): arriving[i] = lax.ppermute(totals[i], 'tm', pair(2 * reach))  1.21 us
  transfers between devices with their start and end apart: 8, of which 3 were waited for; matrix products, arithmetic and copies ran while one was open for 0% of the time, Pallas kernels for 41%

profile of v8, /device:TPU:0, one launch (start us, length us, event | category | flops | bytes accessed | tf_op | source)
XLA Modules:
  0.0 29.0 jit_solution(12557449993299234952)
XLA Ops:
  0.7 5.6 %encode.1 = (bf16[512,1024]{1,0:T(8,128)(2,1)S(1)}, bf16[512,1024]{1,0:T(8,128)(2,1)S(1)}, bf16[512,256]{1,0:T(8,128)(2,1)S(1)}, bf16[128,512]{1,0:T(8,128)(2,1)...) custom-call(s32[1]{0:T(128)} %bitcast.here_ref, ...), custom_call_target="tpu_custom_call" | custom-call | flops 536870912 | bytes 1048576 | tf_op jit(solution)/shard_map/encode/pallas_call | solution.py:389
  6.3 0.5 %collective-permute-start = (bf16[144,512]{1,0:T(8,128)(2,1)S(1)}, bf16[144,512]{1,0:T(8,128)(2,1)S(1)}, u32[]{:S(2)}, u32[]{:S(2)}) collective-permute-start(bf16[144,512]{1,0:T(8,128)(2,1)S(1)} %get-tuple-element.68), channel_id=1, source_target_pairs={{0,4},{4,0},{8,12},{12,8},{16,20},{20,16},{24,28},{28,24},{1,5},{5... | collective-permute-start | bytes 442376 | tf_op jit(solution)/shard_map/ppermute | solution.py:464
  6.8 1.1 %project.3 = (bf16[512,512]{1,0:T(8,128)(2,1)S(1)}, bf16[144,512]{1,0:T(8,128)(2,1)S(1)}) custom-call(s32[1]{0:T(128)} %bitcast.here_ref, bf16[512,1024]{1,0:T(8,128)(2,1)S(1)} %get-tuple-element.60.normed, bf16[128,512]{1,0:T(8,128)(2,1)S(1)} %get-tuple-element.64.b_t, bf16[512,64]{1,0:T(8,128)(2,1)S(1)} %get-tuple-element.65.grow, ...), custom_call_target="tpu_custom_call" | custom-call | flops 2147483648 | bytes 1048576 | tf_op jit(solution)/shard_map/project/pallas_call | solution.py:389
  7.9 0.0 collective-permute-done.got_ref.got_first.theirs_ref.theirs_first
  7.9 0.1 total.2.total_ref.total_first
  8.0 2.8 %collective-permute-start.1 = (bf16[144,512]{1,0:T(8,128)(2,1)S(1)}, bf16[144,512]{1,0:T(8,128)(2,1)S(1)}, u32[]{:S(2)}, u32[]{:S(2)}) collective-permute-start(bf16[144,512]{1,0:T(8,128)(2,1)S(1)} %total.2.total_ref.total_first), channel_id=1, source_target_pairs={{0,8},{4,12},{8,0},{12,4},{16,24},{20,28},{24,16},{28,20},{1,9},{5... | collective-permute-start | bytes 442376 | tf_op jit(solution)/shard_map/ppermute | solution.py:446
  10.8 1.1 %project.4 = (bf16[512,512]{1,0:T(8,128)(2,1)S(1)}, bf16[128,512]{1,0:T(8,128)(2,1)S(1)}) custom-call(s32[1]{0:T(128)} %bitcast.here_ref, bf16[512,1024]{1,0:T(8,128)(2,1)S(1)} %get-tuple-element.60.normed, bf16[128,512]{1,0:T(8,128)(2,1)S(1)} %get-tuple-element.64.b_t, bf16[512,64]{1,0:T(8,128)(2,1)S(1)} %get-tuple-element.65.grow, ...), custom_call_target="tpu_custom_call" | custom-call | flops 2147483648 | bytes 1048576 | tf_op jit(solution)/shard_map/project/pallas_call | solution.py:389
  11.9 0.1 collective-permute-start.2
  12.0 1.1 %project.5 = (bf16[512,512]{1,0:T(8,128)(2,1)S(1)}, bf16[128,512]{1,0:T(8,128)(2,1)S(1)}) custom-call(s32[1]{0:T(128)} %bitcast.here_ref, bf16[512,1024]{1,0:T(8,128)(2,1)S(1)} %get-tuple-element.60.normed, bf16[128,512]{1,0:T(8,128)(2,1)S(1)} %get-tuple-element.64.b_t, bf16[512,64]{1,0:T(8,128)(2,1)S(1)} %get-tuple-element.65.grow, ...), custom_call_target="tpu_custom_call" | custom-call | flops 2147483648 | bytes 1048576 | tf_op jit(solution)/shard_map/project/pallas_call | solution.py:389
  13.0 0.3 collective-permute-done.2.got_ref.theirs_ref
  13.3 0.1 total.3.total_ref
  13.4 0.1 collective-permute-start.4
  13.5 1.3 %inner.4 = (bf16[512,512]{1,0:T(8,128)(2,1)S(1)}, bf16[512,512]{1,0:T(8,128)(2,1)S(1)}, bf16[512,1024]{1,0:T(8,128)(2,1)S(1)}, bf16[512,512]{1,0:T(8,128)(2,1)S(1)}) custom-call(s32[1]{0:T(128)} %bitcast.here_ref, bf16[512,1024]{1,0:T(8,128)(2,1)S(1)} %get-tuple-element.60.normed, bf16[512,256]{1,0:T(8,128)(2,1)S(1)} %get-tuple-element.58.keys, ...), custom_call_target="tpu_custom_call" | custom-call | flops 2147483648 | bytes 1048576 | tf_op jit(solution)/shard_map/inner/pallas_call | solution.py:389
  14.8 0.3 %collective-permute-done.1.got_ref.got_first = bf16[144,512]{1,0:T(8,128)(2,1)S(1)} collective-permute-done((bf16[144,512]{1,0:T(8,128)(2,1)S(1)}, bf16[144,512]{1,0:T(8,128)(2,1)S(1)}, u32[]{:S(2)}, u32[]{:S(2)}) %collective-permute-start.1) | collective-permute-done | bytes 147488 | tf_op jit(solution)/shard_map/ppermute | solution.py:446
  15.1 0.1 step.2
  15.1 1.8 %collective-permute-start.3 = (bf16[128,512]{1,0:T(8,128)(2,1)S(1)}, bf16[128,512]{1,0:T(8,128)(2,1)S(1)}, u32[]{:S(2)}, u32[]{:S(2)}) collective-permute-start(bf16[128,512]{1,0:T(8,128)(2,1)S(1)} %get-tuple-element.80), channel_id=1, source_target_pairs={{0,16},{4,20},{8,24},{12,28},{16,0},{20,4},{24,8},{28,12},{1,17},{... | collective-permute-start | bytes 393224 | tf_op jit(solution)/shard_map/ppermute | solution.py:457
  17.0 1.2 %inner.5 = (bf16[512,512]{1,0:T(8,128)(2,1)S(1)}, bf16[512,512]{1,0:T(8,128)(2,1)S(1)}, bf16[512,1024]{1,0:T(8,128)(2,1)S(1)}) custom-call(s32[1]{0:T(128)} %bitcast.here_ref, bf16[512,1024]{1,0:T(8,128)(2,1)S(1)} %get-tuple-element.60.normed, bf16[512,256]{1,0:T(8,128)(2,1)S(1)} %get-tuple-element.58.keys, bf16[512,64]{1,0:T(8,128)(2,1)S(1)} %get-tuple-element.61.fall, ...), custom_call_target="tpu_custom_call" | custom-call | flops 67108864 | bytes 1048576 | tf_op jit(solution)/shard_map/inner/pallas_call | solution.py:389
  18.2 1.2 %inner.6 = (bf16[512,512]{1,0:T(8,128)(2,1)S(1)}, bf16[512,512]{1,0:T(8,128)(2,1)S(1)}, bf16[512,1024]{1,0:T(8,128)(2,1)S(1)}) custom-call(s32[1]{0:T(128)} %bitcast.here_ref, bf16[512,1024]{1,0:T(8,128)(2,1)S(1)} %get-tuple-element.60.normed, bf16[512,256]{1,0:T(8,128)(2,1)S(1)} %get-tuple-element.58.keys, bf16[512,64]{1,0:T(8,128)(2,1)S(1)} %get-tuple-element.61.fall, ...), custom_call_target="tpu_custom_call" | custom-call | flops 67108864 | bytes 1048576 | tf_op jit(solution)/shard_map/inner/pallas_call | solution.py:389
  19.4 0.0 collective-permute-done.4.got_ref
  19.4 0.1 step.3
  19.5 1.2 %collective-permute-start.5 = (bf16[128,512]{1,0:T(8,128)(2,1)S(1)}, bf16[128,512]{1,0:T(8,128)(2,1)S(1)}, u32[]{:S(2)}, u32[]{:S(2)}) collective-permute-start(bf16[128,512]{1,0:T(8,128)(2,1)S(1)} %get-tuple-element.99), channel_id=1, source_target_pairs={{0,16},{4,20},{8,24},{12,28},{16,0},{20,4},{24,8},{28,12},{1,17},{... | collective-permute-start | bytes 393224 | tf_op jit(solution)/shard_map/ppermute | solution.py:457
  20.8 0.0 collective-permute-done.3.got_ref
  20.8 0.3 last.2
  21.0 1.2 %inner.7 = (bf16[512,512]{1,0:T(8,128)(2,1)S(1)}, bf16[512,512]{1,0:T(8,128)(2,1)S(1)}, bf16[512,1024]{1,0:T(8,128)(2,1)S(1)}) custom-call(s32[1]{0:T(128)} %bitcast.here_ref, bf16[512,1024]{1,0:T(8,128)(2,1)S(1)} %get-tuple-element.60.normed, bf16[512,256]{1,0:T(8,128)(2,1)S(1)} %get-tuple-element.58.keys, bf16[512,64]{1,0:T(8,128)(2,1)S(1)} %get-tuple-element.61.fall, ...), custom_call_target="tpu_custom_call" | custom-call | flops 67108864 | bytes 1048576 | tf_op jit(solution)/shard_map/inner/pallas_call | solution.py:389
  22.3 0.1 collective-permute-start.6
  22.4 1.1 %mix.3.base = f32[512,1024]{1,0:T(8,128)S(1)} custom-call(s32[1]{0:T(128)} %bitcast.here_ref, bf16[512,256]{1,0:T(8,128)(2,1)S(1)} %get-tuple-element.58.keys, bf16[512,1024]{1,0:T(8,128)(2,1)S(1)} %get-tuple-element.95.base, f32[1,2048]{1,0:T(1,128)S(1)} %get-tuple-element.96.gain, bf16[128,512]{1,0:T(8,128)(2,1)S(1)} %get-tuple-element.92.refs_0_, ...), custom_call_target="tpu_custom_call" | custom-call | flops 67108864 | bytes 1048576 | tf_op jit(solution)/shard_map/mix/pallas_call | solution.py:389
  23.4 1.2 %collective-permute-done.5.got_ref = bf16[128,512]{1,0:T(8,128)(2,1)S(1)} collective-permute-done((bf16[128,512]{1,0:T(8,128)(2,1)S(1)}, bf16[128,512]{1,0:T(8,128)(2,1)S(1)}, u32[]{:S(2)}, u32[]{:S(2)}) %collective-permute-start.5) | collective-permute-done | bytes 131104 | tf_op jit(solution)/shard_map/ppermute | solution.py:457
  24.6 0.1 last.3
  24.7 0.1 collective-permute-start.7
  24.8 0.0 collective-permute-done.6.refs_0_
  24.8 2.0 %mix.4.base = f32[512,1024]{1,0:T(8,128)S(1)} custom-call(s32[1]{0:T(128)} %bitcast.here_ref, bf16[512,256]{1,0:T(8,128)(2,1)S(1)} %get-tuple-element.58.keys, f32[512,1024]{1,0:T(8,128)S(1)} %mix.3.base, f32[1,2048]{1,0:T(1,128)S(1)} %get-tuple-element.96.gain, bf16[128,512]{1,0:T(8,128)(2,1)S(1)} %collective-permute-done.6.refs_0_, ...), custom_call_target="tpu_custom_call" | custom-call | flops 67108864 | bytes 1048576 | tf_op jit(solution)/shard_map/mix/pallas_call | solution.py:389
  26.8 0.0 collective-permute-done.7.refs_0_
  26.9 1.9 %mix.5 = bf16[512,1024]{1,0:T(8,128)(2,1)} custom-call(s32[1]{0:T(128)} %bitcast.here_ref, bf16[512,256]{1,0:T(8,128)(2,1)S(1)} %get-tuple-element.58.keys, f32[512,1024]{1,0:T(8,128)S(1)} %mix.4.base, f32[1,2048]{1,0:T(1,128)S(1)} %get-tuple-element.96.gain, bf16[128,512]{1,0:T(8,128)(2,1)S(1)} %collective-permute-done.7.refs_0_, ...), custom_call_target="tpu_custom_call" | custom-call | flops 67108864 | bytes 1048576 | tf_op jit(solution)/shard_map/mix/pallas_call | solution.py:389
Async XLA Ops:
  6.3 1.6 %collective-permute-start = (bf16[144,512]{1,0:T(8,128)(2,1)S(1)}, bf16[144,512]{1,0:T(8,128)(2,1)S(1)}, u32[]{:S(2)}, u32[]{:S(2)}) collective-permute-start(bf16[144,512]{1,0:T(8,128)(2,1)S(1)} %get-tuple-element.68), channel_id=1, source_target_pairs={{0,4},{4,0},{8,12},{12,8},{16,20},{20,16},{24,28},{28,24},{1,5},{5... | collective-permute-start | bytes 442376 | tf_op jit(solution)/shard_map/ppermute | solution.py:464
  8.0 7.1 %collective-permute-start.1 = (bf16[144,512]{1,0:T(8,128)(2,1)S(1)}, bf16[144,512]{1,0:T(8,128)(2,1)S(1)}, u32[]{:S(2)}, u32[]{:S(2)}) collective-permute-start(bf16[144,512]{1,0:T(8,128)(2,1)S(1)} %total.2.total_ref.total_first), channel_id=1, source_target_pairs={{0,8},{4,12},{8,0},{12,4},{16,24},{20,28},{24,16},{28,20},{1,9},{5... | collective-permute-start | bytes 442376 | tf_op jit(solution)/shard_map/ppermute | solution.py:446
  11.9 1.4 %collective-permute-start.2 = (bf16[128,512]{1,0:T(8,128)(2,1)S(1)}, bf16[128,512]{1,0:T(8,128)(2,1)S(1)}, u32[]{:S(2)}, u32[]{:S(2)}) collective-permute-start(bf16[128,512]{1,0:T(8,128)(2,1)S(1)} %get-tuple-element.74), channel_id=1, source_target_pairs={{0,4},{4,0},{8,12},{12,8},{16,20},{20,16},{24,28},{28,24},{1,5},{5... | collective-permute-start | bytes 393224 | tf_op jit(solution)/shard_map/ppermute | solution.py:468
  13.4 6.1 %collective-permute-start.4 = (bf16[128,512]{1,0:T(8,128)(2,1)S(1)}, bf16[128,512]{1,0:T(8,128)(2,1)S(1)}, u32[]{:S(2)}, u32[]{:S(2)}) collective-permute-start(bf16[128,512]{1,0:T(8,128)(2,1)S(1)} %total.3.total_ref), channel_id=1, source_target_pairs={{0,8},{4,12},{8,0},{12,4},{16,24},{20,28},{24,16},{28,20},{1,9},{5... | collective-permute-start | bytes 393224 | tf_op jit(solution)/shard_map/ppermute | solution.py:446
  15.1 5.6 %collective-permute-start.3 = (bf16[128,512]{1,0:T(8,128)(2,1)S(1)}, bf16[128,512]{1,0:T(8,128)(2,1)S(1)}, u32[]{:S(2)}, u32[]{:S(2)}) collective-permute-start(bf16[128,512]{1,0:T(8,128)(2,1)S(1)} %get-tuple-element.80), channel_id=1, source_target_pairs={{0,16},{4,20},{8,24},{12,28},{16,0},{20,4},{24,8},{28,12},{1,17},{... | collective-permute-start | bytes 393224 | tf_op jit(solution)/shard_map/ppermute | solution.py:457
  19.5 5.1 %collective-permute-start.5 = (bf16[128,512]{1,0:T(8,128)(2,1)S(1)}, bf16[128,512]{1,0:T(8,128)(2,1)S(1)}, u32[]{:S(2)}, u32[]{:S(2)}) collective-permute-start(bf16[128,512]{1,0:T(8,128)(2,1)S(1)} %get-tuple-element.99), channel_id=1, source_target_pairs={{0,16},{4,20},{8,24},{12,28},{16,0},{20,4},{24,8},{28,12},{1,17},{... | collective-permute-start | bytes 393224 | tf_op jit(solution)/shard_map/ppermute | solution.py:457
  22.3 2.5 %collective-permute-start.6 = (bf16[128,512]{1,0:T(8,128)(2,1)S(1)}, bf16[128,512]{1,0:T(8,128)(2,1)S(1)}, u32[]{:S(2)}, u32[]{:S(2)}) collective-permute-start(bf16[128,512]{1,0:T(8,128)(2,1)S(1)} %get-tuple-element.103), channel_id=1, source_target_pairs={{0,4},{4,0},{8,12},{12,8},{16,20},{20,16},{24,28},{28,24},{1,5},{5... | collective-permute-start | bytes 393224 | tf_op jit(solution)/shard_map/ppermute | solution.py:462
  24.7 2.1 %collective-permute-start.7 = (bf16[128,512]{1,0:T(8,128)(2,1)S(1)}, bf16[128,512]{1,0:T(8,128)(2,1)S(1)}, u32[]{:S(2)}, u32[]{:S(2)}) collective-permute-start(bf16[128,512]{1,0:T(8,128)(2,1)S(1)} %get-tuple-element.108), channel_id=1, source_target_pairs={{0,4},{4,0},{8,12},{12,8},{16,20},{20,16},{24,28},{28,24},{1,5},{5... | collective-permute-start | bytes 393224 | tf_op jit(solution)/shard_map/ppermute | solution.py:462

commit v9 on v8

--- a/solution.py
+++ b/solution.py
@@ -340,20 +340,19 @@
             carried = dot(keys[:, width:], state[:, cols])
             g = v[:, cols].astype(F32) + u[:, cols].astype(F32) * carried
             work.append((g, dot((g * g).astype(BF), mean)))
-    mixed = []
+    steps = base.shape[1] // CHUNK
+    totals = [base[:, n * CHUNK:(n + 1) * CHUNK].astype(F32) for n in range(steps)]
     for i in range(many):
         parts = []
         for j in range(size // CHUNK):
             g, m = work[i * (size // CHUNK) + j]
             row = gain[:, pl.ds(pl.multiple_of(starts[i] + j * CHUNK, CHUNK), CHUNK)]
             parts.append((g * lax.rsqrt(m + 1e-05) * row).astype(BF))
-        mixed.append(jnp.concatenate(parts, axis=1))
+        mixed = jnp.concatenate(parts, axis=1)
+        totals = [totals[n] + dot(mixed, ws[i][:, n * CHUNK:(n + 1) * CHUNK]) for n in range(steps)]
     copies = []
-    for n in range(base.shape[1] // CHUNK):
+    for n, total in enumerate(totals):
         cols = slice(n * CHUNK, (n + 1) * CHUNK)
-        total = base[:, cols].astype(F32)
-        for part, w in zip(mixed, ws):
-            total = total + dot(part, w[:, cols])
         if last:
             buf, sem = refs[4 * many + 1:]
             buf[:, cols] = total.astype(buf.dtype)

time: 29.2 us -> 29.2 us (level)
  no operation moved by 1% of the time
where the time goes in v9:
time: 29.2 us; the launch traced here: 28.9 us
  Pallas kernels  19.5 us (67%)
  starting transfers between devices  6.72 us (23%)
  waiting for transfers between devices  1.78 us (6%)
  between operations  0.97 us (3%)
    pallas_call x17, Pallas kernels, call(): pl.pallas_call(kernel, out_shape=tuple(outs), in_specs=specs, out_specs=(...  19.5 us
    ppermute x2, starting transfers between devices, advance(): arriving[i] = lax.ppermute(totals[i], 'tm', pair(2 * reach))  3.07 us
    ppermute x2, starting transfers between devices, start_total(): arriving[i] = lax.ppermute(totals[i], 'tm', pair(2))  2.92 us
    ppermute x2, waiting for transfers between devices, advance(): arriving[i] = lax.ppermute(totals[i], 'tm', pair(2 * reach))  1.21 us
  transfers between devices with their start and end apart: 8, of which 3 were waited for; matrix products, arithmetic and copies ran while one was open for 0% of the time, Pallas kernels for 41%

profile of v9, /device:TPU:0, one launch (start us, length us, event | category | flops | bytes accessed | tf_op | source)
XLA Modules:
  0.0 28.9 jit_solution(7443772946220882776)
XLA Ops:
  0.7 5.6 %encode.1 = (bf16[512,1024]{1,0:T(8,128)(2,1)S(1)}, bf16[512,1024]{1,0:T(8,128)(2,1)S(1)}, bf16[512,256]{1,0:T(8,128)(2,1)S(1)}, bf16[128,512]{1,0:T(8,128)(2,1)...) custom-call(s32[1]{0:T(128)} %bitcast.here_ref, ...), custom_call_target="tpu_custom_call" | custom-call | flops 536870912 | bytes 1048576 | tf_op jit(solution)/shard_map/encode/pallas_call | solution.py:388
  6.3 0.5 %collective-permute-start = (bf16[144,512]{1,0:T(8,128)(2,1)S(1)}, bf16[144,512]{1,0:T(8,128)(2,1)S(1)}, u32[]{:S(2)}, u32[]{:S(2)}) collective-permute-start(bf16[144,512]{1,0:T(8,128)(2,1)S(1)} %get-tuple-element.68), channel_id=1, source_target_pairs={{0,4},{4,0},{8,12},{12,8},{16,20},{20,16},{24,28},{28,24},{1,5},{5... | collective-permute-start | bytes 442376 | tf_op jit(solution)/shard_map/ppermute | solution.py:463
  6.8 1.1 %project.3 = (bf16[512,512]{1,0:T(8,128)(2,1)S(1)}, bf16[144,512]{1,0:T(8,128)(2,1)S(1)}) custom-call(s32[1]{0:T(128)} %bitcast.here_ref, bf16[512,1024]{1,0:T(8,128)(2,1)S(1)} %get-tuple-element.60.normed, bf16[128,512]{1,0:T(8,128)(2,1)S(1)} %get-tuple-element.64.b_t, bf16[512,64]{1,0:T(8,128)(2,1)S(1)} %get-tuple-element.65.grow, ...), custom_call_target="tpu_custom_call" | custom-call | flops 2147483648 | bytes 1048576 | tf_op jit(solution)/shard_map/project/pallas_call | solution.py:388
  7.9 0.0 collective-permute-done.got_ref.got_first.theirs_ref.theirs_first
  7.9 0.1 total.2.total_ref.total_first
  8.0 2.8 %collective-permute-start.1 = (bf16[144,512]{1,0:T(8,128)(2,1)S(1)}, bf16[144,512]{1,0:T(8,128)(2,1)S(1)}, u32[]{:S(2)}, u32[]{:S(2)}) collective-permute-start(bf16[144,512]{1,0:T(8,128)(2,1)S(1)} %total.2.total_ref.total_first), channel_id=1, source_target_pairs={{0,8},{4,12},{8,0},{12,4},{16,24},{20,28},{24,16},{28,20},{1,9},{5... | collective-permute-start | bytes 442376 | tf_op jit(solution)/shard_map/ppermute | solution.py:445
  10.8 1.1 %project.4 = (bf16[512,512]{1,0:T(8,128)(2,1)S(1)}, bf16[128,512]{1,0:T(8,128)(2,1)S(1)}) custom-call(s32[1]{0:T(128)} %bitcast.here_ref, bf16[512,1024]{1,0:T(8,128)(2,1)S(1)} %get-tuple-element.60.normed, bf16[128,512]{1,0:T(8,128)(2,1)S(1)} %get-tuple-element.64.b_t, bf16[512,64]{1,0:T(8,128)(2,1)S(1)} %get-tuple-element.65.grow, ...), custom_call_target="tpu_custom_call" | custom-call | flops 2147483648 | bytes 1048576 | tf_op jit(solution)/shard_map/project/pallas_call | solution.py:388
  11.9 0.1 collective-permute-start.2
  12.0 1.1 %project.5 = (bf16[512,512]{1,0:T(8,128)(2,1)S(1)}, bf16[128,512]{1,0:T(8,128)(2,1)S(1)}) custom-call(s32[1]{0:T(128)} %bitcast.here_ref, bf16[512,1024]{1,0:T(8,128)(2,1)S(1)} %get-tuple-element.60.normed, bf16[128,512]{1,0:T(8,128)(2,1)S(1)} %get-tuple-element.64.b_t, bf16[512,64]{1,0:T(8,128)(2,1)S(1)} %get-tuple-element.65.grow, ...), custom_call_target="tpu_custom_call" | custom-call | flops 2147483648 | bytes 1048576 | tf_op jit(solution)/shard_map/project/pallas_call | solution.py:388
  13.0 0.3 collective-permute-done.2.got_ref.theirs_ref
  13.3 0.1 total.3.total_ref
  13.4 0.1 collective-permute-start.4
  13.5 1.3 %inner.4 = (bf16[512,512]{1,0:T(8,128)(2,1)S(1)}, bf16[512,512]{1,0:T(8,128)(2,1)S(1)}, bf16[512,1024]{1,0:T(8,128)(2,1)S(1)}, bf16[512,512]{1,0:T(8,128)(2,1)S(1)}) custom-call(s32[1]{0:T(128)} %bitcast.here_ref, bf16[512,1024]{1,0:T(8,128)(2,1)S(1)} %get-tuple-element.60.normed, bf16[512,256]{1,0:T(8,128)(2,1)S(1)} %get-tuple-element.58.keys, ...), custom_call_target="tpu_custom_call" | custom-call | flops 2147483648 | bytes 1048576 | tf_op jit(solution)/shard_map/inner/pallas_call | solution.py:388
  14.8 0.3 %collective-permute-done.1.got_ref.got_first = bf16[144,512]{1,0:T(8,128)(2,1)S(1)} collective-permute-done((bf16[144,512]{1,0:T(8,128)(2,1)S(1)}, bf16[144,512]{1,0:T(8,128)(2,1)S(1)}, u32[]{:S(2)}, u32[]{:S(2)}) %collective-permute-start.1) | collective-permute-done | bytes 147488 | tf_op jit(solution)/shard_map/ppermute | solution.py:445
  15.1 0.1 step.2
  15.1 1.8 %collective-permute-start.3 = (bf16[128,512]{1,0:T(8,128)(2,1)S(1)}, bf16[128,512]{1,0:T(8,128)(2,1)S(1)}, u32[]{:S(2)}, u32[]{:S(2)}) collective-permute-start(bf16[128,512]{1,0:T(8,128)(2,1)S(1)} %get-tuple-element.80), channel_id=1, source_target_pairs={{0,16},{4,20},{8,24},{12,28},{16,0},{20,4},{24,8},{28,12},{1,17},{... | collective-permute-start | bytes 393224 | tf_op jit(solution)/shard_map/ppermute | solution.py:456
  17.0 1.2 %inner.5 = (bf16[512,512]{1,0:T(8,128)(2,1)S(1)}, bf16[512,512]{1,0:T(8,128)(2,1)S(1)}, bf16[512,1024]{1,0:T(8,128)(2,1)S(1)}) custom-call(s32[1]{0:T(128)} %bitcast.here_ref, bf16[512,1024]{1,0:T(8,128)(2,1)S(1)} %get-tuple-element.60.normed, bf16[512,256]{1,0:T(8,128)(2,1)S(1)} %get-tuple-element.58.keys, bf16[512,64]{1,0:T(8,128)(2,1)S(1)} %get-tuple-element.61.fall, ...), custom_call_target="tpu_custom_call" | custom-call | flops 67108864 | bytes 1048576 | tf_op jit(solution)/shard_map/inner/pallas_call | solution.py:388
  18.2 1.2 %inner.6 = (bf16[512,512]{1,0:T(8,128)(2,1)S(1)}, bf16[512,512]{1,0:T(8,128)(2,1)S(1)}, bf16[512,1024]{1,0:T(8,128)(2,1)S(1)}) custom-call(s32[1]{0:T(128)} %bitcast.here_ref, bf16[512,1024]{1,0:T(8,128)(2,1)S(1)} %get-tuple-element.60.normed, bf16[512,256]{1,0:T(8,128)(2,1)S(1)} %get-tuple-element.58.keys, bf16[512,64]{1,0:T(8,128)(2,1)S(1)} %get-tuple-element.61.fall, ...), custom_call_target="tpu_custom_call" | custom-call | flops 67108864 | bytes 1048576 | tf_op jit(solution)/shard_map/inner/pallas_call | solution.py:388
  19.4 0.0 collective-permute-done.4.got_ref
  19.4 0.1 step.3
  19.5 1.2 %collective-permute-start.5 = (bf16[128,512]{1,0:T(8,128)(2,1)S(1)}, bf16[128,512]{1,0:T(8,128)(2,1)S(1)}, u32[]{:S(2)}, u32[]{:S(2)}) collective-permute-start(bf16[128,512]{1,0:T(8,128)(2,1)S(1)} %get-tuple-element.99), channel_id=1, source_target_pairs={{0,16},{4,20},{8,24},{12,28},{16,0},{20,4},{24,8},{28,12},{1,17},{... | collective-permute-start | bytes 393224 | tf_op jit(solution)/shard_map/ppermute | solution.py:456
  20.8 0.0 collective-permute-done.3.got_ref
  20.8 0.3 last.2
  21.0 1.2 %inner.7 = (bf16[512,512]{1,0:T(8,128)(2,1)S(1)}, bf16[512,512]{1,0:T(8,128)(2,1)S(1)}, bf16[512,1024]{1,0:T(8,128)(2,1)S(1)}) custom-call(s32[1]{0:T(128)} %bitcast.here_ref, bf16[512,1024]{1,0:T(8,128)(2,1)S(1)} %get-tuple-element.60.normed, bf16[512,256]{1,0:T(8,128)(2,1)S(1)} %get-tuple-element.58.keys, bf16[512,64]{1,0:T(8,128)(2,1)S(1)} %get-tuple-element.61.fall, ...), custom_call_target="tpu_custom_call" | custom-call | flops 67108864 | bytes 1048576 | tf_op jit(solution)/shard_map/inner/pallas_call | solution.py:388
  22.3 0.1 collective-permute-start.6
  22.4 1.1 %mix.3.base = f32[512,1024]{1,0:T(8,128)S(1)} custom-call(s32[1]{0:T(128)} %bitcast.here_ref, bf16[512,256]{1,0:T(8,128)(2,1)S(1)} %get-tuple-element.58.keys, bf16[512,1024]{1,0:T(8,128)(2,1)S(1)} %get-tuple-element.95.base, f32[1,2048]{1,0:T(1,128)S(1)} %get-tuple-element.96.gain, bf16[128,512]{1,0:T(8,128)(2,1)S(1)} %get-tuple-element.92.refs_0_, ...), custom_call_target="tpu_custom_call" | custom-call | flops 67108864 | bytes 1048576 | tf_op jit(solution)/shard_map/mix/pallas_call | solution.py:388
  23.4 1.2 %collective-permute-done.5.got_ref = bf16[128,512]{1,0:T(8,128)(2,1)S(1)} collective-permute-done((bf16[128,512]{1,0:T(8,128)(2,1)S(1)}, bf16[128,512]{1,0:T(8,128)(2,1)S(1)}, u32[]{:S(2)}, u32[]{:S(2)}) %collective-permute-start.5) | collective-permute-done | bytes 131104 | tf_op jit(solution)/shard_map/ppermute | solution.py:456
  24.6 0.1 last.3
  24.7 0.1 collective-permute-start.7
  24.8 0.0 collective-permute-done.6.refs_0_
  24.8 2.0 %mix.4.base = f32[512,1024]{1,0:T(8,128)S(1)} custom-call(s32[1]{0:T(128)} %bitcast.here_ref, bf16[512,256]{1,0:T(8,128)(2,1)S(1)} %get-tuple-element.58.keys, f32[512,1024]{1,0:T(8,128)S(1)} %mix.3.base, f32[1,2048]{1,0:T(1,128)S(1)} %get-tuple-element.96.gain, bf16[128,512]{1,0:T(8,128)(2,1)S(1)} %collective-permute-done.6.refs_0_, ...), custom_call_target="tpu_custom_call" | custom-call | flops 67108864 | bytes 1048576 | tf_op jit(solution)/shard_map/mix/pallas_call | solution.py:388
  26.8 0.0 collective-permute-done.7.refs_0_
  26.8 2.0 %mix.5 = bf16[512,1024]{1,0:T(8,128)(2,1)} custom-call(s32[1]{0:T(128)} %bitcast.here_ref, bf16[512,256]{1,0:T(8,128)(2,1)S(1)} %get-tuple-element.58.keys, f32[512,1024]{1,0:T(8,128)S(1)} %mix.4.base, f32[1,2048]{1,0:T(1,128)S(1)} %get-tuple-element.96.gain, bf16[128,512]{1,0:T(8,128)(2,1)S(1)} %collective-permute-done.7.refs_0_, ...), custom_call_target="tpu_custom_call" | custom-call | flops 67108864 | bytes 1048576 | tf_op jit(solution)/shard_map/mix/pallas_call | solution.py:388
Async XLA Ops:
  6.3 1.6 %collective-permute-start = (bf16[144,512]{1,0:T(8,128)(2,1)S(1)}, bf16[144,512]{1,0:T(8,128)(2,1)S(1)}, u32[]{:S(2)}, u32[]{:S(2)}) collective-permute-start(bf16[144,512]{1,0:T(8,128)(2,1)S(1)} %get-tuple-element.68), channel_id=1, source_target_pairs={{0,4},{4,0},{8,12},{12,8},{16,20},{20,16},{24,28},{28,24},{1,5},{5... | collective-permute-start | bytes 442376 | tf_op jit(solution)/shard_map/ppermute | solution.py:463
  8.0 7.1 %collective-permute-start.1 = (bf16[144,512]{1,0:T(8,128)(2,1)S(1)}, bf16[144,512]{1,0:T(8,128)(2,1)S(1)}, u32[]{:S(2)}, u32[]{:S(2)}) collective-permute-start(bf16[144,512]{1,0:T(8,128)(2,1)S(1)} %total.2.total_ref.total_first), channel_id=1, source_target_pairs={{0,8},{4,12},{8,0},{12,4},{16,24},{20,28},{24,16},{28,20},{1,9},{5... | collective-permute-start | bytes 442376 | tf_op jit(solution)/shard_map/ppermute | solution.py:445
  11.9 1.4 %collective-permute-start.2 = (bf16[128,512]{1,0:T(8,128)(2,1)S(1)}, bf16[128,512]{1,0:T(8,128)(2,1)S(1)}, u32[]{:S(2)}, u32[]{:S(2)}) collective-permute-start(bf16[128,512]{1,0:T(8,128)(2,1)S(1)} %get-tuple-element.74), channel_id=1, source_target_pairs={{0,4},{4,0},{8,12},{12,8},{16,20},{20,16},{24,28},{28,24},{1,5},{5... | collective-permute-start | bytes 393224 | tf_op jit(solution)/shard_map/ppermute | solution.py:467
  13.4 6.1 %collective-permute-start.4 = (bf16[128,512]{1,0:T(8,128)(2,1)S(1)}, bf16[128,512]{1,0:T(8,128)(2,1)S(1)}, u32[]{:S(2)}, u32[]{:S(2)}) collective-permute-start(bf16[128,512]{1,0:T(8,128)(2,1)S(1)} %total.3.total_ref), channel_id=1, source_target_pairs={{0,8},{4,12},{8,0},{12,4},{16,24},{20,28},{24,16},{28,20},{1,9},{5... | collective-permute-start | bytes 393224 | tf_op jit(solution)/shard_map/ppermute | solution.py:445
  15.1 5.6 %collective-permute-start.3 = (bf16[128,512]{1,0:T(8,128)(2,1)S(1)}, bf16[128,512]{1,0:T(8,128)(2,1)S(1)}, u32[]{:S(2)}, u32[]{:S(2)}) collective-permute-start(bf16[128,512]{1,0:T(8,128)(2,1)S(1)} %get-tuple-element.80), channel_id=1, source_target_pairs={{0,16},{4,20},{8,24},{12,28},{16,0},{20,4},{24,8},{28,12},{1,17},{... | collective-permute-start | bytes 393224 | tf_op jit(solution)/shard_map/ppermute | solution.py:456
  19.5 5.1 %collective-permute-start.5 = (bf16[128,512]{1,0:T(8,128)(2,1)S(1)}, bf16[128,512]{1,0:T(8,128)(2,1)S(1)}, u32[]{:S(2)}, u32[]{:S(2)}) collective-permute-start(bf16[128,512]{1,0:T(8,128)(2,1)S(1)} %get-tuple-element.99), channel_id=1, source_target_pairs={{0,16},{4,20},{8,24},{12,28},{16,0},{20,4},{24,8},{28,12},{1,17},{... | collective-permute-start | bytes 393224 | tf_op jit(solution)/shard_map/ppermute | solution.py:456
  22.3 2.5 %collective-permute-start.6 = (bf16[128,512]{1,0:T(8,128)(2,1)S(1)}, bf16[128,512]{1,0:T(8,128)(2,1)S(1)}, u32[]{:S(2)}, u32[]{:S(2)}) collective-permute-start(bf16[128,512]{1,0:T(8,128)(2,1)S(1)} %get-tuple-element.103), channel_id=1, source_target_pairs={{0,4},{4,0},{8,12},{12,8},{16,20},{20,16},{24,28},{28,24},{1,5},{5... | collective-permute-start | bytes 393224 | tf_op jit(solution)/shard_map/ppermute | solution.py:461
  24.7 2.1 %collective-permute-start.7 = (bf16[128,512]{1,0:T(8,128)(2,1)S(1)}, bf16[128,512]{1,0:T(8,128)(2,1)S(1)}, u32[]{:S(2)}, u32[]{:S(2)}) collective-permute-start(bf16[128,512]{1,0:T(8,128)(2,1)S(1)} %get-tuple-element.108), channel_id=1, source_target_pairs={{0,4},{4,0},{8,12},{12,8},{16,20},{20,16},{24,28},{28,24},{1,5},{5... | collective-permute-start | bytes 393224 | tf_op jit(solution)/shard_map/ppermute | solution.py:461

commit v10 on v9

--- a/solution.py
+++ b/solution.py
@@ -202,9 +202,16 @@
     return w_any.at[:, pl.ds(pl.multiple_of((half * 2 + group) * size, size), size)]
 
 
-def project_kernel(heads, head_dim, own, group, here_ref, normed, b_t, grow, fall, w, xs_ref, s_ref):
+def project_kernel(heads, head_dim, own, group, here_ref, normed, b_t, grow, fall, w, *refs):
     half = (here_ref[0] + 1 - own) % 2
     rows = normed.shape[0]
+    if len(refs) == 2:
+        xs_ref, s_ref = refs
+    else:
+        keys, xs_ref, s_ref, scores_ref = refs
+        width = keys.shape[1] // 2
+        scores = dot_t(keys[:, width:], keys[:, :width])
+        scores_ref[...] = jnp.where(iota((rows, rows), 0) >= iota((rows, rows), 1), scores, 0.0).astype(BF)
     first = (half * 2 + group) * (xs_ref.shape[1] // head_dim)
     project(first, w, xs_ref, s_ref, heads, head_dim, normed, b_t[...], grow[...], fall[rows - EXTRA:])
 
@@ -410,9 +417,10 @@
 
     long, short = 8 * rows * depth * size, rows * depth * size // 4
 
-    def projected(own, group, w):
+    def projected(own, group, w, *keys):
         return call(functools.partial(project_kernel, heads, head_dim, own, group), "project",
-                    (part, kinds[group]), where + vm(normed, b_t, grow, fall, w), (), long)
+                    (part, kinds[group]) + (near((rows, rows)),) * len(keys),
+                    where + vm(normed, b_t, grow, fall, w, *keys), (), long)
 
     scores = []
 
@@ -465,7 +473,8 @@
     start_total(0, s_m1, got_1)
     xs_o2, s_o2 = projected(0, 1, after(w_o2, totals[0]))
     got_2 = lax.ppermute(s_o2, "tm", pair(1))
-    xs_m2, s_m2 = projected(1, 1, after(w_m2, s_o2))
+    xs_m2, s_m2, early = projected(1, 1, after(w_m2, s_o2), keys)
+    scores.append(early)
     start_total(1, s_m2, got_2)
     stamp = work(0, 0, w_o1, xs_o1, totals[1], long)
     advance(0, 2, after(arriving[0], stamp))

time: 29.2 us -> 29.3 us (level)
  no operation moved by 1% of the time
where the time goes in v10:
time: 29.3 us; the launch traced here: 29 us
  Pallas kernels  19.5 us (67%)
  starting transfers between devices  6.92 us (24%)
  waiting for transfers between devices  1.61 us (5%)
  between operations  0.97 us (3%)
    pallas_call x17, Pallas kernels, call(): pl.pallas_call(kernel, out_shape=tuple(outs), in_specs=specs, out_specs=(...  19.5 us
    ppermute x2, starting transfers between devices, advance(): arriving[i] = lax.ppermute(totals[i], 'tm', pair(2 * reach))  3.19 us
    ppermute x2, starting transfers between devices, start_total(): arriving[i] = lax.ppermute(totals[i], 'tm', pair(2))  3.01 us
    ppermute x2, waiting for transfers between devices, advance(): arriving[i] = lax.ppermute(totals[i], 'tm', pair(2 * reach))  1.16 us
  transfers between devices with their start and end apart: 8, of which 3 were waited for; matrix products, arithmetic and copies ran while one was open for 0% of the time, Pallas kernels for 41%

profile of v10, /device:TPU:0, one launch (start us, length us, event | category | flops | bytes accessed | tf_op | source)
XLA Modules:
  0.0 29.0 jit_solution(13767444164936479648)
XLA Ops:
  0.7 5.6 %encode.1 = (bf16[512,1024]{1,0:T(8,128)(2,1)S(1)}, bf16[512,1024]{1,0:T(8,128)(2,1)S(1)}, bf16[512,256]{1,0:T(8,128)(2,1)S(1)}, bf16[128,512]{1,0:T(8,128)(2,1)...) custom-call(s32[1]{0:T(128)} %bitcast.here_ref, ...), custom_call_target="tpu_custom_call" | custom-call | flops 536870912 | bytes 1048576 | tf_op jit(solution)/shard_map/encode/pallas_call | solution.py:395
  6.3 0.5 %collective-permute-start = (bf16[144,512]{1,0:T(8,128)(2,1)S(1)}, bf16[144,512]{1,0:T(8,128)(2,1)S(1)}, u32[]{:S(2)}, u32[]{:S(2)}) collective-permute-start(bf16[144,512]{1,0:T(8,128)(2,1)S(1)} %get-tuple-element.68), channel_id=1, source_target_pairs={{0,4},{4,0},{8,12},{12,8},{16,20},{20,16},{24,28},{28,24},{1,5},{5... | collective-permute-start | bytes 442376 | tf_op jit(solution)/shard_map/ppermute | solution.py:471
  6.8 1.1 %project.3 = (bf16[512,512]{1,0:T(8,128)(2,1)S(1)}, bf16[144,512]{1,0:T(8,128)(2,1)S(1)}) custom-call(s32[1]{0:T(128)} %bitcast.here_ref, bf16[512,1024]{1,0:T(8,128)(2,1)S(1)} %get-tuple-element.60.normed, bf16[128,512]{1,0:T(8,128)(2,1)S(1)} %get-tuple-element.64.b_t, bf16[512,64]{1,0:T(8,128)(2,1)S(1)} %get-tuple-element.65.grow, ...), custom_call_target="tpu_custom_call" | custom-call | flops 2147483648 | bytes 1048576 | tf_op jit(solution)/shard_map/project/pallas_call | solution.py:395
  7.9 0.0 collective-permute-done.got_ref.got_first.theirs_ref.theirs_first
  7.9 0.1 total.2.total_ref.total_first
  8.0 2.8 %collective-permute-start.1 = (bf16[144,512]{1,0:T(8,128)(2,1)S(1)}, bf16[144,512]{1,0:T(8,128)(2,1)S(1)}, u32[]{:S(2)}, u32[]{:S(2)}) collective-permute-start(bf16[144,512]{1,0:T(8,128)(2,1)S(1)} %total.2.total_ref.total_first), channel_id=1, source_target_pairs={{0,8},{4,12},{8,0},{12,4},{16,24},{20,28},{24,16},{28,20},{1,9},{5... | collective-permute-start | bytes 442376 | tf_op jit(solution)/shard_map/ppermute | solution.py:453
  10.8 1.1 %project.4 = (bf16[512,512]{1,0:T(8,128)(2,1)S(1)}, bf16[128,512]{1,0:T(8,128)(2,1)S(1)}) custom-call(s32[1]{0:T(128)} %bitcast.here_ref, bf16[512,1024]{1,0:T(8,128)(2,1)S(1)} %get-tuple-element.60.normed, bf16[128,512]{1,0:T(8,128)(2,1)S(1)} %get-tuple-element.64.b_t, bf16[512,64]{1,0:T(8,128)(2,1)S(1)} %get-tuple-element.65.grow, ...), custom_call_target="tpu_custom_call" | custom-call | flops 2147483648 | bytes 1048576 | tf_op jit(solution)/shard_map/project/pallas_call | solution.py:395
  11.9 0.1 collective-permute-start.2
  12.0 1.2 %project.5 = (bf16[512,512]{1,0:T(8,128)(2,1)S(1)}, bf16[128,512]{1,0:T(8,128)(2,1)S(1)}, bf16[512,512]{1,0:T(8,128)(2,1)S(1)}) custom-call(s32[1]{0:T(128)} %bitcast.here_ref, bf16[512,1024]{1,0:T(8,128)(2,1)S(1)} %get-tuple-element.60.normed, bf16[128,512]{1,0:T(8,128)(2,1)S(1)} %get-tuple-element.64.b_t, bf16[512,64]{1,0:T(8,128)(2,1)S(1)} %get-tuple-element.65.grow, ...), custom_call_target="tpu_custom_call" | custom-call | flops 2147483648 | bytes 1048576 | tf_op jit(solution)/shard_map/project/pallas_call | solution.py:395
  13.2 0.1 collective-permute-done.2.got_ref.theirs_ref
  13.3 0.1 total.3.total_ref
  13.4 0.2 collective-permute-start.4
  13.5 1.2 %inner.4 = (bf16[512,512]{1,0:T(8,128)(2,1)S(1)}, bf16[512,512]{1,0:T(8,128)(2,1)S(1)}, bf16[512,1024]{1,0:T(8,128)(2,1)S(1)}) custom-call(s32[1]{0:T(128)} %bitcast.here_ref, bf16[512,1024]{1,0:T(8,128)(2,1)S(1)} %get-tuple-element.60.normed, bf16[512,256]{1,0:T(8,128)(2,1)S(1)} %get-tuple-element.58.refs_0_.keys, ...), custom_call_target="tpu_custom_call" | custom-call | flops 2147483648 | bytes 1048576 | tf_op jit(solution)/shard_map/inner/pallas_call | solution.py:395
  14.8 0.3 %collective-permute-done.1.got_ref.got_first = bf16[144,512]{1,0:T(8,128)(2,1)S(1)} collective-permute-done((bf16[144,512]{1,0:T(8,128)(2,1)S(1)}, bf16[144,512]{1,0:T(8,128)(2,1)S(1)}, u32[]{:S(2)}, u32[]{:S(2)}) %collective-permute-start.1) | collective-permute-done | bytes 147488 | tf_op jit(solution)/shard_map/ppermute | solution.py:453
  15.1 0.1 step.2
  15.1 1.8 %collective-permute-start.3 = (bf16[128,512]{1,0:T(8,128)(2,1)S(1)}, bf16[128,512]{1,0:T(8,128)(2,1)S(1)}, u32[]{:S(2)}, u32[]{:S(2)}) collective-permute-start(bf16[128,512]{1,0:T(8,128)(2,1)S(1)} %get-tuple-element.81), channel_id=1, source_target_pairs={{0,16},{4,20},{8,24},{12,28},{16,0},{20,4},{24,8},{28,12},{1,17},{... | collective-permute-start | bytes 393224 | tf_op jit(solution)/shard_map/ppermute | solution.py:464
  17.0 1.2 %inner.5 = (bf16[512,512]{1,0:T(8,128)(2,1)S(1)}, bf16[512,512]{1,0:T(8,128)(2,1)S(1)}, bf16[512,1024]{1,0:T(8,128)(2,1)S(1)}) custom-call(s32[1]{0:T(128)} %bitcast.here_ref, bf16[512,1024]{1,0:T(8,128)(2,1)S(1)} %get-tuple-element.60.normed, bf16[512,256]{1,0:T(8,128)(2,1)S(1)} %get-tuple-element.58.refs_0_.keys, ...), custom_call_target="tpu_custom_call" | custom-call | flops 67108864 | bytes 1048576 | tf_op jit(solution)/shard_map/inner/pallas_call | solution.py:395
  18.2 1.2 %inner.6 = (bf16[512,512]{1,0:T(8,128)(2,1)S(1)}, bf16[512,512]{1,0:T(8,128)(2,1)S(1)}, bf16[512,1024]{1,0:T(8,128)(2,1)S(1)}) custom-call(s32[1]{0:T(128)} %bitcast.here_ref, bf16[512,1024]{1,0:T(8,128)(2,1)S(1)} %get-tuple-element.60.normed, bf16[512,256]{1,0:T(8,128)(2,1)S(1)} %get-tuple-element.58.refs_0_.keys, ...), custom_call_target="tpu_custom_call" | custom-call | flops 67108864 | bytes 1048576 | tf_op jit(solution)/shard_map/inner/pallas_call | solution.py:395
  19.4 0.0 collective-permute-done.4.got_ref
  19.4 0.1 step.3
  19.5 1.4 %collective-permute-start.5 = (bf16[128,512]{1,0:T(8,128)(2,1)S(1)}, bf16[128,512]{1,0:T(8,128)(2,1)S(1)}, u32[]{:S(2)}, u32[]{:S(2)}) collective-permute-start(bf16[128,512]{1,0:T(8,128)(2,1)S(1)} %get-tuple-element.99), channel_id=1, source_target_pairs={{0,16},{4,20},{8,24},{12,28},{16,0},{20,4},{24,8},{28,12},{1,17},{... | collective-permute-start | bytes 393224 | tf_op jit(solution)/shard_map/ppermute | solution.py:464
  20.9 0.0 collective-permute-done.3.got_ref
  20.9 0.3 last.2
  21.2 1.2 %inner.7 = (bf16[512,512]{1,0:T(8,128)(2,1)S(1)}, bf16[512,512]{1,0:T(8,128)(2,1)S(1)}, bf16[512,1024]{1,0:T(8,128)(2,1)S(1)}) custom-call(s32[1]{0:T(128)} %bitcast.here_ref, bf16[512,1024]{1,0:T(8,128)(2,1)S(1)} %get-tuple-element.60.normed, bf16[512,256]{1,0:T(8,128)(2,1)S(1)} %get-tuple-element.58.refs_0_.keys, ...), custom_call_target="tpu_custom_call" | custom-call | flops 67108864 | bytes 1048576 | tf_op jit(solution)/shard_map/inner/pallas_call | solution.py:395
  22.4 0.1 collective-permute-start.6
  22.5 1.1 %mix.3.base = f32[512,1024]{1,0:T(8,128)S(1)} custom-call(s32[1]{0:T(128)} %bitcast.here_ref, bf16[512,256]{1,0:T(8,128)(2,1)S(1)} %get-tuple-element.58.refs_0_.keys, bf16[512,1024]{1,0:T(8,128)(2,1)S(1)} %get-tuple-element.95.base, f32[1,2048]{1,0:T(1,128)S(1)} %get-tuple-element.96.gain, bf16[128,512]{1,0:T(8,128)(2,1)S(1)} %get-tuple-element.92.refs_0_, ...), custom_call_target="tpu_custom_call" | custom-call | flops 67108864 | bytes 1048576 | tf_op jit(solution)/shard_map/mix/pallas_call | solution.py:395
  23.5 1.2 %collective-permute-done.5.got_ref = bf16[128,512]{1,0:T(8,128)(2,1)S(1)} collective-permute-done((bf16[128,512]{1,0:T(8,128)(2,1)S(1)}, bf16[128,512]{1,0:T(8,128)(2,1)S(1)}, u32[]{:S(2)}, u32[]{:S(2)}) %collective-permute-start.5) | collective-permute-done | bytes 131104 | tf_op jit(solution)/shard_map/ppermute | solution.py:464
  24.7 0.1 last.3
  24.8 0.1 collective-permute-start.7
  24.9 0.0 collective-permute-done.6.refs_0_
  24.9 2.0 %mix.4.base = f32[512,1024]{1,0:T(8,128)S(1)} custom-call(s32[1]{0:T(128)} %bitcast.here_ref, bf16[512,256]{1,0:T(8,128)(2,1)S(1)} %get-tuple-element.58.refs_0_.keys, f32[512,1024]{1,0:T(8,128)S(1)} %mix.3.base, f32[1,2048]{1,0:T(1,128)S(1)} %get-tuple-element.96.gain, bf16[128,512]{1,0:T(8,128)(2,1)S(1)} %collective-permute-done.6.refs_0_, ...), custom_call_target="tpu_custom_call" | custom-call | flops 67108864 | bytes 1048576 | tf_op jit(solution)/shard_map/mix/pallas_call | solution.py:395
  26.9 0.0 collective-permute-done.7.refs_0_
  26.9 1.9 %mix.5 = bf16[512,1024]{1,0:T(8,128)(2,1)} custom-call(s32[1]{0:T(128)} %bitcast.here_ref, bf16[512,256]{1,0:T(8,128)(2,1)S(1)} %get-tuple-element.58.refs_0_.keys, f32[512,1024]{1,0:T(8,128)S(1)} %mix.4.base, f32[1,2048]{1,0:T(1,128)S(1)} %get-tuple-element.96.gain, bf16[128,512]{1,0:T(8,128)(2,1)S(1)} %collective-permute-done.7.refs_0_, ...), custom_call_target="tpu_custom_call" | custom-call | flops 67108864 | bytes 1048576 | tf_op jit(solution)/shard_map/mix/pallas_call | solution.py:395
Async XLA Ops:
  6.3 1.6 %collective-permute-start = (bf16[144,512]{1,0:T(8,128)(2,1)S(1)}, bf16[144,512]{1,0:T(8,128)(2,1)S(1)}, u32[]{:S(2)}, u32[]{:S(2)}) collective-permute-start(bf16[144,512]{1,0:T(8,128)(2,1)S(1)} %get-tuple-element.68), channel_id=1, source_target_pairs={{0,4},{4,0},{8,12},{12,8},{16,20},{20,16},{24,28},{28,24},{1,5},{5... | collective-permute-start | bytes 442376 | tf_op jit(solution)/shard_map/ppermute | solution.py:471
  8.0 7.1 %collective-permute-start.1 = (bf16[144,512]{1,0:T(8,128)(2,1)S(1)}, bf16[144,512]{1,0:T(8,128)(2,1)S(1)}, u32[]{:S(2)}, u32[]{:S(2)}) collective-permute-start(bf16[144,512]{1,0:T(8,128)(2,1)S(1)} %total.2.total_ref.total_first), channel_id=1, source_target_pairs={{0,8},{4,12},{8,0},{12,4},{16,24},{20,28},{24,16},{28,20},{1,9},{5... | collective-permute-start | bytes 442376 | tf_op jit(solution)/shard_map/ppermute | solution.py:453
  11.9 1.4 %collective-permute-start.2 = (bf16[128,512]{1,0:T(8,128)(2,1)S(1)}, bf16[128,512]{1,0:T(8,128)(2,1)S(1)}, u32[]{:S(2)}, u32[]{:S(2)}) collective-permute-start(bf16[128,512]{1,0:T(8,128)(2,1)S(1)} %get-tuple-element.74), channel_id=1, source_target_pairs={{0,4},{4,0},{8,12},{12,8},{16,20},{20,16},{24,28},{28,24},{1,5},{5... | collective-permute-start | bytes 393224 | tf_op jit(solution)/shard_map/ppermute | solution.py:475
  13.4 6.1 %collective-permute-start.4 = (bf16[128,512]{1,0:T(8,128)(2,1)S(1)}, bf16[128,512]{1,0:T(8,128)(2,1)S(1)}, u32[]{:S(2)}, u32[]{:S(2)}) collective-permute-start(bf16[128,512]{1,0:T(8,128)(2,1)S(1)} %total.3.total_ref), channel_id=1, source_target_pairs={{0,8},{4,12},{8,0},{12,4},{16,24},{20,28},{24,16},{28,20},{1,9},{5... | collective-permute-start | bytes 393224 | tf_op jit(solution)/shard_map/ppermute | solution.py:453
  15.1 5.7 %collective-permute-start.3 = (bf16[128,512]{1,0:T(8,128)(2,1)S(1)}, bf16[128,512]{1,0:T(8,128)(2,1)S(1)}, u32[]{:S(2)}, u32[]{:S(2)}) collective-permute-start(bf16[128,512]{1,0:T(8,128)(2,1)S(1)} %get-tuple-element.81), channel_id=1, source_target_pairs={{0,16},{4,20},{8,24},{12,28},{16,0},{20,4},{24,8},{28,12},{1,17},{... | collective-permute-start | bytes 393224 | tf_op jit(solution)/shard_map/ppermute | solution.py:464
  19.5 5.2 %collective-permute-start.5 = (bf16[128,512]{1,0:T(8,128)(2,1)S(1)}, bf16[128,512]{1,0:T(8,128)(2,1)S(1)}, u32[]{:S(2)}, u32[]{:S(2)}) collective-permute-start(bf16[128,512]{1,0:T(8,128)(2,1)S(1)} %get-tuple-element.99), channel_id=1, source_target_pairs={{0,16},{4,20},{8,24},{12,28},{16,0},{20,4},{24,8},{28,12},{1,17},{... | collective-permute-start | bytes 393224 | tf_op jit(solution)/shard_map/ppermute | solution.py:464
  22.4 2.5 %collective-permute-start.6 = (bf16[128,512]{1,0:T(8,128)(2,1)S(1)}, bf16[128,512]{1,0:T(8,128)(2,1)S(1)}, u32[]{:S(2)}, u32[]{:S(2)}) collective-permute-start(bf16[128,512]{1,0:T(8,128)(2,1)S(1)} %get-tuple-element.103), channel_id=1, source_target_pairs={{0,4},{4,0},{8,12},{12,8},{16,20},{20,16},{24,28},{28,24},{1,5},{5... | collective-permute-start | bytes 393224 | tf_op jit(solution)/shard_map/ppermute | solution.py:469
  24.8 2.1 %collective-permute-start.7 = (bf16[128,512]{1,0:T(8,128)(2,1)S(1)}, bf16[128,512]{1,0:T(8,128)(2,1)S(1)}, u32[]{:S(2)}, u32[]{:S(2)}) collective-permute-start(bf16[128,512]{1,0:T(8,128)(2,1)S(1)} %get-tuple-element.108), channel_id=1, source_target_pairs={{0,4},{4,0},{8,12},{12,8},{16,20},{20,16},{24,28},{28,24},{1,5},{5... | collective-permute-start | bytes 393224 | tf_op jit(solution)/shard_map/ppermute | solution.py:469

commit v11 on v9

--- a/solution.py
+++ b/solution.py
@@ -408,7 +408,7 @@
          near((1, heads), jnp.int32), sems(7), pltpu.SemaphoreType.DMA((9, 2))],
         rows * depth * depth)
 
-    long, short = 8 * rows * depth * size, rows * depth * size // 4
+    long, short = 4 * rows * depth * size, rows * depth * size // 4
 
     def projected(own, group, w):
         return call(functools.partial(project_kernel, heads, head_dim, own, group), "project",

time: 29.2 us -> 31.1 us (1.065)
  waiting for transfers between devices: 1.78 us -> 4.33 us
  starting transfers between devices: 6.72 us -> 6.08 us
    ppermute x2, waiting for transfers between devices: 0.3 us -> 2.07 us  [start_total(): arriving[i] = lax.ppermute(totals[i], 'tm', pair(2))]
    ppermute x2, waiting for transfers between devices: 1.21 us -> 2.26 us  [advance(): arriving[i] = lax.ppermute(totals[i], 'tm', pair(2 * reach))]
    ppermute x2, starting transfers between devices: 3.07 us -> 2.26 us  [advance(): arriving[i] = lax.ppermute(totals[i], 'tm', pair(2 * reach))]
  transfers between devices with their start and end apart: 8 -> 8, of which waited for: 3 -> 3; matrix products, arithmetic and copies ran while one was open for 0% -> 0% of each run, Pallas kernels for 41% -> 35%
where the time goes in v11:
time: 31.1 us; the launch traced here: 30.8 us
  Pallas kernels  19.5 us (63%)
  starting transfers between devices  6.08 us (20%)
  waiting for transfers between devices  4.33 us (14%)
  between operations  0.97 us (3%)
    pallas_call x17, Pallas kernels, call(): pl.pallas_call(kernel, out_shape=tuple(outs), in_specs=specs, out_specs=(...  19.5 us
    ppermute x2, starting transfers between devices, start_total(): arriving[i] = lax.ppermute(totals[i], 'tm', pair(2))  2.81 us
    ppermute x2, waiting for transfers between devices, advance(): arriving[i] = lax.ppermute(totals[i], 'tm', pair(2 * reach))  2.26 us
    ppermute x2, starting transfers between devices, advance(): arriving[i] = lax.ppermute(totals[i], 'tm', pair(2 * reach))  2.26 us
    ppermute x2, waiting for transfers between devices, start_total(): arriving[i] = lax.ppermute(totals[i], 'tm', pair(2))  2.07 us
  transfers between devices with their start and end apart: 8, of which 3 were waited for; matrix products, arithmetic and copies ran while one was open for 0% of the time, Pallas kernels for 35%

profile of v11, /device:TPU:0, one launch (start us, length us, event | category | flops | bytes accessed | tf_op | source)
XLA Modules:
  0.0 30.8 jit_solution(6060098791025470990)
XLA Ops:
  0.7 5.6 %encode.1 = (bf16[512,1024]{1,0:T(8,128)(2,1)S(1)}, bf16[512,1024]{1,0:T(8,128)(2,1)S(1)}, bf16[512,256]{1,0:T(8,128)(2,1)S(1)}, bf16[128,512]{1,0:T(8,128)(2,1)...) custom-call(s32[1]{0:T(128)} %bitcast.here_ref, ...), custom_call_target="tpu_custom_call" | custom-call | flops 536870912 | bytes 1048576 | tf_op jit(solution)/shard_map/encode/pallas_call | solution.py:388
  6.3 0.5 %collective-permute-start = (bf16[144,512]{1,0:T(8,128)(2,1)S(1)}, bf16[144,512]{1,0:T(8,128)(2,1)S(1)}, u32[]{:S(2)}, u32[]{:S(2)}) collective-permute-start(bf16[144,512]{1,0:T(8,128)(2,1)S(1)} %get-tuple-element.68), channel_id=1, source_target_pairs={{0,4},{4,0},{8,12},{12,8},{16,20},{20,16},{24,28},{28,24},{1,5},{5... | collective-permute-start | bytes 442376 | tf_op jit(solution)/shard_map/ppermute | solution.py:463
  6.8 1.1 %project.3 = (bf16[512,512]{1,0:T(8,128)(2,1)S(1)}, bf16[144,512]{1,0:T(8,128)(2,1)S(1)}) custom-call(s32[1]{0:T(128)} %bitcast.here_ref, bf16[512,1024]{1,0:T(8,128)(2,1)S(1)} %get-tuple-element.60.normed, bf16[128,512]{1,0:T(8,128)(2,1)S(1)} %get-tuple-element.64.b_t, bf16[512,64]{1,0:T(8,128)(2,1)S(1)} %get-tuple-element.65.grow, ...), custom_call_target="tpu_custom_call" | custom-call | flops 1073741824 | bytes 1048576 | tf_op jit(solution)/shard_map/project/pallas_call | solution.py:388
  7.9 0.0 collective-permute-done.got_ref.got_first.theirs_ref.theirs_first
  7.9 0.1 total.2.total_ref.total_first
  8.0 1.1 %project.4 = (bf16[512,512]{1,0:T(8,128)(2,1)S(1)}, bf16[128,512]{1,0:T(8,128)(2,1)S(1)}) custom-call(s32[1]{0:T(128)} %bitcast.here_ref, bf16[512,1024]{1,0:T(8,128)(2,1)S(1)} %get-tuple-element.60.normed, bf16[128,512]{1,0:T(8,128)(2,1)S(1)} %get-tuple-element.64.b_t, bf16[512,64]{1,0:T(8,128)(2,1)S(1)} %get-tuple-element.65.grow, ...), custom_call_target="tpu_custom_call" | custom-call | flops 1073741824 | bytes 1048576 | tf_op jit(solution)/shard_map/project/pallas_call | solution.py:388
  9.1 0.4 %collective-permute-start.2 = (bf16[128,512]{1,0:T(8,128)(2,1)S(1)}, bf16[128,512]{1,0:T(8,128)(2,1)S(1)}, u32[]{:S(2)}, u32[]{:S(2)}) collective-permute-start(bf16[128,512]{1,0:T(8,128)(2,1)S(1)} %get-tuple-element.74), channel_id=1, source_target_pairs={{0,4},{4,0},{8,12},{12,8},{16,20},{20,16},{24,28},{28,24},{1,5},{5... | collective-permute-start | bytes 393224 | tf_op jit(solution)/shard_map/ppermute | solution.py:467
  9.4 2.7 %collective-permute-start.1 = (bf16[144,512]{1,0:T(8,128)(2,1)S(1)}, bf16[144,512]{1,0:T(8,128)(2,1)S(1)}, u32[]{:S(2)}, u32[]{:S(2)}) collective-permute-start(bf16[144,512]{1,0:T(8,128)(2,1)S(1)} %total.2.total_ref.total_first), channel_id=1, source_target_pairs={{0,8},{4,12},{8,0},{12,4},{16,24},{20,28},{24,16},{28,20},{1,9},{5... | collective-permute-start | bytes 442376 | tf_op jit(solution)/shard_map/ppermute | solution.py:445
  12.1 1.1 %project.5 = (bf16[512,512]{1,0:T(8,128)(2,1)S(1)}, bf16[128,512]{1,0:T(8,128)(2,1)S(1)}) custom-call(s32[1]{0:T(128)} %bitcast.here_ref, bf16[512,1024]{1,0:T(8,128)(2,1)S(1)} %get-tuple-element.60.normed, bf16[128,512]{1,0:T(8,128)(2,1)S(1)} %get-tuple-element.64.b_t, bf16[512,64]{1,0:T(8,128)(2,1)S(1)} %get-tuple-element.65.grow, ...), custom_call_target="tpu_custom_call" | custom-call | flops 1073741824 | bytes 1048576 | tf_op jit(solution)/shard_map/project/pallas_call | solution.py:388
  13.2 0.0 collective-permute-done.2.got_ref.theirs_ref
  13.2 0.1 total.3.total_ref
  13.3 0.1 collective-permute-start.4
  13.4 1.3 %inner.4 = (bf16[512,512]{1,0:T(8,128)(2,1)S(1)}, bf16[512,512]{1,0:T(8,128)(2,1)S(1)}, bf16[512,1024]{1,0:T(8,128)(2,1)S(1)}, bf16[512,512]{1,0:T(8,128)(2,1)S(1)}) custom-call(s32[1]{0:T(128)} %bitcast.here_ref, bf16[512,1024]{1,0:T(8,128)(2,1)S(1)} %get-tuple-element.60.normed, bf16[512,256]{1,0:T(8,128)(2,1)S(1)} %get-tuple-element.58.keys, ...), custom_call_target="tpu_custom_call" | custom-call | flops 1073741824 | bytes 1048576 | tf_op jit(solution)/shard_map/inner/pallas_call | solution.py:388
  14.7 2.1 %collective-permute-done.1.got_ref.got_first = bf16[144,512]{1,0:T(8,128)(2,1)S(1)} collective-permute-done((bf16[144,512]{1,0:T(8,128)(2,1)S(1)}, bf16[144,512]{1,0:T(8,128)(2,1)S(1)}, u32[]{:S(2)}, u32[]{:S(2)}) %collective-permute-start.1) | collective-permute-done | bytes 147488 | tf_op jit(solution)/shard_map/ppermute | solution.py:445
  16.7 0.1 step.2
  16.8 2.2 %collective-permute-start.3 = (bf16[128,512]{1,0:T(8,128)(2,1)S(1)}, bf16[128,512]{1,0:T(8,128)(2,1)S(1)}, u32[]{:S(2)}, u32[]{:S(2)}) collective-permute-start(bf16[128,512]{1,0:T(8,128)(2,1)S(1)} %get-tuple-element.80), channel_id=1, source_target_pairs={{0,16},{4,20},{8,24},{12,28},{16,0},{20,4},{24,8},{28,12},{1,17},{... | collective-permute-start | bytes 393224 | tf_op jit(solution)/shard_map/ppermute | solution.py:456
  19.0 1.2 %inner.5 = (bf16[512,512]{1,0:T(8,128)(2,1)S(1)}, bf16[512,512]{1,0:T(8,128)(2,1)S(1)}, bf16[512,1024]{1,0:T(8,128)(2,1)S(1)}) custom-call(s32[1]{0:T(128)} %bitcast.here_ref, bf16[512,1024]{1,0:T(8,128)(2,1)S(1)} %get-tuple-element.60.normed, bf16[512,256]{1,0:T(8,128)(2,1)S(1)} %get-tuple-element.58.keys, bf16[512,64]{1,0:T(8,128)(2,1)S(1)} %get-tuple-element.61.fall, ...), custom_call_target="tpu_custom_call" | custom-call | flops 67108864 | bytes 1048576 | tf_op jit(solution)/shard_map/inner/pallas_call | solution.py:388
  20.2 1.2 %inner.6 = (bf16[512,512]{1,0:T(8,128)(2,1)S(1)}, bf16[512,512]{1,0:T(8,128)(2,1)S(1)}, bf16[512,1024]{1,0:T(8,128)(2,1)S(1)}) custom-call(s32[1]{0:T(128)} %bitcast.here_ref, bf16[512,1024]{1,0:T(8,128)(2,1)S(1)} %get-tuple-element.60.normed, bf16[512,256]{1,0:T(8,128)(2,1)S(1)} %get-tuple-element.58.keys, bf16[512,64]{1,0:T(8,128)(2,1)S(1)} %get-tuple-element.61.fall, ...), custom_call_target="tpu_custom_call" | custom-call | flops 67108864 | bytes 1048576 | tf_op jit(solution)/shard_map/inner/pallas_call | solution.py:388
  21.4 0.0 collective-permute-done.4.got_ref
  21.4 0.1 step.3
  21.5 0.1 collective-permute-start.5
  21.6 0.5 %collective-permute-done.3.got_ref = bf16[128,512]{1,0:T(8,128)(2,1)S(1)} collective-permute-done((bf16[128,512]{1,0:T(8,128)(2,1)S(1)}, bf16[128,512]{1,0:T(8,128)(2,1)S(1)}, u32[]{:S(2)}, u32[]{:S(2)}) %collective-permute-start.3) | collective-permute-done | bytes 131104 | tf_op jit(solution)/shard_map/ppermute | solution.py:456
  22.1 0.3 last.2
  22.4 1.2 %inner.7 = (bf16[512,512]{1,0:T(8,128)(2,1)S(1)}, bf16[512,512]{1,0:T(8,128)(2,1)S(1)}, bf16[512,1024]{1,0:T(8,128)(2,1)S(1)}) custom-call(s32[1]{0:T(128)} %bitcast.here_ref, bf16[512,1024]{1,0:T(8,128)(2,1)S(1)} %get-tuple-element.60.normed, bf16[512,256]{1,0:T(8,128)(2,1)S(1)} %get-tuple-element.58.keys, bf16[512,64]{1,0:T(8,128)(2,1)S(1)} %get-tuple-element.61.fall, ...), custom_call_target="tpu_custom_call" | custom-call | flops 67108864 | bytes 1048576 | tf_op jit(solution)/shard_map/inner/pallas_call | solution.py:388
  23.6 0.1 collective-permute-start.6
  23.7 1.1 %mix.3.base = f32[512,1024]{1,0:T(8,128)S(1)} custom-call(s32[1]{0:T(128)} %bitcast.here_ref, bf16[512,256]{1,0:T(8,128)(2,1)S(1)} %get-tuple-element.58.keys, bf16[512,1024]{1,0:T(8,128)(2,1)S(1)} %get-tuple-element.95.base, f32[1,2048]{1,0:T(1,128)S(1)} %get-tuple-element.96.gain, bf16[128,512]{1,0:T(8,128)(2,1)S(1)} %get-tuple-element.92.refs_0_, ...), custom_call_target="tpu_custom_call" | custom-call | flops 67108864 | bytes 1048576 | tf_op jit(solution)/shard_map/mix/pallas_call | solution.py:388
  24.8 1.8 %collective-permute-done.5.got_ref = bf16[128,512]{1,0:T(8,128)(2,1)S(1)} collective-permute-done((bf16[128,512]{1,0:T(8,128)(2,1)S(1)}, bf16[128,512]{1,0:T(8,128)(2,1)S(1)}, u32[]{:S(2)}, u32[]{:S(2)}) %collective-permute-start.5) | collective-permute-done | bytes 131104 | tf_op jit(solution)/shard_map/ppermute | solution.py:456
  26.5 0.1 last.3
  26.7 0.1 collective-permute-start.7
  26.7 0.0 collective-permute-done.6.refs_0_
  26.7 2.0 %mix.4.base = f32[512,1024]{1,0:T(8,128)S(1)} custom-call(s32[1]{0:T(128)} %bitcast.here_ref, bf16[512,256]{1,0:T(8,128)(2,1)S(1)} %get-tuple-element.58.keys, f32[512,1024]{1,0:T(8,128)S(1)} %mix.3.base, f32[1,2048]{1,0:T(1,128)S(1)} %get-tuple-element.96.gain, bf16[128,512]{1,0:T(8,128)(2,1)S(1)} %collective-permute-done.6.refs_0_, ...), custom_call_target="tpu_custom_call" | custom-call | flops 67108864 | bytes 1048576 | tf_op jit(solution)/shard_map/mix/pallas_call | solution.py:388
  28.7 0.0 collective-permute-done.7.refs_0_
  28.7 2.0 %mix.5 = bf16[512,1024]{1,0:T(8,128)(2,1)} custom-call(s32[1]{0:T(128)} %bitcast.here_ref, bf16[512,256]{1,0:T(8,128)(2,1)S(1)} %get-tuple-element.58.keys, f32[512,1024]{1,0:T(8,128)S(1)} %mix.4.base, f32[1,2048]{1,0:T(1,128)S(1)} %get-tuple-element.96.gain, bf16[128,512]{1,0:T(8,128)(2,1)S(1)} %collective-permute-done.7.refs_0_, ...), custom_call_target="tpu_custom_call" | custom-call | flops 67108864 | bytes 1048576 | tf_op jit(solution)/shard_map/mix/pallas_call | solution.py:388
Async XLA Ops:
  6.3 1.6 %collective-permute-start = (bf16[144,512]{1,0:T(8,128)(2,1)S(1)}, bf16[144,512]{1,0:T(8,128)(2,1)S(1)}, u32[]{:S(2)}, u32[]{:S(2)}) collective-permute-start(bf16[144,512]{1,0:T(8,128)(2,1)S(1)} %get-tuple-element.68), channel_id=1, source_target_pairs={{0,4},{4,0},{8,12},{12,8},{16,20},{20,16},{24,28},{28,24},{1,5},{5... | collective-permute-start | bytes 442376 | tf_op jit(solution)/shard_map/ppermute | solution.py:463
  9.1 4.1 %collective-permute-start.2 = (bf16[128,512]{1,0:T(8,128)(2,1)S(1)}, bf16[128,512]{1,0:T(8,128)(2,1)S(1)}, u32[]{:S(2)}, u32[]{:S(2)}) collective-permute-start(bf16[128,512]{1,0:T(8,128)(2,1)S(1)} %get-tuple-element.74), channel_id=1, source_target_pairs={{0,4},{4,0},{8,12},{12,8},{16,20},{20,16},{24,28},{28,24},{1,5},{5... | collective-permute-start | bytes 393224 | tf_op jit(solution)/shard_map/ppermute | solution.py:467
  9.4 7.3 %collective-permute-start.1 = (bf16[144,512]{1,0:T(8,128)(2,1)S(1)}, bf16[144,512]{1,0:T(8,128)(2,1)S(1)}, u32[]{:S(2)}, u32[]{:S(2)}) collective-permute-start(bf16[144,512]{1,0:T(8,128)(2,1)S(1)} %total.2.total_ref.total_first), channel_id=1, source_target_pairs={{0,8},{4,12},{8,0},{12,4},{16,24},{20,28},{24,16},{28,20},{1,9},{5... | collective-permute-start | bytes 442376 | tf_op jit(solution)/shard_map/ppermute | solution.py:445
  13.3 8.1 %collective-permute-start.4 = (bf16[128,512]{1,0:T(8,128)(2,1)S(1)}, bf16[128,512]{1,0:T(8,128)(2,1)S(1)}, u32[]{:S(2)}, u32[]{:S(2)}) collective-permute-start(bf16[128,512]{1,0:T(8,128)(2,1)S(1)} %total.3.total_ref), channel_id=1, source_target_pairs={{0,8},{4,12},{8,0},{12,4},{16,24},{20,28},{24,16},{28,20},{1,9},{5... | collective-permute-start | bytes 393224 | tf_op jit(solution)/shard_map/ppermute | solution.py:445
  16.8 5.3 %collective-permute-start.3 = (bf16[128,512]{1,0:T(8,128)(2,1)S(1)}, bf16[128,512]{1,0:T(8,128)(2,1)S(1)}, u32[]{:S(2)}, u32[]{:S(2)}) collective-permute-start(bf16[128,512]{1,0:T(8,128)(2,1)S(1)} %get-tuple-element.80), channel_id=1, source_target_pairs={{0,16},{4,20},{8,24},{12,28},{16,0},{20,4},{24,8},{28,12},{1,17},{... | collective-permute-start | bytes 393224 | tf_op jit(solution)/shard_map/ppermute | solution.py:456
  21.5 5.0 %collective-permute-start.5 = (bf16[128,512]{1,0:T(8,128)(2,1)S(1)}, bf16[128,512]{1,0:T(8,128)(2,1)S(1)}, u32[]{:S(2)}, u32[]{:S(2)}) collective-permute-start(bf16[128,512]{1,0:T(8,128)(2,1)S(1)} %get-tuple-element.99), channel_id=1, source_target_pairs={{0,16},{4,20},{8,24},{12,28},{16,0},{20,4},{24,8},{28,12},{1,17},{... | collective-permute-start | bytes 393224 | tf_op jit(solution)/shard_map/ppermute | solution.py:456
  23.6 3.1 %collective-permute-start.6 = (bf16[128,512]{1,0:T(8,128)(2,1)S(1)}, bf16[128,512]{1,0:T(8,128)(2,1)S(1)}, u32[]{:S(2)}, u32[]{:S(2)}) collective-permute-start(bf16[128,512]{1,0:T(8,128)(2,1)S(1)} %get-tuple-element.103), channel_id=1, source_target_pairs={{0,4},{4,0},{8,12},{12,8},{16,20},{20,16},{24,28},{28,24},{1,5},{5... | collective-permute-start | bytes 393224 | tf_op jit(solution)/shard_map/ppermute | solution.py:461
  26.7 2.1 %collective-permute-start.7 = (bf16[128,512]{1,0:T(8,128)(2,1)S(1)}, bf16[128,512]{1,0:T(8,128)(2,1)S(1)}, u32[]{:S(2)}, u32[]{:S(2)}) collective-permute-start(bf16[128,512]{1,0:T(8,128)(2,1)S(1)} %get-tuple-element.108), channel_id=1, source_target_pairs={{0,4},{4,0},{8,12},{12,8},{16,20},{20,16},{24,28},{28,24},{1,5},{5... | collective-permute-start | bytes 393224 | tf_op jit(solution)/shard_map/ppermute | solution.py:461
